TPU v7x, 128 devices: a whole 4x4x4 slice. The times are simulated.
128 devices in a mesh: occ: 4 (over z), virt: 32 (over y, x, core).
Axes of the slice: x: 4, y: 4, z: 4, core: 2. Of those that a mesh axis runs over, the one named last changes fastest.
Arguments:
- amplitudes: bfloat16 [256, 512, 512], P('occ', 'virt'), may hold values from -0.15625 to 0.15625
- ac_factor: bfloat16 [8, 512, 3072], P(None, ('virt', 'occ')), may hold values from -2 to 2
- bd_factor: bfloat16 [512, 128, 3072], P(('virt', 'occ')), may hold values from -2 to 2
- irrep_a: int32 [8], replicated, may hold values from 0 to 7
- irrep_b: int32 [128], replicated, may hold values from 0 to 7
- irrep_c: int32 [512], replicated, may hold values from 0 to 7
- irrep_d: int32 [512], P(('virt', 'occ')), may hold values from 0 to 7
Outputs:
- ladder: bfloat16 [256, 8, 128], P(('occ', 'virt'))
All inputs are finite; a program needn't handle non-finite values.
Results may differ from a plain program's by a relative error of at most 0.0049.
Values may be sent and summed in bfloat16 or wider, within the bound.
No kernel may reach another device: no remote copies, remote signals or barrier semaphores. Data moves between devices by JAX's collectives and lax.ppermute only.
A program may use at most 128 MiB of HBM per device.

v0:
```python
import jax
import jax.numpy as jnp
from jax import lax
from jax.sharding import PartitionSpec as P


def make_folder(amps_all, labels_all, irrep_a, pair_bd, bd_factor):

    def add_piece(total, piece, start):
        pair_ac = jnp.bitwise_xor(irrep_a[:, None], labels_all[None, :])
        integral = lax.dot_general(
            piece, bd_factor, (((2,), (2,)), ((), ())), preferred_element_type=jnp.float32
        )
        keep = pair_ac[:, :, None, None] == pair_bd[None, None, :, :]
        integral = jnp.where(keep, integral, jnp.float32(0.0)).astype(jnp.bfloat16)
        return jnp.einsum("pdc,acdb->pab", amps_all, integral, preferred_element_type=jnp.float32)

    return add_piece


def body(amplitudes, ac_factor, bd_factor, irrep_a, irrep_b, irrep_c, irrep_d):
    regrouped = lax.all_to_all(amplitudes, "occ", split_axis=1, concat_axis=0, tiled=True)
    pair_bd = jnp.bitwise_xor(irrep_d[:, None], irrep_b[None, :])
    start_total = jnp.zeros(
        (regrouped.shape[0], ac_factor.shape[0], bd_factor.shape[1]), jnp.float32
    )
    folder = make_folder(regrouped, irrep_c, irrep_a, pair_bd, bd_factor)
    quarter_slab = lax.all_gather(ac_factor, "occ", axis=1, tiled=True)
    total = folder(
        start_total, lax.all_gather(quarter_slab, "virt", axis=1, tiled=True), jnp.int32(0)
    )
    summed = lax.psum_scatter(total, ("occ", "virt"), scatter_dimension=0, tiled=True)
    return summed.astype(jnp.bfloat16)


def solution(mesh):
    return jax.shard_map(
        body,
        mesh=mesh,
        in_specs=(
            P("occ", "virt", None),
            P(None, ("virt", "occ"), None),
            P(("virt", "occ"), None, None),
            P(),
            P(),
            P(),
            P(("virt", "occ")),
        ),
        out_specs=P(("occ", "virt"), None, None),
        check_vma=False,
    )
```

profile of v0, /device:TPU:1, one launch (start us, length us, event | category | flops | bytes accessed | tf_op | source)
XLA Modules:
  0.0 780.3 jit_solution(17288543885408562222)
XLA Ops:
  6.5 0.0 copy-start
  6.5 0.0 copy-start.5
  6.5 0.0 copy-start.4
  6.5 0.0 copy-start.2
  6.5 0.0 copy-start.3
  6.5 0.0 all-gather.2.cloned.1.call-start
  6.6 1.1 copy.14
  7.7 14.8 %all_gather.6 = bf16[8,16,3072]{2,0,1:T(8,128)(2,1)} all-gather(bf16[8,4,3072]{2,0,1:T(8,128)(2,1)S(1)} %copy.14), channel_id=1, replica_groups=mesh['occ'=4,'virt'=32] {'occ'}, dimensions={1}, use_global_device_ids=true | all-gather | bytes 983040 | tf_op jit(solution)/shard_map/all_gather | solution.py:28
  22.6 0.0 all-gather.2.cloned.1.call-update
  22.6 2.9 copy.15
  25.4 4.2 all-to-all-start
  29.7 0.0 reduce-scatter.2.cloned.1.call-start
  29.7 0.0 copy-done.5
  29.7 0.0 copy-done.4
  29.8 0.1 broadcast_xor_fusion.1
  29.8 0.0 copy-done.2
  29.8 0.0 copy-done.3
  29.8 0.1 broadcast_xor_fusion
  30.0 11.8 %all-to-all-done = bf16[64,16,512]{2,0,1:T(8,128)(2,1)} async-done(((bf16[64,16,512]{2,0,1:T(8,128)(2,1)}), bf16[64,16,512]{2,0,1:T(8,128)(2,1)}, u32[]{:S(2)}, u32[]{:S(2)}) %all-to-all-start) | async-done | bytes 1048608 | tf_op jit(solution)/shard_map/all_to_all | solution.py:22
  41.8 2.4 copy.16
  44.2 74.4 %all-gather.2.cloned.1.call-done = bf16[8,512,3072]{2,0,1:T(8,128)(2,1)} async-done(((bf16[8,16,3072]{2,0,1:T(8,128)(2,1)}), bf16[8,512,3072]{2,0,1:T(8,128)(2,1)}) %all-gather.2.cloned.1.call-update) | async-done | bytes 25165840 | tf_op jit(solution)/shard_map/all_gather | solution.py:30
  118.6 0.0 copy-done
  118.6 0.0 copy-start.1
  118.6 16.7 %select_convert_fusion = bf16[8,512,4,128]{3,0,2,1:T(8,128)(2,1)S(1)} fusion(s32[4,128]{1,0:T(4,128)S(1)} %broadcast_xor_fusion.1, s32[8,512]{0,1:T(8,128)S(1)} %broadcast_xor_fusion, bf16[4,128,3072]{2,1,0:T(8,128)(2,1)S(1)} %copy-done, bf16[8,512,3072]{2,0,1:T(8,128)(2,1)} %all-gather.2.cloned.1.call-done), kind=kOutput, calls=%fused_computation.2 | convolution fusion | flops 12891193344 | bytes 32524288 | tf_op jit(solution)/shard_map/dot_general | solution.py:11
  135.3 0.0 copy-done.1
  135.3 4.7 fusion.9
  139.9 2.5 copy.18
  142.5 0.0 reduce-scatter.2.cloned.1.call-update
  142.5 629.6 %reduce-scatter.2.cloned.1.call-done = f32[2,8,128]{2,1,0:T(8,128)} async-done(((f32[256,8,128]{2,1,0:T(8,128)}), f32[2,8,128]{2,1,0:T(8,128)}) %reduce-scatter.2.cloned.1.call-update) | async-done | bytes 8208 | tf_op jit(solution)/shard_map/reduce_scatter | solution.py:32
  772.1 1.3 convert_element_type.7
Async XLA Ops:
  6.5 112.0 %copy-start = (bf16[4,128,3072]{2,1,0:T(8,128)(2,1)S(1)}, bf16[4,128,3072]{2,1,0:T(8,128)(2,1)}, u32[]{:S(2)}) copy-start(bf16[4,128,3072]{2,1,0:T(8,128)(2,1)} %param.9) | copy-start | bytes 9437188
  6.5 23.2 %copy-start.5 = (s32[4]{0:T(128)S(1)}, s32[4]{0:T(128)}, u32[]{:S(2)}) copy-start(s32[4]{0:T(128)} %param.13) | copy-start | bytes 52
  6.5 23.2 %copy-start.4 = (s32[128]{0:T(128)S(1)}, s32[128]{0:T(128)}, u32[]{:S(2)}) copy-start(s32[128]{0:T(128)} %param.11) | copy-start | bytes 1540
  6.5 23.3 %copy-start.2 = (s32[512]{0:T(512)S(1)}, s32[512]{0:T(512)}, u32[]{:S(2)}) copy-start(s32[512]{0:T(512)} %param.12) | copy-start | bytes 6148
  6.5 23.3 %copy-start.3 = (s32[8]{0:T(128)S(1)}, s32[8]{0:T(128)}, u32[]{:S(2)}) copy-start(s32[8]{0:T(128)} %param.10) | copy-start | bytes 100
  6.5 112.0 %all-gather.2.cloned.1.call-start = ((), (), s32[]{:S(2)}) async-start(), calls=%async_computation.2 | async-start | bytes 25952256 | tf_op jit(solution)/shard_map/all_gather | solution.py:30
  25.4 16.3 %all-to-all-start = ((bf16[64,16,512]{2,0,1:T(8,128)(2,1)}), bf16[64,16,512]{2,0,1:T(8,128)(2,1)}, u32[]{:S(2)}, u32[]{:S(2)}) async-start(bf16[64,16,512]{2,0,1:T(8,128)(2,1)} %copy.15), calls=%async_computation | async-start | bytes 2097152 | tf_op jit(solution)/shard_map/all_to_all | solution.py:22
  29.7 742.4 %reduce-scatter.2.cloned.1.call-start = ((), (), s32[]{:S(2)}) async-start(), calls=%async_computation.3 | async-start | bytes 1056768 | tf_op jit(solution)/shard_map/reduce_scatter | solution.py:32
  118.6 16.7 %copy-start.1 = (bf16[64,4,4,512]{3,0,1,2:T(8,128)(2,1)S(1)}, bf16[64,4,4,512]{3,0,1,2:T(8,128)(2,1)}, u32[]{:S(2)}) copy-start(bf16[64,4,4,512]{3,0,1,2:T(8,128)(2,1)} %copy.16) | copy-start | bytes 3145732
Sparse Core Ops, SparseCore 0:
  22.7 95.8 all-gather.1
  142.6 629.4 reduce-scatter.1
where the time goes:
time: 787 us; the launch traced here: 780 us
  waiting for transfers between devices  716 us (91%)
  matrix products  21.4 us (3%)
  blocking collectives  14.8 us (2%)
  between operations  13.5 us (2%)
  local copies, waits for them, and re-layouts  8.97 us (1%)
    reduce_scatter x1, waiting for transfers between devices, body(): lax.psum_scatter(total, ('occ', 'virt'), scatter_dimension=0, tiled=True)  630 us
    all_gather x1, waiting for transfers between devices, body(): lax.all_gather(quarter_slab, 'virt', axis=1, tiled=True)  74.4 us
    dot_general x1, matrix products, add_piece(): lax.dot_general(piece, bd_factor, (((2,), (2,)), ((), ())), preferred_ele...  16.7 us
  transfers between devices with their start and end apart: 3, of which 3 were waited for; matrix products, arithmetic and copies ran while one was open for 1% of the time, Pallas kernels for 0%

commit v1 on v0

v1 whole, which is shorter than its diff:
```python
import jax
import jax.numpy as jnp
from jax import lax
from jax.sharding import PartitionSpec as P


def body(amplitudes, ac_factor, bd_factor, irrep_a, irrep_b, irrep_c, irrep_d):
    left = lax.all_gather(ac_factor, ("virt", "occ"), axis=1, tiled=True)
    regrouped = lax.all_to_all(amplitudes, "occ", split_axis=1, concat_axis=0, tiled=True)
    pair_bd = jnp.bitwise_xor(irrep_d[:, None], irrep_b[None, :])
    pair_ac = jnp.bitwise_xor(irrep_a[:, None], irrep_c[None, :])
    integral = lax.dot_general(
        left, bd_factor, (((2,), (2,)), ((), ())), preferred_element_type=jnp.float32
    )
    keep = pair_ac[:, :, None, None] == pair_bd[None, None, :, :]
    integral = jnp.where(keep, integral, jnp.float32(0.0)).astype(jnp.bfloat16)
    total = jnp.einsum("pdc,acdb->pab", regrouped, integral, preferred_element_type=jnp.float32)
    pieces = total.astype(jnp.bfloat16).reshape(128, 2, total.shape[1], total.shape[2])
    pieces = lax.all_to_all(pieces, ("occ", "virt"), split_axis=0, concat_axis=0, tiled=True)
    return jnp.sum(pieces.astype(jnp.float32), axis=0).astype(jnp.bfloat16)


def solution(mesh):
    return jax.shard_map(
        body,
        mesh=mesh,
        in_specs=(
            P("occ", "virt", None),
            P(None, ("virt", "occ"), None),
            P(("virt", "occ"), None, None),
            P(),
            P(),
            P(),
            P(("virt", "occ")),
        ),
        out_specs=P(("occ", "virt"), None, None),
        check_vma=False,
    )
```

time: 787 us -> 164 us (0.21)
  waiting for transfers between devices: 716 us -> 90.4 us
    reduce_scatter x1 -> x0, waiting for transfers between devices: 630 us -> none  [body(): lax.psum_scatter(total, ('occ', 'virt'), scatter_dimension=0, tiled=True)]
    all_to_all x0 -> x1, blocking collectives: none -> 21.1 us  [body(): lax.all_to_all(pieces, ('occ', 'virt'), split_axis=0, concat_axis=0, tile...]
    all_gather x1 -> x0, blocking collectives: 14.8 us -> none  [body(): quarter_slab = lax.all_gather(ac_factor, 'occ', axis=1, tiled=True)]
  transfers between devices with their start and end apart: 3 -> 2, of which waited for: 3 -> 2; matrix products, arithmetic and copies ran while one was open for 1% -> 3% of each run, Pallas kernels for 0% -> 0%
where the time goes in v1:
time: 164 us
  waiting for transfers between devices  90.4 us (55%)
  matrix products  22 us (13%)
  blocking collectives  21.1 us (13%)
  between operations  13.4 us (8%)
  local copies, waits for them, and re-layouts  9.21 us (6%)
  starting transfers between devices  5.89 us (4%)
  other arithmetic  1.92 us (1%)
    all_gather x1, waiting for transfers between devices, body(): left = lax.all_gather(ac_factor, ('virt', 'occ'), axis=1, tiled=True)  75.6 us
    all_to_all x1, blocking collectives, body(): lax.all_to_all(pieces, ('occ', 'virt'), split_axis=0, concat_axis=0, tile...  21.1 us
    dot_general x1, matrix products, body(): lax.dot_general(left, bd_factor, (((2,), (2,)), ((), ())), preferred_elem...  16.7 us
    all_to_all x1, waiting for transfers between devices, body(): lax.all_to_all(amplitudes, 'occ', split_axis=1, concat_axis=0, tiled=True)  14.8 us
    all_to_all x1, starting transfers between devices, body(): lax.all_to_all(amplitudes, 'occ', split_axis=1, concat_axis=0, tiled=True)  5.86 us
    dot_general x1, matrix products, body(): jnp.einsum('pdc,acdb->pab', regrouped, integral, preferred_element_type=j...  5.31 us
    unnamed x14, local copies, waits for them, and re-layouts  4.7 us
  transfers between devices with their start and end apart: 2, of which 2 were waited for; matrix products, arithmetic and copies ran while one was open for 3% of the time, Pallas kernels for 0%

profile of v1, /device:TPU:1, one launch (start us, length us, event | category | flops | bytes accessed | tf_op | source)
XLA Modules:
  0.0 164.0 jit_solution(6514727550119524547)
XLA Ops:
  6.5 0.0 copy-start
  6.5 0.0 copy-start.4
  6.5 0.0 copy-start.5
  6.5 0.0 copy-start.3
  6.5 0.0 copy-start.2
  6.5 0.0 all-gather.2.cloned.1.call-start
  6.6 1.8 %copy.11 = bf16[8,4,3072]{2,0,1:T(8,128)(2,1)} copy(bf16[8,4,3072]{2,1,0:T(4,128)(2,1)} %param.8) | data formatting | bytes 393216 | tf_op args[1]
  8.4 0.0 all-gather.2.cloned.1.call-update
  8.4 2.9 %copy.13 = bf16[64,16,512]{2,0,1:T(8,128)(2,1)} copy(bf16[64,16,512]{2,1,0:T(8,128)(2,1)} %param.7) | data formatting | bytes 2097152 | tf_op args[0]
  11.3 5.9 %all-to-all-start = ((bf16[64,16,512]{2,0,1:T(8,128)(2,1)}), bf16[64,16,512]{2,0,1:T(8,128)(2,1)}, u32[]{:S(2)}, u32[]{:S(2)}) async-start(bf16[64,16,512]{2,0,1:T(8,128)(2,1)} %copy.13), calls=%async_computation | async-start | bytes 2097152 | tf_op jit(solution)/shard_map/all_to_all | solution.py:9
  17.2 0.0 copy-done.4
  17.2 0.0 copy-done.5
  17.2 0.1 broadcast_xor_fusion.1
  17.2 0.0 copy-done.3
  17.2 0.0 copy-done.2
  17.2 0.1 broadcast_xor_fusion
  17.3 14.8 %all-to-all-done = bf16[64,16,512]{2,0,1:T(8,128)(2,1)} async-done(((bf16[64,16,512]{2,0,1:T(8,128)(2,1)}), bf16[64,16,512]{2,0,1:T(8,128)(2,1)}, u32[]{:S(2)}, u32[]{:S(2)}) %all-to-all-start) | async-done | bytes 1048608 | tf_op jit(solution)/shard_map/all_to_all | solution.py:9
  32.1 2.4 %copy.14 = bf16[64,4,4,512]{3,0,1,2:T(8,128)(2,1)} copy(bf16[64,4,4,512]{3,0,2,1:T(8,128)(2,1)} %bitcast.2) | data formatting | bytes 2097152 | tf_op jit(solution)/shard_map/all_to_all | solution.py:9
  34.5 75.6 %all-gather.2.cloned.1.call-done = bf16[8,512,3072]{2,0,1:T(8,128)(2,1)} async-done(((bf16[8,4,3072]{2,0,1:T(8,128)(2,1)}), bf16[8,512,3072]{2,0,1:T(8,128)(2,1)}) %all-gather.2.cloned.1.call-update) | async-done | bytes 25165840 | tf_op jit(solution)/shard_map/all_gather | solution.py:8
  110.1 0.0 copy-done
  110.1 0.0 copy-start.1
  110.1 16.7 %fusion = bf16[8,512,4,128]{3,0,2,1:T(8,128)(2,1)S(1)} fusion(bf16[8,512,3072]{2,0,1:T(8,128)(2,1)} %all-gather.2.cloned.1.call-done, bf16[4,128,3072]{2,1,0:T(8,128)(2,1)S(1)} %copy-done), kind=kOutput, calls=%fused_computation | convolution fusion | flops 12884901888 | bytes 32505856 | tf_op jit(solution)/shard_map/dot_general | solution.py:12
  126.8 0.0 copy-done.1
  126.8 5.3 %fusion.15 = bf16[256,8,128]{0,2,1:T(8,128)(2,1)} fusion(bf16[256,4,512,1]{2,0,1,3:T(8,128)(2,1)S(1)} %bitcast.26, bf16[8,512,4,128]{3,0,2,1:T(8,128)(2,1)S(1)} %fusion, s32[4,128]{1,0:T(4,128)S(1)} %broadcast_xor_fusion.1, s32[8,512]{1,0:T(8,128)S(1)} %broadcast_xor_fusion), kind=kOutput, calls=%fused_computation.11 | convolution fusion | flops 1078198272 | bytes 5785600 | tf_op jit(solution)/shard_map/pdc,acdb->pab/dot_general | solution.py:17
  132.1 2.1 %copy.16 = bf16[256,8,128]{2,1,0:T(8,128)(2,1)} copy(bf16[256,8,128]{0,2,1:T(8,128)(2,1)} %fusion.15) | data formatting | bytes 1048576 | tf_op jit(solution)/shard_map/convert_element_type | solution.py:18
  134.3 21.1 %all_to_all.23 = bf16[128,2,8,128]{3,2,1,0:T(8,128)(2,1)} all-to-all(bf16[128,2,8,128]{3,2,1,0:T(8,128)(2,1)} %bitcast.25), channel_id=1, replica_groups=mesh['occ'=4,'virt'=32] {'occ','virt'}, dimensions={0} | all-to-all | bytes 1048576 | tf_op jit(solution)/shard_map/all_to_all | solution.py:19
  155.4 1.8 %reduce_sum.12 = bf16[2,8,128]{2,1,0:T(8,128)(2,1)} reduce(bf16[128,2,8,128]{3,2,1,0:T(8,128)(2,1)} %all_to_all.23, bf16[]{:T(256)} %constant.3.clone.1), dimensions={0}, to_apply=%region_0.1 | reduce | flops 260096 | bytes 528386 | tf_op jit(solution)/shard_map/reduce_sum | solution.py:20
Async XLA Ops:
  6.5 103.6 %copy-start = (bf16[4,128,3072]{2,1,0:T(8,128)(2,1)S(1)}, bf16[4,128,3072]{2,1,0:T(8,128)(2,1)}, u32[]{:S(2)}) copy-start(bf16[4,128,3072]{2,1,0:T(8,128)(2,1)} %param.9) | copy-start | bytes 9437188
  6.5 10.6 %copy-start.4 = (s32[128]{0:T(128)S(1)}, s32[128]{0:T(128)}, u32[]{:S(2)}) copy-start(s32[128]{0:T(128)} %param.11) | copy-start | bytes 1540
  6.5 10.6 %copy-start.5 = (s32[4]{0:T(128)S(1)}, s32[4]{0:T(128)}, u32[]{:S(2)}) copy-start(s32[4]{0:T(128)} %param.13) | copy-start | bytes 52
  6.5 10.7 %copy-start.3 = (s32[8]{0:T(128)S(1)}, s32[8]{0:T(128)}, u32[]{:S(2)}) copy-start(s32[8]{0:T(128)} %param.10) | copy-start | bytes 100
  6.5 10.7 %copy-start.2 = (s32[512]{0:T(512)S(1)}, s32[512]{0:T(512)}, u32[]{:S(2)}) copy-start(s32[512]{0:T(512)} %param.12) | copy-start | bytes 6148
  6.5 103.5 %all-gather.2.cloned.1.call-start = ((), (), s32[]{:S(2)}) async-start(), calls=%async_computation.2 | async-start | bytes 25362432 | tf_op jit(solution)/shard_map/all_gather | solution.py:8
  11.3 20.8 %all-to-all-start = ((bf16[64,16,512]{2,0,1:T(8,128)(2,1)}), bf16[64,16,512]{2,0,1:T(8,128)(2,1)}, u32[]{:S(2)}, u32[]{:S(2)}) async-start(bf16[64,16,512]{2,0,1:T(8,128)(2,1)} %copy.13), calls=%async_computation | async-start | bytes 2097152 | tf_op jit(solution)/shard_map/all_to_all | solution.py:9
  110.1 16.7 %copy-start.1 = (bf16[64,4,4,512]{3,0,1,2:T(8,128)(2,1)S(1)}, bf16[64,4,4,512]{3,0,1,2:T(8,128)(2,1)}, u32[]{:S(2)}) copy-start(bf16[64,4,4,512]{3,0,1,2:T(8,128)(2,1)} %copy.14) | copy-start | bytes 3145732
Sparse Core Ops, SparseCore 0:
  10.5 99.5 all-gather.1

commit v2 on v1

v2 whole, which is shorter than its diff:
```python
import functools

import jax
import jax.numpy as jnp
from jax import lax
from jax.experimental import pallas as pl
from jax.experimental.pallas import tpu as pltpu
from jax.sharding import Mesh, PartitionSpec as P

ALL = ("zh", "zl", "y", "x", "core")
Z = ("zh", "zl")


def swap(block):
    return lax.ppermute(block, "core", [(0, 1), (1, 0)])


def around(block):
    pairs = [
        (z * 2 + core, (z + (1 - 2 * core)) % 4 * 2 + core) for z in range(4) for core in range(2)
    ]
    return lax.ppermute(block, Z + ("core",), pairs)


def along(block, axes):
    def moved(step):
        pairs = []
        for y in range(4):
            for x in range(4):
                for core in range(2):
                    to = ((y + step) % 4, x) if axes[core] == "y" else (y, (x + step) % 4)
                    pairs.append(((y * 4 + x) * 2 + core, (to[0] * 4 + to[1]) * 2 + core))
        return lax.ppermute(block, ("y", "x", "core"), pairs)

    return [moved(step) for step in (1, 3, 2)]


def part_kernel(amps, where, out, whole):
    spot = lax.broadcasted_iota(jnp.int32, (512, 512), 0)
    lane = lax.broadcasted_iota(jnp.int32, (512, 512), 1)
    z = lane // 8 % 2 * 2 + lane // 256
    place = lane // 64 % 4 * 128 + lane // 16 % 4 * 32 + lane // 4 % 2 * 16 + z * 4 + lane % 4
    pick = (spot == place).astype(jnp.bfloat16)
    for k in range(4):
        whole[k * 16 : k * 16 + 16] = jnp.dot(
            amps[k * 16 : k * 16 + 16].reshape(256, 512), pick, preferred_element_type=jnp.float32
        ).reshape(16, 16, 512)
    for z in range(4):
        lanes = slice(z % 2 * 256, z % 2 * 256 + 256)
        for j in range(4):
            out[z, j] = whole[:, 4 * z + j, lanes].astype(jnp.bfloat16)
        for core in range(2):

            @pl.when(where[3] == core)
            def _():
                near = (z + 2 * core - 1) % 4
                for j in range(4):
                    out[z, 4 + j] = whole[:, 4 * near + j, lanes].astype(jnp.bfloat16)


def part_amplitudes(amps, where):
    return pl.pallas_call(
        part_kernel,
        out_shape=jax.ShapeDtypeStruct((4, 8, 64, 256), jnp.bfloat16),
        in_specs=[pl.BlockSpec(memory_space=pltpu.VMEM), pl.BlockSpec(memory_space=pltpu.SMEM)],
        out_specs=pl.BlockSpec(memory_space=pltpu.VMEM),
        scratch_shapes=[pltpu.VMEM((64, 16, 512), jnp.float32)],
        compiler_params=pltpu.CompilerParams(vmem_limit_bytes=24 * 1024 * 1024),
        cost_estimate=pl.CostEstimate(flops=1 << 29, bytes_accessed=2 << 20, transcendentals=0),
    )(amps, where)


def corner(where, step, shift):
    y, x, core = where[0], where[1], where[3]
    far, near = (0, 3, 1, 2)[step], (0, 3, 1, 2)[shift] if isinstance(shift, int) else shift
    return (
        (y + jnp.where(core == 0, far, near)) % 4,
        (x + jnp.where(core == 0, near, far)) % 4,
    )


def fold_kernel(steps, offsets, *refs):
    n, n_groups = len(steps), len(offsets)
    blocks, refs = refs[:n], refs[n:]
    bds, amps, irreps = refs[:n_groups], refs[n_groups : 2 * n_groups], refs[2 * n_groups : 3 * n_groups]
    where, irrep_a, irrep_b, irrep_c, start, total, left, held, labels, sem = refs[3 * n_groups :]
    i = pl.program_id(0)

    @pl.when(i == 0)
    def _():
        copies = [
            pltpu.make_async_copy(block, left.at[pl.ds(256 * k, 256)], sem.at[k])
            for k, block in enumerate(blocks)
        ]
        for copy in copies:
            copy.start()
        total[...] = start[...]
        held[...] = jnp.zeros_like(held)
        row = lax.broadcasted_iota(jnp.int32, (256, 1), 0)
        shift, inner = row // 64, row % 16
        shift = jnp.where(shift == 1, 3, jnp.where(shift == 0, 0, shift - 1))
        lane = lax.broadcasted_iota(jnp.int32, (256, 512), 1)
        label_a = jnp.zeros((256, 1), jnp.int32)
        for a in range(4):
            label_a = jnp.where(row // 16 % 4 == a, irrep_a[where[3] * 4 + a], label_a)
        for k, step in enumerate(steps):
            y, x = corner(where, step, shift)
            z = inner // 8 * 2 + where[2]
            place = y * 128 + x * 32 + inner // 4 % 2 * 16 + z * 4 + inner % 4
            found = jnp.sum(
                jnp.where(lane == place, irrep_c[...].astype(jnp.float32), 0.0), axis=1, keepdims=True
            )
            labels[k * 256 : k * 256 + 256] = found.astype(jnp.int32) ^ label_a
        for copy in copies:
            copy.wait()

    for g in range(n_groups):
        for half in range(2):

            @pl.when(i == 2 * g + half)
            def _():
                integral = lax.dot_general(
                    left[...], bds[g][...].reshape(256, 3072), (((1,), (1,)), ((), ())),
                    preferred_element_type=jnp.float32,
                )
                pair = jnp.concatenate(
                    [irrep_b[...] ^ irreps[g][offsets[g] + 2 * half + d] for d in range(2)], axis=1
                )
                kept = jnp.where(labels[...] == pair, integral, 0.0).astype(jnp.bfloat16)
                for k, step in enumerate(steps):
                    for shift in range(4):
                        y, x = corner(where, step, shift)
                        to = pl.ds(pl.multiple_of(y * 64 + x * 16, 16), 16)
                        for a in range(4):
                            row = k * 256 + shift * 64 + a * 16
                            for d in range(2):
                                held[d, to, a * 128 : a * 128 + 128] = kept[
                                    row : row + 16, d * 128 : d * 128 + 128
                                ]
                total[...] += sum(
                    jnp.dot(
                        amps[g][:, d].reshape(256, 256), held[d], preferred_element_type=jnp.float32
                    )
                    for d in range(2)
                )


def fold(steps, blocks, groups, where, irrep_a, irrep_b, irrep_c, start):
    n, n_groups = len(steps), len(groups)
    rows = 256 * n
    smem, any_spec = pl.BlockSpec(memory_space=pltpu.SMEM), pl.BlockSpec(memory_space=pl.ANY)

    def half_of(g, i):
        return (jnp.clip(i - 2 * g, 0, 1), 0, 0)

    def amps_of(g, first, i):
        return (0, jnp.clip(i - 2 * g, 0, 1) + first, 0, 0)

    return pl.pallas_call(
        functools.partial(fold_kernel, steps, tuple(g[4] for g in groups)),
        grid=(2 * n_groups,),
        out_shape=jax.ShapeDtypeStruct((256, 512), jnp.float32),
        in_specs=[any_spec] * n
        + [pl.BlockSpec((2, 128, 3072), functools.partial(half_of, g)) for g in range(n_groups)]
        + [
            pl.BlockSpec((4, 2, 64, 256), functools.partial(amps_of, g, group[2]))
            for g, group in enumerate(groups)
        ]
        + [smem] * (n_groups + 2)
        + [
            pl.BlockSpec((1, 128), lambda i: (0, 0)),
            pl.BlockSpec((1, 512), lambda i: (0, 0)),
            pl.BlockSpec((256, 512), lambda i: (0, 0)),
        ],
        out_specs=pl.BlockSpec((256, 512), lambda i: (0, 0)),
        scratch_shapes=[
            pltpu.VMEM((rows, 3072), jnp.bfloat16),
            pltpu.VMEM((2, 256, 512), jnp.bfloat16),
            pltpu.VMEM((rows, 1), jnp.int32),
            pltpu.SemaphoreType.DMA((n,)),
        ],
        compiler_params=pltpu.CompilerParams(vmem_limit_bytes=30 * 1024 * 1024),
        cost_estimate=pl.CostEstimate(
            flops=2 * rows * 512 * n_groups * 3072, bytes_accessed=rows * 6144 + (n_groups * 3 << 20), transcendentals=0
        ),
    )(
        *[blocks[s] for s in steps], *[g[0] for g in groups], *[g[1] for g in groups],
        *[g[3] for g in groups], where, irrep_a, irrep_b, irrep_c, start,
    )


def body(amplitudes, ac_factor, bd_factor, irrep_a, irrep_b, irrep_c, irrep_d):
    where = jnp.stack([lax.axis_index(name) for name in ("y", "x", "zl", "core")]).astype(jnp.int32)
    zh, core = lax.axis_index("zh"), lax.axis_index("core")

    by_core = ac_factor.reshape(2, 16, 3072)
    mine = lax.dynamic_index_in_dim(by_core, core, 0, keepdims=False)
    theirs = lax.dynamic_index_in_dim(by_core, 1 - core, 0, keepdims=False)
    mine, theirs, amplitudes = lax.optimization_barrier((mine, theirs, amplitudes))
    from_core = swap(theirs)
    from_z = lax.ppermute(mine, "zh", [(0, 1), (1, 0)])
    from_both = lax.ppermute(theirs, ("zh", "core"), [(0, 3), (1, 2), (2, 1), (3, 0)])

    amps = part_amplitudes(amplitudes, where)
    near = around(irrep_d)
    other_far = swap(jnp.concatenate([irrep_d, near]))
    bd_core = swap(bd_factor)
    mine, from_core, from_z, from_both, amps, other_far, bd_sent = lax.optimization_barrier(
        (mine, from_core, from_z, from_both, amps, other_far, bd_factor)
    )

    amps = lax.all_to_all(amps, Z, split_axis=0, concat_axis=0, tiled=True)
    amps_other = swap(amps)

    first, second = jnp.where(core == 0, mine, from_core), jnp.where(core == 0, from_core, mine)
    third, fourth = jnp.where(core == 0, from_z, from_both), jnp.where(core == 0, from_both, from_z)
    pieces = jnp.stack([
        jnp.where(zh == 0, first, third), jnp.where(zh == 0, second, fourth),
        jnp.where(zh == 0, third, first), jnp.where(zh == 0, fourth, second),
    ])
    rows = pieces.reshape(4, 4, 4, 3072).transpose(1, 0, 2, 3).reshape(64, 3072)
    rows = jnp.concatenate([rows] + along(rows, "xy"), axis=0)
    blocks = [rows] + along(rows, "yx")

    bd_near = around(bd_sent)

    early = [(bd_factor, amps, 0, irrep_d, 0), (bd_core, amps_other, 0, other_far, 0)]
    rest = (where, irrep_a, irrep_b.reshape(1, 128), irrep_c.reshape(1, 512))
    total = jnp.zeros((256, 512), jnp.float32)
    total = fold((0, 1, 2), blocks, early, *rest, total)
    bd_near, total = lax.optimization_barrier((bd_near, total))
    bd_far = swap(bd_near)
    late = [(bd_near, amps, 2, near, 0), (bd_far, amps_other, 2, other_far, 4)]
    total = fold((0, 1, 2), blocks, late, *rest, total)
    total = fold((3,), blocks, early + late, *rest, total)

    pieces = total.astype(jnp.bfloat16).reshape(128, 2, 512)
    pieces = lax.all_to_all(pieces, ALL, split_axis=0, concat_axis=0, tiled=True)
    summed = jnp.sum(pieces.reshape(64, 2, 2, 512).astype(jnp.float32), axis=0)
    return summed.reshape(2, 2, 4, 128).transpose(1, 0, 2, 3).reshape(2, 8, 128).astype(jnp.bfloat16)


def solution(mesh):
    fine = Mesh(mesh.devices.reshape(2, 2, 4, 4, 2), ALL)
    virt = ("y", "x", "core")
    return jax.shard_map(
        body,
        mesh=fine,
        in_specs=(
            P(Z, virt, None),
            P(None, virt + Z, None),
            P(virt + Z, None, None),
            P(),
            P(),
            P(),
            P(virt + Z),
        ),
        out_specs=P(ALL, None, None),
        check_vma=False,
    )
```

time: 164 us -> 140 us (0.85)
  waiting for transfers between devices: 90.4 us -> 45 us
  Pallas kernels: 0 us -> 42.4 us
  matrix products: 22 us -> 0 us
  starting transfers between devices: 5.89 us -> 27.7 us
  between operations: 13.4 us -> 0.19 us
  local copies, waits for them, and re-layouts: 9.21 us -> 5.4 us
  blocking collectives: 21.1 us -> 17.9 us
    all_gather x1 -> x0, waiting for transfers between devices: 75.6 us -> none  [body(): left = lax.all_gather(ac_factor, ('virt', 'occ'), axis=1, tiled=True)]
    pallas_call x0 -> x4, Pallas kernels: none -> 42.4 us  [the longest x3 38.2 us: fold(): pl.pallas_call(functools.partial(fold_kernel, steps, tuple((g[4] for g in...]
    ppermute x0 -> x15, starting transfers between devices: none -> 24.2 us  [the longest x6 8.81 us: moved(): return lax.ppermute(block, ('y', 'x', 'core'), pairs)]
    dot_general x2 -> x0, matrix products: 22 us -> none  [the longest x1 16.7 us: body(): lax.dot_general(left, bd_factor, (((2,), (2,)), ((), ())), preferred_elem...]
    all_to_all x1, waiting for transfers between devices: 14.8 us -> 30.4 us  [body(): amps = lax.all_to_all(amps, Z, split_axis=0, concat_axis=0, tiled=True)]
    ppermute x0 -> x15, waiting for transfers between devices: none -> 14.6 us  [the longest x6 7.52 us: moved(): return lax.ppermute(block, ('y', 'x', 'core'), pairs)]
    all_to_all x1, blocking collectives: 21.1 us -> 17.9 us  [body(): lax.all_to_all(pieces, ALL, split_axis=0, concat_axis=0, tiled=True)]
    all_to_all x1 -> x0, local copies, waits for them, and re-layouts: 2.38 us -> none  [body(): lax.all_to_all(amplitudes, 'occ', split_axis=1, concat_axis=0, tiled=True)]
  transfers between devices with their start and end apart: 2 -> 16, of which waited for: 2 -> 7; matrix products, arithmetic and copies ran while one was open for 3% -> 2% of each run, Pallas kernels for 0% -> 21%
where the time goes in v2:
time: 140 us; the launch traced here: 139 us
  waiting for transfers between devices  45 us (32%)
  Pallas kernels  42.4 us (30%)
  starting transfers between devices  27.7 us (20%)
  blocking collectives  17.9 us (13%)
  local copies, waits for them, and re-layouts  5.4 us (4%)
    pallas_call x3, Pallas kernels, fold(): pl.pallas_call(functools.partial(fold_kernel, steps, tuple((g[4] for g in...  38.2 us
    all_to_all x1, waiting for transfers between devices, body(): amps = lax.all_to_all(amps, Z, split_axis=0, concat_axis=0, tiled=True)  30.4 us
    all_to_all x1, blocking collectives, body(): lax.all_to_all(pieces, ALL, split_axis=0, concat_axis=0, tiled=True)  17.9 us
    ppermute x6, starting transfers between devices, moved(): return lax.ppermute(block, ('y', 'x', 'core'), pairs)  8.81 us
    ppermute x5, starting transfers between devices, swap(): return lax.ppermute(block, 'core', [(0, 1), (1, 0)])  8.05 us
    ppermute x6, waiting for transfers between devices, moved(): return lax.ppermute(block, ('y', 'x', 'core'), pairs)  7.52 us
    ppermute x5, waiting for transfers between devices, swap(): return lax.ppermute(block, 'core', [(0, 1), (1, 0)])  7.09 us
    pallas_call x1, Pallas kernels, part_amplitudes(): pl.pallas_call(part_kernel, out_shape=jax.ShapeDtypeStruct((4, 8, 64, 256...  4.19 us
  transfers between devices with their start and end apart: 16, of which 7 were waited for; matrix products, arithmetic and copies ran while one was open for 2% of the time, Pallas kernels for 21%

profile of v2, /device:TPU:1, one launch (start us, length us, event | category | flops | bytes accessed | tf_op | source)
XLA Modules:
  0.0 139.4 jit_solution(8320929707876481280)
XLA Ops:
  0.0 0.0 copy-start.2
  0.0 1.0 reshape.31
  1.0 1.5 %collective-permute-start = (bf16[16,3072]{1,0:T(8,128)(2,1)S(1)}, bf16[16,3072]{1,0:T(8,128)(2,1)S(1)}, u32[]{:S(2)}, u32[]{:S(2)}) collective-permute-start(bf16[16,3072]{1,0:T(8,128)(2,1)S(1)} %get-tuple-element.18), channel_id=1, source_target_pairs={{0,1},{1,0},{2,3},{3,2},{4,5},{5,4},{6,7},{7,6},{8,9},{9,8},{10,11... | collective-permute-start | bytes 294920 | tf_op jit(solution)/shard_map/ppermute | solution.py:15
  2.5 3.7 %collective-permute-start.2 = (bf16[16,3072]{1,0:T(8,128)(2,1)S(1)}, bf16[16,3072]{1,0:T(8,128)(2,1)S(1)}, u32[]{:S(2)}, u32[]{:S(2)}) collective-permute-start(bf16[16,3072]{1,0:T(8,128)(2,1)S(1)} %get-tuple-element.18), channel_id=1, source_target_pairs={{0,65},{1,64},{64,1},{65,0},{2,67},{3,66},{66,3},{67,2},{4,69},{5,... | collective-permute-start | bytes 294920 | tf_op jit(solution)/shard_map/ppermute | solution.py:202
  6.2 0.1 collective-permute-start.1
  6.2 3.1 %collective-permute-start.3 = (s32[4]{0:T(128)}, s32[4]{0:T(128)S(1)}, u32[]{:S(2)}, u32[]{:S(2)}) collective-permute-start(s32[4]{0:T(128)} %refs_9_.1), channel_id=1, source_target_pairs={{0,32},{1,97},{32,64},{33,1},{64,96},{65,33},{96,0},{97,65},{2,34}... | collective-permute-start | bytes 56 | tf_op jit(solution)/shard_map/ppermute | solution.py:22
  9.3 0.0 collective-permute-start.9
  9.3 0.1 pad_add_fusion.where.refs_9_.refs_13_
  9.4 0.0 copy-start
  9.4 1.2 copy-done
  10.6 4.2 %shard_map.73 = bf16[4,8,64,256]{3,2,1,0:T(8,128)(2,1)} custom-call(bf16[64,16,512]{2,1,0:T(8,128)(2,1)S(1)} %copy-done, s32[4]{0:T(128)S(1)} %pad_add_fusion.where.refs_9_.refs_13_), custom_call_target="tpu_custom_call" | custom-call | flops 536870912 | bytes 2097152 | tf_op jit(solution)/shard_map/pallas_call | solution.py:62
  14.8 0.0 collective-permute-done.3.refs_7_.refs_11_
  14.8 0.0 copy-done.2
  14.8 0.1 pad_add_fusion.1
  14.9 0.5 collective-permute-start.4
  15.4 0.8 collective-permute-done.4.refs_8_.refs_10_.refs_12_
  16.2 0.0 collective-permute-done
  16.3 0.0 collective-permute-done.1
  16.3 0.0 collective-permute-done.2
  16.5 0.3 maximum_bitcast_fusion
  16.8 0.1 reshape.32
  16.9 1.4 collective-permute-start.5
  18.3 1.5 %collective-permute-start.6 = (bf16[64,3072]{1,0:T(8,128)(2,1)S(1)}, bf16[64,3072]{1,0:T(8,128)(2,1)S(1)}, u32[]{:S(2)}, u32[]{:S(2)}) collective-permute-start(bf16[64,3072]{1,0:T(8,128)(2,1)S(1)} %reshape.32), channel_id=1, source_target_pairs={{0,6},{1,25},{2,0},{3,27},{4,2},{5,29},{6,4},{7,31},{8,14},{9,1},{... | collective-permute-start | bytes 1179656 | tf_op jit(solution)/shard_map/ppermute | solution.py:33
  19.8 0.5 collective-permute-start.10
  20.3 1.6 %collective-permute-start.7 = (bf16[64,3072]{1,0:T(8,128)(2,1)S(1)}, bf16[64,3072]{1,0:T(8,128)(2,1)}, u32[]{:S(2)}, u32[]{:S(2)}) collective-permute-start(bf16[64,3072]{1,0:T(8,128)(2,1)S(1)} %reshape.32), channel_id=1, source_target_pairs={{0,4},{1,17},{2,6},{3,19},{4,0},{5,21},{6,2},{7,23},{8,12},{9,25},... | collective-permute-start | bytes 1179656 | tf_op jit(solution)/shard_map/ppermute | solution.py:33
  22.0 3.5 %all-to-all-start = ((bf16[4,8,64,256]{3,2,1,0:T(8,128)(2,1)}), bf16[4,8,64,256]{3,2,1,0:T(8,128)(2,1)S(1)}, u32[]{:S(2)}, u32[]{:S(2)}) async-start(bf16[4,8,64,256]{3,2,1,0:T(8,128)(2,1)} %shard_map.73), calls=%async_computation | async-start | bytes 2097152 | tf_op jit(solution)/shard_map/all_to_all | solution.py:212
  25.5 0.0 copy-start.1
  25.5 0.0 copy-start.3
  25.5 0.0 copy-start.4
  25.5 0.0 collective-permute-done.5
  25.5 1.0 constant_dynamic-update-slice_fusion.2
  26.6 2.2 %collective-permute-done.6 = bf16[64,3072]{1,0:T(8,128)(2,1)S(1)} collective-permute-done((bf16[64,3072]{1,0:T(8,128)(2,1)S(1)}, bf16[64,3072]{1,0:T(8,128)(2,1)S(1)}, u32[]{:S(2)}, u32[]{:S(2)}) %collective-permute-start.6) | collective-permute-done | bytes 393248 | tf_op jit(solution)/shard_map/ppermute | solution.py:33
  28.8 1.9 %collective-permute-done.7 = bf16[64,3072]{1,0:T(8,128)(2,1)} collective-permute-done((bf16[64,3072]{1,0:T(8,128)(2,1)S(1)}, bf16[64,3072]{1,0:T(8,128)(2,1)}, u32[]{:S(2)}, u32[]{:S(2)}) %collective-permute-start.7) | collective-permute-done | bytes 393248 | tf_op jit(solution)/shard_map/ppermute | solution.py:33
  30.7 1.0 constant_dynamic-update-slice_fusion.refs_0_
  31.7 1.0 collective-permute-start.11
  32.7 1.8 %collective-permute-start.12 = (bf16[256,3072]{1,0:T(8,128)(2,1)S(1)}, bf16[256,3072]{1,0:T(8,128)(2,1)}, u32[]{:S(2)}, u32[]{:S(2)}) collective-permute-start(bf16[256,3072]{1,0:T(8,128)(2,1)S(1)} %constant_dynamic-update-slice_fusion.refs_0_), channel_id=1, source_target_pairs={{0,24},{1,7},{2,26},{3,1},{4,28},{5,3},{6,30},{7,5},{8,0},{9,15},{... | collective-permute-start | bytes 4718600 | tf_op jit(solution)/shard_map/ppermute | solution.py:33
  34.4 30.4 %all-to-all-done.refs_5_.refs_7_ = bf16[4,8,64,256]{3,2,1,0:T(8,128)(2,1)S(1)} async-done(((bf16[4,8,64,256]{3,2,1,0:T(8,128)(2,1)}), bf16[4,8,64,256]{3,2,1,0:T(8,128)(2,1)S(1)}, u32[]{:S(2)}, u32[]{:S(2)}) %all-to-all-start) | async-done | bytes 1048608 | tf_op jit(solution)/shard_map/all_to_all | solution.py:212
  64.9 5.6 %collective-permute-start.13 = (bf16[4,8,64,256]{3,2,1,0:T(8,128)(2,1)S(1)}, bf16[4,8,64,256]{3,2,1,0:T(8,128)(2,1)S(1)}, u32[]{:S(2)}, u32[]{:S(2)}) collective-permute-start(bf16[4,8,64,256]{3,2,1,0:T(8,128)(2,1)S(1)} %all-to-all-done.refs_5_.refs_7_), channel_id=1, source_target_pairs={{0,1},{1,0},{2,3},{3,2},{4,5},{5,4},{6,7},{7,6},{8,9},{9,8},{10,11... | collective-permute-start | bytes 3145736 | tf_op jit(solution)/shard_map/ppermute | solution.py:15
  70.4 2.3 %collective-permute-done.13.refs_6_.refs_8_ = bf16[4,8,64,256]{3,2,1,0:T(8,128)(2,1)S(1)} collective-permute-done((bf16[4,8,64,256]{3,2,1,0:T(8,128)(2,1)S(1)}, bf16[4,8,64,256]{3,2,1,0:T(8,128)(2,1)S(1)}, u32[]{:S(2)}, u32[]{:S(2)}) %collective-permute-start.13) | collective-permute-done | bytes 1048608 | tf_op jit(solution)/shard_map/ppermute | solution.py:15
  72.7 0.0 collective-permute-done.11.refs_1_
  72.7 0.0 collective-permute-done.12.refs_2_
  72.7 0.0 collective-permute-done.9.refs_4_.refs_2_
  72.7 0.1 broadcast_in_dim.3.refs_13_
  72.8 0.0 copy-done.1
  72.8 0.0 copy-done.3
  72.8 0.0 copy-done.4
  72.8 12.6 %shard_map.74.refs_13_ = f32[256,512]{1,0:T(8,128)S(1)} custom-call(bf16[256,3072]{1,0:T(8,128)(2,1)S(1)} %constant_dynamic-update-slice_fusion.refs_0_, bf16[256,3072]{1,0:T(8,128)(2,1)} %collective-permute-done.11.refs_1_, bf16[256,3072]{1,0:T(8,128)(2,1)} %collective-permute-done.12.refs_2_, bf16[4,128,3072]{2,1,0:T(8,128)(2,1)} %refs_1_.1, ...), custom_call_target="tpu_custom_call" | custom-call | flops 4831838208 | bytes 11010048 | tf_op jit(solution)/shard_map/pallas_call | solution.py:159
  85.4 0.0 collective-permute-done.10.refs_3_
  85.4 0.4 collective-permute-start.14
  85.9 1.5 %collective-permute-start.8 = (bf16[256,3072]{1,0:T(8,128)(2,1)S(1)}, bf16[256,3072]{1,0:T(8,128)(2,1)S(1)}, u32[]{:S(2)}, u32[]{:S(2)}) collective-permute-start(bf16[256,3072]{1,0:T(8,128)(2,1)S(1)} %constant_dynamic-update-slice_fusion.refs_0_), channel_id=1, source_target_pairs={{0,16},{1,5},{2,18},{3,7},{4,20},{5,1},{6,22},{7,3},{8,24},{9,13},... | collective-permute-start | bytes 4718600 | tf_op jit(solution)/shard_map/ppermute | solution.py:33
  87.4 4.0 %collective-permute-done.14.refs_4_ = bf16[4,128,3072]{2,1,0:T(8,128)(2,1)S(1)} collective-permute-done((bf16[4,128,3072]{2,1,0:T(8,128)(2,1)}, bf16[4,128,3072]{2,1,0:T(8,128)(2,1)S(1)}, u32[]{:S(2)}, u32[]{:S(2)}) %collective-permute-start.14) | collective-permute-done | bytes 3145760 | tf_op jit(solution)/shard_map/ppermute | solution.py:15
  91.4 12.1 %shard_map.75.refs_17_ = f32[256,512]{1,0:T(8,128)S(1)} custom-call(bf16[256,3072]{1,0:T(8,128)(2,1)S(1)} %constant_dynamic-update-slice_fusion.refs_0_, bf16[256,3072]{1,0:T(8,128)(2,1)} %collective-permute-done.11.refs_1_, bf16[256,3072]{1,0:T(8,128)(2,1)} %collective-permute-done.12.refs_2_, bf16[4,128,3072]{2,1,0:T(8,128)(2,1)} %collective-permute-done.10.refs_3_, ...), custom_call_target="tpu_custom_call" | custom-call | flops 4831838208 | bytes 11010048 | tf_op jit(solution)/shard_map/pallas_call | solution.py:159
  103.5 3.4 %collective-permute-done.8.refs_0_ = bf16[256,3072]{1,0:T(8,128)(2,1)S(1)} collective-permute-done((bf16[256,3072]{1,0:T(8,128)(2,1)S(1)}, bf16[256,3072]{1,0:T(8,128)(2,1)S(1)}, u32[]{:S(2)}, u32[]{:S(2)}) %collective-permute-start.8) | collective-permute-done | bytes 1572896 | tf_op jit(solution)/shard_map/ppermute | solution.py:33
  106.9 13.5 %shard_map.76 = f32[256,512]{1,0:T(8,128)S(1)} custom-call(bf16[256,3072]{1,0:T(8,128)(2,1)S(1)} %collective-permute-done.8.refs_0_, bf16[4,128,3072]{2,1,0:T(8,128)(2,1)} %refs_1_.1, bf16[4,128,3072]{2,1,0:T(8,128)(2,1)} %collective-permute-done.9.refs_4_.refs_2_, bf16[4,128,3072]{2,1,0:T(8,128)(2,1)} %collective-permute-done.10.refs_3_, ...), custom_call_target="tpu_custom_call" | custom-call | flops 3221225472 | bytes 14155776 | tf_op jit(solution)/shard_map/pallas_call | solution.py:159
  120.5 0.1 reshape.35
  120.6 17.9 %all_to_all.10 = bf16[128,2,512]{2,1,0:T(2,128)(2,1)S(1)} all-to-all(bf16[128,2,512]{2,1,0:T(2,128)(2,1)S(1)} %reshape.35), channel_id=1, replica_groups=mesh['zh'=2,'zl'=2,'y'=4,'x'=4,'core'=2] {'zh','zl','y','x','core'}, dimensions={0} | all-to-all | bytes 524288 | tf_op jit(solution)/shard_map/all_to_all | solution.py:238
  138.5 0.2 reduce
  138.8 0.6 copy.8
  (10 shorter events, 0.3 us)
Async XLA Ops:
  0.0 14.8 %copy-start.2 = (s32[4]{0:T(128)S(1)}, s32[4]{0:T(128)}, u32[]{:S(2)}) copy-start(s32[4]{0:T(128)} %refs_9_.1) | copy-start | bytes 52
  1.0 15.2 %collective-permute-start = (bf16[16,3072]{1,0:T(8,128)(2,1)S(1)}, bf16[16,3072]{1,0:T(8,128)(2,1)S(1)}, u32[]{:S(2)}, u32[]{:S(2)}) collective-permute-start(bf16[16,3072]{1,0:T(8,128)(2,1)S(1)} %get-tuple-element.18), channel_id=1, source_target_pairs={{0,1},{1,0},{2,3},{3,2},{4,5},{5,4},{6,7},{7,6},{8,9},{9,8},{10,11... | collective-permute-start | bytes 294920 | tf_op jit(solution)/shard_map/ppermute | solution.py:15
  2.5 13.7 %collective-permute-start.2 = (bf16[16,3072]{1,0:T(8,128)(2,1)S(1)}, bf16[16,3072]{1,0:T(8,128)(2,1)S(1)}, u32[]{:S(2)}, u32[]{:S(2)}) collective-permute-start(bf16[16,3072]{1,0:T(8,128)(2,1)S(1)} %get-tuple-element.18), channel_id=1, source_target_pairs={{0,65},{1,64},{64,1},{65,0},{2,67},{3,66},{66,3},{67,2},{4,69},{5,... | collective-permute-start | bytes 294920 | tf_op jit(solution)/shard_map/ppermute | solution.py:202
  6.2 10.1 %collective-permute-start.1 = (bf16[16,3072]{1,0:T(8,128)(2,1)S(1)}, bf16[16,3072]{1,0:T(8,128)(2,1)S(1)}, u32[]{:S(2)}, u32[]{:S(2)}) collective-permute-start(bf16[16,3072]{1,0:T(8,128)(2,1)S(1)} %get-tuple-element.20), channel_id=1, source_target_pairs={{0,64},{64,0},{1,65},{65,1},{2,66},{66,2},{3,67},{67,3},{4,68},{68... | collective-permute-start | bytes 294920 | tf_op jit(solution)/shard_map/ppermute | solution.py:201
  6.2 8.6 %collective-permute-start.3 = (s32[4]{0:T(128)}, s32[4]{0:T(128)S(1)}, u32[]{:S(2)}, u32[]{:S(2)}) collective-permute-start(s32[4]{0:T(128)} %refs_9_.1), channel_id=1, source_target_pairs={{0,32},{1,97},{32,64},{33,1},{64,96},{65,33},{96,0},{97,65},{2,34}... | collective-permute-start | bytes 56 | tf_op jit(solution)/shard_map/ppermute | solution.py:22
  9.3 63.4 %collective-permute-start.9 = (bf16[4,128,3072]{2,1,0:T(8,128)(2,1)}, bf16[4,128,3072]{2,1,0:T(8,128)(2,1)}, u32[]{:S(2)}, u32[]{:S(2)}) collective-permute-start(bf16[4,128,3072]{2,1,0:T(8,128)(2,1)} %refs_1_.1), channel_id=1, source_target_pairs={{0,1},{1,0},{2,3},{3,2},{4,5},{5,4},{6,7},{7,6},{8,9},{9,8},{10,11... | collective-permute-start | bytes 9437192 | tf_op jit(solution)/shard_map/ppermute | solution.py:15
  9.4 1.2 copy-start
  14.9 1.3 collective-permute-start.4
  16.9 8.6 %collective-permute-start.5 = (bf16[64,3072]{1,0:T(8,128)(2,1)S(1)}, bf16[64,3072]{1,0:T(8,128)(2,1)}, u32[]{:S(2)}, u32[]{:S(2)}) collective-permute-start(bf16[64,3072]{1,0:T(8,128)(2,1)S(1)} %reshape.32), channel_id=1, source_target_pairs={{0,2},{1,9},{2,4},{3,11},{4,6},{5,13},{6,0},{7,15},{8,10},{9,17},{... | collective-permute-start | bytes 1179656 | tf_op jit(solution)/shard_map/ppermute | solution.py:33
  18.3 10.5 %collective-permute-start.6 = (bf16[64,3072]{1,0:T(8,128)(2,1)S(1)}, bf16[64,3072]{1,0:T(8,128)(2,1)S(1)}, u32[]{:S(2)}, u32[]{:S(2)}) collective-permute-start(bf16[64,3072]{1,0:T(8,128)(2,1)S(1)} %reshape.32), channel_id=1, source_target_pairs={{0,6},{1,25},{2,0},{3,27},{4,2},{5,29},{6,4},{7,31},{8,14},{9,1},{... | collective-permute-start | bytes 1179656 | tf_op jit(solution)/shard_map/ppermute | solution.py:33
  19.8 65.6 %collective-permute-start.10 = (bf16[4,128,3072]{2,1,0:T(8,128)(2,1)}, bf16[4,128,3072]{2,1,0:T(8,128)(2,1)}, u32[]{:S(2)}, u32[]{:S(2)}) collective-permute-start(bf16[4,128,3072]{2,1,0:T(8,128)(2,1)} %refs_1_.1), channel_id=1, source_target_pairs={{0,32},{1,97},{32,64},{33,1},{64,96},{65,33},{96,0},{97,65},{2,34}... | collective-permute-start | bytes 9437192 | tf_op jit(solution)/shard_map/ppermute | solution.py:22
  20.3 10.3 %collective-permute-start.7 = (bf16[64,3072]{1,0:T(8,128)(2,1)S(1)}, bf16[64,3072]{1,0:T(8,128)(2,1)}, u32[]{:S(2)}, u32[]{:S(2)}) collective-permute-start(bf16[64,3072]{1,0:T(8,128)(2,1)S(1)} %reshape.32), channel_id=1, source_target_pairs={{0,4},{1,17},{2,6},{3,19},{4,0},{5,21},{6,2},{7,23},{8,12},{9,25},... | collective-permute-start | bytes 1179656 | tf_op jit(solution)/shard_map/ppermute | solution.py:33
  22.0 42.9 %all-to-all-start = ((bf16[4,8,64,256]{3,2,1,0:T(8,128)(2,1)}), bf16[4,8,64,256]{3,2,1,0:T(8,128)(2,1)S(1)}, u32[]{:S(2)}, u32[]{:S(2)}) async-start(bf16[4,8,64,256]{3,2,1,0:T(8,128)(2,1)} %shard_map.73), calls=%async_computation | async-start | bytes 2097152 | tf_op jit(solution)/shard_map/all_to_all | solution.py:212
  25.5 47.3 %copy-start.1 = (s32[512]{0:T(512)S(1)}, s32[512]{0:T(512)}, u32[]{:S(2)}) copy-start(s32[512]{0:T(512)} %param.12) | copy-start | bytes 6148
  25.5 47.3 %copy-start.3 = (s32[8]{0:T(128)S(1)}, s32[8]{0:T(128)}, u32[]{:S(2)}) copy-start(s32[8]{0:T(128)} %refs_14_.1) | copy-start | bytes 100
  25.5 47.3 %copy-start.4 = (s32[128]{0:T(128)S(1)}, s32[128]{0:T(128)}, u32[]{:S(2)}) copy-start(s32[128]{0:T(128)} %param.11) | copy-start | bytes 1540
  31.7 41.0 %collective-permute-start.11 = (bf16[256,3072]{1,0:T(8,128)(2,1)S(1)}, bf16[256,3072]{1,0:T(8,128)(2,1)}, u32[]{:S(2)}, u32[]{:S(2)}) collective-permute-start(bf16[256,3072]{1,0:T(8,128)(2,1)S(1)} %constant_dynamic-update-slice_fusion.refs_0_), channel_id=1, source_target_pairs={{0,8},{1,3},{2,10},{3,5},{4,12},{5,7},{6,14},{7,1},{8,16},{9,11},{... | collective-permute-start | bytes 4718600 | tf_op jit(solution)/shard_map/ppermute | solution.py:33
  32.7 40.1 %collective-permute-start.12 = (bf16[256,3072]{1,0:T(8,128)(2,1)S(1)}, bf16[256,3072]{1,0:T(8,128)(2,1)}, u32[]{:S(2)}, u32[]{:S(2)}) collective-permute-start(bf16[256,3072]{1,0:T(8,128)(2,1)S(1)} %constant_dynamic-update-slice_fusion.refs_0_), channel_id=1, source_target_pairs={{0,24},{1,7},{2,26},{3,1},{4,28},{5,3},{6,30},{7,5},{8,0},{9,15},{... | collective-permute-start | bytes 4718600 | tf_op jit(solution)/shard_map/ppermute | solution.py:33
  64.9 7.9 %collective-permute-start.13 = (bf16[4,8,64,256]{3,2,1,0:T(8,128)(2,1)S(1)}, bf16[4,8,64,256]{3,2,1,0:T(8,128)(2,1)S(1)}, u32[]{:S(2)}, u32[]{:S(2)}) collective-permute-start(bf16[4,8,64,256]{3,2,1,0:T(8,128)(2,1)S(1)} %all-to-all-done.refs_5_.refs_7_), channel_id=1, source_target_pairs={{0,1},{1,0},{2,3},{3,2},{4,5},{5,4},{6,7},{7,6},{8,9},{9,8},{10,11... | collective-permute-start | bytes 3145736 | tf_op jit(solution)/shard_map/ppermute | solution.py:15
  85.4 6.0 %collective-permute-start.14 = (bf16[4,128,3072]{2,1,0:T(8,128)(2,1)}, bf16[4,128,3072]{2,1,0:T(8,128)(2,1)S(1)}, u32[]{:S(2)}, u32[]{:S(2)}) collective-permute-start(bf16[4,128,3072]{2,1,0:T(8,128)(2,1)} %collective-permute-done.10.refs_3_), channel_id=1, source_target_pairs={{0,1},{1,0},{2,3},{3,2},{4,5},{5,4},{6,7},{7,6},{8,9},{9,8},{10,11... | collective-permute-start | bytes 9437192 | tf_op jit(solution)/shard_map/ppermute | solution.py:15
  85.9 21.1 %collective-permute-start.8 = (bf16[256,3072]{1,0:T(8,128)(2,1)S(1)}, bf16[256,3072]{1,0:T(8,128)(2,1)S(1)}, u32[]{:S(2)}, u32[]{:S(2)}) collective-permute-start(bf16[256,3072]{1,0:T(8,128)(2,1)S(1)} %constant_dynamic-update-slice_fusion.refs_0_), channel_id=1, source_target_pairs={{0,16},{1,5},{2,18},{3,7},{4,20},{5,1},{6,22},{7,3},{8,24},{9,13},... | collective-permute-start | bytes 4718600 | tf_op jit(solution)/shard_map/ppermute | solution.py:33

commit v3 on v1

v3 whole, which is shorter than its diff:
```python
import functools

import jax
import jax.numpy as jnp
from jax import lax
from jax.experimental import pallas as pl
from jax.experimental.pallas import tpu as pltpu
from jax.sharding import Mesh, PartitionSpec as P

ALL = ("zh", "zl", "y", "x", "core")
Z = ("zh", "zl")


def swap(block):
    return lax.ppermute(block, "core", [(0, 1), (1, 0)])


def around(block):
    pairs = [
        (z * 2 + core, (z + (1 - 2 * core)) % 4 * 2 + core) for z in range(4) for core in range(2)
    ]
    return lax.ppermute(block, Z + ("core",), pairs)


def along(block, axes, steps=(1, 3, 2)):
    def moved(step):
        pairs = []
        for y in range(4):
            for x in range(4):
                for core in range(2):
                    to = ((y + step) % 4, x) if axes[core] == "y" else (y, (x + step) % 4)
                    pairs.append(((y * 4 + x) * 2 + core, (to[0] * 4 + to[1]) * 2 + core))
        return lax.ppermute(block, ("y", "x", "core"), pairs)

    return [moved(step) for step in steps]


def part_kernel(amps, where, own, one, two, three, whole):
    spot = lax.broadcasted_iota(jnp.int32, (512, 512), 0)
    lane = lax.broadcasted_iota(jnp.int32, (512, 512), 1)
    z = lane // 8 % 2 * 2 + lane // 256
    place = lane // 64 % 4 * 128 + lane // 16 % 4 * 32 + lane // 4 % 2 * 16 + z * 4 + lane % 4
    pick = (spot == place).astype(jnp.bfloat16)
    for k in range(4):
        picked = jnp.dot(
            amps[k * 16 : k * 16 + 16].reshape(256, 512), pick, preferred_element_type=jnp.float32
        )
        for role in range(2):
            whole[role, k * 16 : k * 16 + 16] = picked[:, role * 256 : role * 256 + 256].reshape(16, 16, 256)
    for step, out in enumerate((own, one, two, three)):
        z = (where[4] * 2 + where[2] + step) % 4
        near = (z + 2 * where[3] + 3) % 4
        for j in range(4):
            out[j] = whole[z % 2, :, 4 * z + j, :].astype(jnp.bfloat16)
            out[4 + j] = whole[z % 2, :, 4 * near + j, :].astype(jnp.bfloat16)


def part_amplitudes(amps, where):
    return pl.pallas_call(
        part_kernel,
        out_shape=[jax.ShapeDtypeStruct((8, 64, 256), jnp.bfloat16)] * 4,
        in_specs=[pl.BlockSpec(memory_space=pltpu.VMEM), pl.BlockSpec(memory_space=pltpu.SMEM)],
        out_specs=[pl.BlockSpec(memory_space=pltpu.VMEM)] * 4,
        scratch_shapes=[pltpu.VMEM((2, 64, 16, 256), jnp.float32)],
        compiler_params=pltpu.CompilerParams(vmem_limit_bytes=10 * 1024 * 1024),
        cost_estimate=pl.CostEstimate(flops=1 << 20, bytes_accessed=1 << 10, transcendentals=0),
    )(amps, where)


def order_kernel(own, one, two, three, where, out):
    for step, piece in enumerate((own, one, two, three)):
        out[(where[4] * 2 + where[2] + 4 - step) % 4] = piece[...]


def order_pairs(*args):
    smem, vmem = (pl.BlockSpec(memory_space=space) for space in (pltpu.SMEM, pltpu.VMEM))
    return pl.pallas_call(
        order_kernel,
        out_shape=jax.ShapeDtypeStruct((4, 8, 64, 256), jnp.bfloat16),
        in_specs=[vmem] * 4 + [smem],
        out_specs=vmem,
        compiler_params=pltpu.CompilerParams(vmem_limit_bytes=6 * 1024 * 1024),
        cost_estimate=pl.CostEstimate(flops=1 << 20, bytes_accessed=1 << 10, transcendentals=0),
    )(*args)


def halve_kernel(one, three, one_half, three_half):
    one_half[...] = one[:128]
    three_half[...] = three[128:]


def halve(*args):
    vmem = pl.BlockSpec(memory_space=pltpu.VMEM)
    return pl.pallas_call(
        halve_kernel,
        out_shape=[jax.ShapeDtypeStruct((128, 3072), jnp.bfloat16)] * 2,
        in_specs=[vmem] * 2,
        out_specs=[vmem] * 2,
        compiler_params=pltpu.CompilerParams(vmem_limit_bytes=6 * 1024 * 1024),
        cost_estimate=pl.CostEstimate(flops=1 << 20, bytes_accessed=1 << 10, transcendentals=0),
    )(*args)


def gather_kernel(mine, from_core, from_z, from_both, where, out):
    core, zh = where[3], where[4]
    same = [jnp.where(core == k, mine[...], from_core[...]) for k in range(2)]
    across = [jnp.where(core == k, from_z[...], from_both[...]) for k in range(2)]
    parts = [jnp.where(zh == k, same[c], across[c]) for k in range(2) for c in range(2)]
    for a in range(4):
        out[a * 16 : a * 16 + 16] = jnp.concatenate([part[a * 4 : a * 4 + 4] for part in parts], axis=0)


def gather_rows(*args):
    smem, vmem = (pl.BlockSpec(memory_space=space) for space in (pltpu.SMEM, pltpu.VMEM))
    return pl.pallas_call(
        gather_kernel,
        out_shape=jax.ShapeDtypeStruct((64, 3072), jnp.bfloat16),
        in_specs=[vmem] * 4 + [smem],
        out_specs=vmem,
        compiler_params=pltpu.CompilerParams(vmem_limit_bytes=6 * 1024 * 1024),
        cost_estimate=pl.CostEstimate(flops=1 << 20, bytes_accessed=1 << 10, transcendentals=0),
    )(*args)


def join_kernel(*refs):
    for k in range(4):
        refs[4][k * 64 : k * 64 + 64] = refs[k][...]


def join(pieces):
    vmem = pl.BlockSpec(memory_space=pltpu.VMEM)
    return pl.pallas_call(
        join_kernel,
        out_shape=jax.ShapeDtypeStruct((256, 3072), jnp.bfloat16),
        in_specs=[vmem] * 4,
        out_specs=vmem,
        compiler_params=pltpu.CompilerParams(vmem_limit_bytes=6 * 1024 * 1024),
        cost_estimate=pl.CostEstimate(flops=1 << 20, bytes_accessed=1 << 10, transcendentals=0),
    )(*pieces)


def corner(where, step, shift):
    y, x, core = where[0], where[1], where[3]
    far, near = (0, 3, 1, 2)[step], (0, 3, 1, 2)[shift] if isinstance(shift, int) else shift
    return (
        (y + jnp.where(core == 0, far, near)) % 4,
        (x + jnp.where(core == 0, near, far)) % 4,
    )


def integral_kernel(steps, chunks, counts, *refs):
    groups = []
    for count in counts:
        groups.append(refs[:count])
        refs = refs[count:]
    blocks, bds, irreps = groups
    where, irrep_a, irrep_b, irrep_c, held, labels, fourth = refs
    if 3 in steps:
        fourth[:128], fourth[128:] = blocks[-2][...], blocks[-1][...]
        blocks = [*blocks[:-2], fourth]

    if any(len(chunk[4]) < 4 for chunk in chunks):
        held[...] = jnp.zeros_like(held)
    row = lax.broadcasted_iota(jnp.int32, (256, 1), 0)
    shift, inner = row // 64, row % 16
    shift = jnp.where(shift == 1, 3, jnp.where(shift == 0, 0, shift - 1))
    lane = lax.broadcasted_iota(jnp.int32, (256, 512), 1)
    label_a = jnp.zeros((256, 1), jnp.int32)
    for a in range(4):
        label_a = jnp.where(row // 16 % 4 == a, irrep_a[where[3] * 4 + a], label_a)
    for k, step in enumerate(steps):
        y, x = corner(where, step, shift)
        z = inner // 8 * 2 + where[2]
        place = y * 128 + x * 32 + inner // 4 % 2 * 16 + z * 4 + inner % 4
        found = jnp.sum(
            jnp.where(lane == place, irrep_c[...].astype(jnp.float32), 0.0), axis=1, keepdims=True
        )
        labels[k * 256 : k * 256 + 256] = found.astype(jnp.int32) ^ label_a

    for i, (bd, bd_at, irrep, irrep_at, used) in enumerate(chunks):
        right = bds[bd][bd_at : bd_at + 2].reshape(256, 3072)
        pair = jnp.concatenate([irrep_b[...] ^ irreps[irrep][irrep_at + d] for d in range(2)], axis=1)
        for step in used:
            k = steps.index(step)
            integral = lax.dot_general(
                blocks[k][...], right, (((1,), (1,)), ((), ())), preferred_element_type=jnp.float32
            )
            same = labels[k * 256 : k * 256 + 256] == pair
            kept = jnp.where(same, integral, 0.0).astype(jnp.bfloat16)
            for shift in range(4):
                y, x = corner(where, step, shift)
                to = pl.ds(pl.multiple_of(y * 64 + x * 16, 16), 16)
                for a in range(4):
                    for d in range(2):
                        held[2 * i + d, to, a * 128 : a * 128 + 128] = kept[
                            shift * 64 + a * 16 : shift * 64 + a * 16 + 16, d * 128 : d * 128 + 128
                        ]


def integrals(blocks, pairs, where, irrep_a, irrep_b, irrep_c):
    arrays = [[], []]
    chunks = []
    for *pair, used in pairs:
        chunk = []
        for kind, (array, at) in zip(arrays, pair):
            if not any(array is known for known in kind):
                kind.append(array)
            chunk += [[array is known for known in kind].index(True), at]
        chunks.append((*chunk, used))
    steps = sorted({step for chunk in chunks for step in chunk[4]})
    pieces = [piece for s in steps for piece in blocks[s]]
    counts = (len(pieces), *[len(kind) for kind in arrays])
    smem, vmem = (pl.BlockSpec(memory_space=space) for space in (pltpu.SMEM, pltpu.VMEM))
    return pl.pallas_call(
        functools.partial(integral_kernel, tuple(steps), tuple(chunks), counts),
        out_shape=jax.ShapeDtypeStruct((2 * len(pairs), 256, 512), jnp.bfloat16),
        in_specs=[vmem] * sum(counts[:2]) + [smem] * (counts[2] + 2) + [vmem] * 2,
        out_specs=vmem,
        scratch_shapes=[
            pltpu.VMEM((256 * len(steps), 1), jnp.int32),
            pltpu.VMEM((256 if 3 in steps else 16, 3072), jnp.bfloat16),
        ],
        compiler_params=pltpu.CompilerParams(vmem_limit_bytes=12 * 1024 * 1024),
        cost_estimate=pl.CostEstimate(flops=1 << 20, bytes_accessed=1 << 10, transcendentals=0),
    )(*pieces, *arrays[0], *arrays[1], where, irrep_a, irrep_b, irrep_c)


def ladder_kernel(amps, amps_other, one, two, out):
    order = [(amps, d) for d in range(4)] + [(amps_other, d) for d in range(4)]
    order += [(t, 4 + d) for d0 in (0, 2) for t in (amps, amps_other) for d in (d0, d0 + 1)]
    left = jnp.concatenate([t[:, d].reshape(256, 256) for t, d in order], axis=1)
    n = one.shape[0] * 256
    total = jnp.dot(left[:, :n], one[...].reshape(n, 512), preferred_element_type=jnp.float32)
    total += jnp.dot(left, two[...].reshape(4096, 512), preferred_element_type=jnp.float32)
    out[...] = total.astype(out.dtype)


def ladder(*args):
    vmem = pl.BlockSpec(memory_space=pltpu.VMEM)
    return pl.pallas_call(
        ladder_kernel,
        out_shape=jax.ShapeDtypeStruct((256, 512), jnp.bfloat16),
        in_specs=[vmem] * 4,
        out_specs=vmem,
        compiler_params=pltpu.CompilerParams(vmem_limit_bytes=12 * 1024 * 1024),
        cost_estimate=pl.CostEstimate(flops=1 << 20, bytes_accessed=1 << 10, transcendentals=0),
    )(*args)


def body(amplitudes, ac_factor, bd_factor, irrep_a, irrep_b, irrep_c, irrep_d):
    where = jnp.stack([lax.axis_index(name) for name in ("y", "x", "zl", "core", "zh")]).astype(jnp.int32)
    core = lax.axis_index("core")

    by_core = ac_factor.reshape(2, 16, 3072)
    mine = lax.dynamic_index_in_dim(by_core, core, 0, keepdims=False)
    theirs = lax.dynamic_index_in_dim(by_core, 1 - core, 0, keepdims=False)
    from_core = swap(theirs)
    from_z = lax.ppermute(mine, "zh", [(0, 1), (1, 0)])
    from_both = lax.ppermute(theirs, ("zh", "core"), [(0, 3), (1, 2), (2, 1), (3, 0)])

    near = around(irrep_d)
    bd_core = swap(bd_factor)
    mine, from_core, from_z, from_both, near_irreps, bd_core, bd_first, bd_last = lax.optimization_barrier(
        (mine, from_core, from_z, from_both, jnp.concatenate([irrep_d, near]), bd_core, bd_factor[:2], bd_factor[2:])
    )

    rows = gather_rows(mine, from_core, from_z, from_both, where)
    lines = along(rows, "xy")
    near_first, near_last = around(bd_first), around(bd_last)
    other_far = swap(near_irreps)
    rows = join([rows] + lines)
    rows, amplitudes = lax.optimization_barrier((rows, amplitudes))
    one, three = along(rows, "yx", (1, 3))

    parted = part_amplitudes(amplitudes, where)
    one, three, near_first, *parted = lax.optimization_barrier((one, three, near_first, *parted))
    parted = [
        lax.ppermute(part, Z, [(z, (z + step) % 4) for z in range(4)]) if step else part
        for step, part in enumerate(parted)
    ]

    far_first = swap(near_first)
    one_half, three_half = halve(one, three)
    (two_first,) = along(one_half, "yx", (1,))
    (two_last,) = along(three_half, "yx", (3,))

    rest = (where, irrep_a, irrep_b.reshape(1, 128), irrep_c.reshape(1, 512))
    blocks = [[rows], [one], [three], [two_first, two_last]]
    first = [((bd_factor, at), (near_irreps, at)) for at in (0, 2)]
    first += [((bd_core, at), (other_far, at)) for at in (0, 2)]
    first += [((near_first, 0), (near_irreps, 4))]
    held_first = integrals(blocks, [(*pair, (0, 1, 2)) for pair in first], *rest)
    near_last, held_first, two_first, two_last, far_first = lax.optimization_barrier(
        (near_last, held_first, two_first, two_last, far_first)
    )
    blocks[3] = [two_first, two_last]
    far_last = swap(near_last)
    last = [((far_first, 0), (other_far, 4)), ((near_last, 0), (near_irreps, 6)), ((far_last, 0), (other_far, 6))]
    held_last = integrals(
        blocks, [(*pair, (3,)) for pair in first] + [(*pair, (0, 1, 2, 3)) for pair in last], *rest
    )
    held_last, *parted = lax.optimization_barrier((held_last, *parted))
    amps = order_pairs(*parted, where)
    amps_other = swap(amps)
    total = ladder(amps, amps_other, held_first, held_last)

    pieces = total.reshape(128, 2, 512)
    pieces = lax.all_to_all(pieces, ALL, split_axis=0, concat_axis=0, tiled=True)
    summed = jnp.sum(pieces.reshape(64, 2, 2, 512).astype(jnp.float32), axis=0)
    return summed.reshape(2, 2, 4, 128).transpose(1, 0, 2, 3).reshape(2, 8, 128).astype(jnp.bfloat16)


def solution(mesh):
    fine = Mesh(mesh.devices.reshape(2, 2, 4, 4, 2), ALL)
    virt = ("y", "x", "core")
    return jax.shard_map(
        body,
        mesh=fine,
        in_specs=(
            P(Z, virt, None),
            P(None, virt + Z, None),
            P(virt + Z, None, None),
            P(),
            P(),
            P(),
            P(virt + Z),
        ),
        out_specs=P(ALL, None, None),
        check_vma=False,
    )
```

time: 164 us -> 109 us (0.66)
  waiting for transfers between devices: 90.4 us -> 28.9 us
  starting transfers between devices: 5.89 us -> 31.1 us
  Pallas kernels: 0 us -> 24 us
  matrix products: 22 us -> 0 us
  between operations: 13.4 us -> 0.15 us
  local copies, waits for them, and re-layouts: 9.21 us -> 4.6 us
    all_gather x1 -> x0, waiting for transfers between devices: 75.6 us -> none  [body(): left = lax.all_gather(ac_factor, ('virt', 'occ'), axis=1, tiled=True)]
    ppermute x0 -> x21, starting transfers between devices: none -> 31.1 us  [the longest x7 9.75 us: moved(): return lax.ppermute(block, ('y', 'x', 'core'), pairs)]
    ppermute x0 -> x21, waiting for transfers between devices: none -> 28.9 us  [the longest x7 19.7 us: moved(): return lax.ppermute(block, ('y', 'x', 'core'), pairs)]
    pallas_call x0 -> x8, Pallas kernels: none -> 24 us  [the longest x2 16.6 us: integrals(): pl.pallas_call(functools.partial(integral_kernel, tuple(steps), tuple(chu...]
    dot_general x2 -> x0, matrix products: 22 us -> none  [the longest x1 16.7 us: body(): lax.dot_general(left, bd_factor, (((2,), (2,)), ((), ())), preferred_elem...]
    all_to_all x1 -> x0, waiting for transfers between devices: 14.8 us -> none  [body(): lax.all_to_all(amplitudes, 'occ', split_axis=1, concat_axis=0, tiled=True)]
    all_to_all x1 -> x0, starting transfers between devices: 5.86 us -> none  [body(): lax.all_to_all(amplitudes, 'occ', split_axis=1, concat_axis=0, tiled=True)]
    unnamed x14 -> x12, local copies, waits for them, and re-layouts: 4.7 us -> 0.02 us
  transfers between devices with their start and end apart: 2 -> 21, of which waited for: 2 -> 10; matrix products, arithmetic and copies ran while one was open for 3% -> 4% of each run, Pallas kernels for 0% -> 19%
where the time goes in v3:
time: 109 us
  starting transfers between devices  31.1 us (29%)
  waiting for transfers between devices  28.9 us (27%)
  Pallas kernels  24 us (22%)
  blocking collectives  19.9 us (18%)
  local copies, waits for them, and re-layouts  4.6 us (4%)
    all_to_all x1, blocking collectives, body(): lax.all_to_all(pieces, ALL, split_axis=0, concat_axis=0, tiled=True)  19.9 us
    ppermute x7, waiting for transfers between devices, moved(): return lax.ppermute(block, ('y', 'x', 'core'), pairs)  19.7 us
    pallas_call x2, Pallas kernels, integrals(): pl.pallas_call(functools.partial(integral_kernel, tuple(steps), tuple(chu...  16.6 us
    ppermute x7, starting transfers between devices, moved(): return lax.ppermute(block, ('y', 'x', 'core'), pairs)  9.75 us
    ppermute x6, starting transfers between devices, swap(): return lax.ppermute(block, 'core', [(0, 1), (1, 0)])  8.33 us
    pallas_call x1, Pallas kernels, part_amplitudes(): pl.pallas_call(part_kernel, out_shape=[jax.ShapeDtypeStruct((8, 64, 256),...  3.97 us
    ppermute x3, starting transfers between devices, body(): lax.ppermute(part, Z, [(z, (z + step) % 4) for z in range(4)])  3.84 us
    ppermute x1, starting transfers between devices, body(): lax.ppermute(theirs, ('zh', 'core'), [(0, 3), (1, 2), (2, 1), (3, 0)])  3.57 us
  transfers between devices with their start and end apart: 21, of which 10 were waited for; matrix products, arithmetic and copies ran while one was open for 4% of the time, Pallas kernels for 19%

profile of v3, /device:TPU:1, one launch (start us, length us, event | category | flops | bytes accessed | tf_op | source)
XLA Modules:
  0.0 109.0 jit_solution(7071380440387818663)
XLA Ops:
  0.0 1.4 %collective-permute-start.4 = (bf16[4,128,3072]{2,1,0:T(8,128)(2,1)}, bf16[4,128,3072]{2,1,0:T(8,128)(2,1)S(1)}, u32[]{:S(2)}, u32[]{:S(2)}) collective-permute-start(bf16[4,128,3072]{2,1,0:T(8,128)(2,1)} %refs_5_.1), channel_id=1, source_target_pairs={{0,1},{1,0},{2,3},{3,2},{4,5},{5,4},{6,7},{7,6},{8,9},{9,8},{10,11... | collective-permute-start | bytes 9437192 | tf_op jit(solution)/shard_map/ppermute | solution.py:15
  1.4 1.0 reshape.19
  2.4 0.7 dynamic-slice_bitcast_fusion
  3.1 3.6 %collective-permute-start.2 = (bf16[16,3072]{1,0:T(8,128)(2,1)}, bf16[16,3072]{1,0:T(8,128)(2,1)S(1)}, u32[]{:S(2)}, u32[]{:S(2)}) collective-permute-start(bf16[16,3072]{1,0:T(8,128)(2,1)} %get-tuple-element.73), channel_id=1, source_target_pairs={{0,65},{1,64},{64,1},{65,0},{2,67},{3,66},{66,3},{67,2},{4,69},{5,... | collective-permute-start | bytes 294920 | tf_op jit(solution)/shard_map/ppermute | solution.py:259
  6.6 0.5 collective-permute-start
  7.1 0.4 collective-permute-start.3
  7.6 2.1 %collective-permute-start.1 = (bf16[16,3072]{1,0:T(8,128)(2,1)S(1)}, bf16[16,3072]{1,0:T(8,128)(2,1)S(1)}, u32[]{:S(2)}, u32[]{:S(2)}) collective-permute-start(bf16[16,3072]{1,0:T(8,128)(2,1)S(1)} %get-tuple-element.38.mine), channel_id=1, source_target_pairs={{0,64},{64,0},{1,65},{65,1},{2,66},{66,2},{3,67},{67,3},{4,68},{68... | collective-permute-start | bytes 294920 | tf_op jit(solution)/shard_map/ppermute | solution.py:258
  9.7 0.1 stack.23.where.refs_8_.refs_13_
  9.8 2.1 %fusion = (bf16[2,128,3072]{2,1,0:T(8,128)(2,1)S(1)}, bf16[2,128,3072]{2,1,0:T(8,128)(2,1)S(1)}) fusion(bf16[4,128,3072]{2,1,0:T(8,128)(2,1)} %refs_5_.1), kind=kLoop, calls=%fused_computation.3 | loop fusion | bytes 6291456 | tf_op jit(solution)/shard_map/slice | solution.py:264
  11.9 0.0 collective-permute-done.3
  11.9 0.0 copy-done.5
  11.9 0.1 pad_add_fusion.refs_6_.refs_11_
  12.0 0.0 collective-permute-done.2.from_both
  12.0 0.0 collective-permute-done.from_core
  12.0 0.6 collective-permute-done.1.from_z
  12.6 0.0 collective-permute-done.4.refs_4_.refs_6_
  12.6 0.7 shard_map.73.refs_0_
  13.2 0.0 copy-start.1
  13.3 3.0 %collective-permute-start.7 = (bf16[64,3072]{1,0:T(8,128)(2,1)S(1)}, bf16[64,3072]{1,0:T(8,128)(2,1)S(1)}, u32[]{:S(2)}, u32[]{:S(2)}) collective-permute-start(bf16[64,3072]{1,0:T(8,128)(2,1)S(1)} %shard_map.73.refs_0_), channel_id=1, source_target_pairs={{0,4},{1,17},{2,6},{3,19},{4,0},{5,21},{6,2},{7,23},{8,12},{9,25},... | collective-permute-start | bytes 1179656 | tf_op jit(solution)/shard_map/ppermute | solution.py:33
  16.3 0.8 collective-permute-start.6
  17.0 0.7 collective-permute-start.5
  17.7 1.5 %collective-permute-start.10 = (bf16[2,128,3072]{2,1,0:T(8,128)(2,1)S(1)}, bf16[2,128,3072]{2,1,0:T(8,128)(2,1)S(1)}, u32[]{:S(2)}, u32[]{:S(2)}) collective-permute-start(bf16[2,128,3072]{2,1,0:T(8,128)(2,1)S(1)} %get-tuple-element.43), channel_id=1, source_target_pairs={{0,32},{1,97},{32,64},{33,1},{64,96},{65,33},{96,0},{97,65},{2,34}... | collective-permute-start | bytes 4718600 | tf_op jit(solution)/shard_map/ppermute | solution.py:22
  19.3 2.5 %collective-permute-done.7.refs_3_ = bf16[64,3072]{1,0:T(8,128)(2,1)S(1)} collective-permute-done((bf16[64,3072]{1,0:T(8,128)(2,1)S(1)}, bf16[64,3072]{1,0:T(8,128)(2,1)S(1)}, u32[]{:S(2)}, u32[]{:S(2)}) %collective-permute-start.7) | collective-permute-done | bytes 393248 | tf_op jit(solution)/shard_map/ppermute | solution.py:33
  21.8 4.6 %collective-permute-done.6.refs_2_ = bf16[64,3072]{1,0:T(8,128)(2,1)S(1)} collective-permute-done((bf16[64,3072]{1,0:T(8,128)(2,1)S(1)}, bf16[64,3072]{1,0:T(8,128)(2,1)S(1)}, u32[]{:S(2)}, u32[]{:S(2)}) %collective-permute-start.6) | collective-permute-done | bytes 393248 | tf_op jit(solution)/shard_map/ppermute | solution.py:33
  26.4 0.0 collective-permute-done.5.refs_1_
  26.4 0.1 shard_map.74.refs_0_
  26.5 2.5 %collective-permute-start.9 = (bf16[256,3072]{1,0:T(8,128)(2,1)S(1)}, bf16[256,3072]{1,0:T(8,128)(2,1)S(1)}, u32[]{:S(2)}, u32[]{:S(2)}) collective-permute-start(bf16[256,3072]{1,0:T(8,128)(2,1)S(1)} %shard_map.74.refs_0_), channel_id=1, source_target_pairs={{0,24},{1,7},{2,26},{3,1},{4,28},{5,3},{6,30},{7,5},{8,0},{9,15},{... | collective-permute-start | bytes 4718600 | tf_op jit(solution)/shard_map/ppermute | solution.py:33
  29.0 0.0 collective-permute-start.8
  29.0 1.5 %collective-permute-start.11 = (bf16[2,128,3072]{2,1,0:T(8,128)(2,1)S(1)}, bf16[2,128,3072]{2,1,0:T(8,128)(2,1)S(1)}, u32[]{:S(2)}, u32[]{:S(2)}) collective-permute-start(bf16[2,128,3072]{2,1,0:T(8,128)(2,1)S(1)} %get-tuple-element.51), channel_id=1, source_target_pairs={{0,32},{1,97},{32,64},{33,1},{64,96},{65,33},{96,0},{97,65},{2,34}... | collective-permute-start | bytes 4718600 | tf_op jit(solution)/shard_map/ppermute | solution.py:22
  30.6 0.0 copy-done.1
  30.6 4.0 %shard_map.75 = (bf16[8,64,256]{2,1,0:T(8,128)(2,1)S(1)}, bf16[8,64,256]{2,1,0:T(8,128)(2,1)S(1)}, bf16[8,64,256]{2,1,0:T(8,128)(2,1)S(1)}, bf16[8,64,256]{2,1,0:T(8,128)(2,1)S(1)}) custom-call(bf16[64,16,512]{2,1,0:T(8,128)(2,1)S(1)} %copy-done.1, s32[5]{0:T(128)S(1)} %stack.23.where.refs_8_.refs_13_), custom_call_target="tpu_custom_call" | custom-call | flops 1048576 | bytes 1024 | tf_op jit(solution)/shard_map/pallas_call | solution.py:59
  34.5 3.1 %collective-permute-done.10.refs_5_.refs_7_ = bf16[2,128,3072]{2,1,0:T(8,128)(2,1)S(1)} collective-permute-done((bf16[2,128,3072]{2,1,0:T(8,128)(2,1)S(1)}, bf16[2,128,3072]{2,1,0:T(8,128)(2,1)S(1)}, u32[]{:S(2)}, u32[]{:S(2)}) %collective-permute-start.10) | collective-permute-done | bytes 1572896 | tf_op jit(solution)/shard_map/ppermute | solution.py:22
  37.7 8.7 %collective-permute-done.9.refs_2_.three = bf16[256,3072]{1,0:T(8,128)(2,1)S(1)} collective-permute-done((bf16[256,3072]{1,0:T(8,128)(2,1)S(1)}, bf16[256,3072]{1,0:T(8,128)(2,1)S(1)}, u32[]{:S(2)}, u32[]{:S(2)}) %collective-permute-start.9) | collective-permute-done | bytes 1572896 | tf_op jit(solution)/shard_map/ppermute | solution.py:33
  46.4 3.4 %collective-permute-done.8.refs_1_.one = bf16[256,3072]{1,0:T(8,128)(2,1)S(1)} collective-permute-done((bf16[256,3072]{1,0:T(8,128)(2,1)S(1)}, bf16[256,3072]{1,0:T(8,128)(2,1)S(1)}, u32[]{:S(2)}, u32[]{:S(2)}) %collective-permute-start.8) | collective-permute-done | bytes 1572896 | tf_op jit(solution)/shard_map/ppermute | solution.py:33
  49.8 3.8 %collective-permute-start.15 = (bf16[2,128,3072]{2,1,0:T(8,128)(2,1)S(1)}, bf16[2,128,3072]{2,1,0:T(8,128)(2,1)S(1)}, u32[]{:S(2)}, u32[]{:S(2)}) collective-permute-start(bf16[2,128,3072]{2,1,0:T(8,128)(2,1)S(1)} %collective-permute-done.10.refs_5_.refs_7_), channel_id=1, source_target_pairs={{0,1},{1,0},{2,3},{3,2},{4,5},{5,4},{6,7},{7,6},{8,9},{9,8},{10,11... | collective-permute-start | bytes 4718600 | tf_op jit(solution)/shard_map/ppermute | solution.py:15
  53.6 0.1 shard_map.77
  53.7 1.2 %collective-permute-start.13 = (bf16[128,3072]{1,0:T(8,128)(2,1)S(1)}, bf16[128,3072]{1,0:T(8,128)(2,1)S(1)}, u32[]{:S(2)}, u32[]{:S(2)}) collective-permute-start(bf16[128,3072]{1,0:T(8,128)(2,1)S(1)} %get-tuple-element.55), channel_id=1, source_target_pairs={{0,8},{1,3},{2,10},{3,5},{4,12},{5,7},{6,14},{7,1},{8,16},{9,11},{... | collective-permute-start | bytes 2359304 | tf_op jit(solution)/shard_map/ppermute | solution.py:33
  54.9 1.5 %collective-permute-start.14 = (bf16[128,3072]{1,0:T(8,128)(2,1)S(1)}, bf16[128,3072]{1,0:T(8,128)(2,1)S(1)}, u32[]{:S(2)}, u32[]{:S(2)}) collective-permute-start(bf16[128,3072]{1,0:T(8,128)(2,1)S(1)} %get-tuple-element.56), channel_id=1, source_target_pairs={{0,24},{1,7},{2,26},{3,1},{4,28},{5,3},{6,30},{7,5},{8,0},{9,15},{... | collective-permute-start | bytes 2359304 | tf_op jit(solution)/shard_map/ppermute | solution.py:33
  56.5 0.6 collective-permute-start.12
  57.0 0.8 collective-permute-done.12.refs_7_.refs_12_
  57.9 0.0 copy-done
  57.9 0.0 copy-done.3
  57.9 7.8 %shard_map.76.one = bf16[10,256,512]{2,1,0:T(8,128)(2,1)S(1)} custom-call(bf16[256,3072]{1,0:T(8,128)(2,1)S(1)} %shard_map.74.refs_0_, bf16[256,3072]{1,0:T(8,128)(2,1)S(1)} %collective-permute-done.8.refs_1_.one, bf16[256,3072]{1,0:T(8,128)(2,1)S(1)} %collective-permute-done.9.refs_2_.three, bf16[4,128,3072]{2,1,0:T(8,128)(2,1)S(1)} %copy-done, ...), custom_call_target="tpu_custom_call" | custom-call | flops 1048576 | bytes 1024 | tf_op jit(solution)/shard_map/pallas_call | solution.py:214
  65.7 0.0 collective-permute-done.11.refs_9_
  65.7 0.4 collective-permute-done.13.refs_3_
  66.1 0.0 collective-permute-done.14.refs_4_
  66.1 0.0 collective-permute-done.15.refs_8_
  66.1 0.9 collective-permute-start.16
  67.0 0.5 collective-permute-start.17
  67.5 2.6 %collective-permute-start.18 = (bf16[8,64,256]{2,1,0:T(8,128)(2,1)S(1)}, bf16[8,64,256]{2,1,0:T(8,128)(2,1)S(1)}, u32[]{:S(2)}, u32[]{:S(2)}) collective-permute-start(bf16[8,64,256]{2,1,0:T(8,128)(2,1)S(1)} %get-tuple-element.63), channel_id=1, source_target_pairs={{0,64},{32,96},{64,0},{96,32},{1,65},{33,97},{65,1},{97,33},{2,66}... | collective-permute-start | bytes 786440 | tf_op jit(solution)/shard_map/ppermute | solution.py:278
  70.1 0.7 collective-permute-start.19
  70.9 0.0 collective-permute-done.16.refs_10_
  70.9 8.8 %shard_map.78.two = bf16[16,256,512]{2,1,0:T(8,128)(2,1)S(1)} custom-call(bf16[256,3072]{1,0:T(8,128)(2,1)S(1)} %shard_map.74.refs_0_, bf16[256,3072]{1,0:T(8,128)(2,1)S(1)} %collective-permute-done.8.refs_1_.one, bf16[256,3072]{1,0:T(8,128)(2,1)S(1)} %collective-permute-done.9.refs_2_.three, bf16[128,3072]{1,0:T(8,128)(2,1)S(1)} %collective-permute-done.13.refs_3_, ...), custom_call_target="tpu_custom_call" | custom-call | flops 1048576 | bytes 1024 | tf_op jit(solution)/shard_map/pallas_call | solution.py:214
  79.7 0.0 collective-permute-done.17.one
  79.7 2.5 %collective-permute-done.18.two = bf16[8,64,256]{2,1,0:T(8,128)(2,1)S(1)} collective-permute-done((bf16[8,64,256]{2,1,0:T(8,128)(2,1)S(1)}, bf16[8,64,256]{2,1,0:T(8,128)(2,1)S(1)}, u32[]{:S(2)}, u32[]{:S(2)}) %collective-permute-start.18) | collective-permute-done | bytes 262176 | tf_op jit(solution)/shard_map/ppermute | solution.py:278
  82.1 0.0 collective-permute-done.19.three
  82.1 0.6 shard_map.79.amps
  82.8 1.1 %collective-permute-start.20 = (bf16[4,8,64,256]{3,2,1,0:T(8,128)(2,1)S(1)}, bf16[4,8,64,256]{3,2,1,0:T(8,128)(2,1)S(1)}, u32[]{:S(2)}, u32[]{:S(2)}) collective-permute-start(bf16[4,8,64,256]{3,2,1,0:T(8,128)(2,1)S(1)} %shard_map.79.amps), channel_id=1, source_target_pairs={{0,1},{1,0},{2,3},{3,2},{4,5},{5,4},{6,7},{7,6},{8,9},{9,8},{10,11... | collective-permute-start | bytes 3145736 | tf_op jit(solution)/shard_map/ppermute | solution.py:15
  83.9 2.3 %collective-permute-done.20.amps_other = bf16[4,8,64,256]{3,2,1,0:T(8,128)(2,1)S(1)} collective-permute-done((bf16[4,8,64,256]{3,2,1,0:T(8,128)(2,1)S(1)}, bf16[4,8,64,256]{3,2,1,0:T(8,128)(2,1)S(1)}, u32[]{:S(2)}, u32[]{:S(2)}) %collective-permute-start.20) | collective-permute-done | bytes 1048608 | tf_op jit(solution)/shard_map/ppermute | solution.py:15
  86.2 1.9 %shard_map.80 = bf16[256,512]{1,0:T(8,128)(2,1)S(1)} custom-call(bf16[4,8,64,256]{3,2,1,0:T(8,128)(2,1)S(1)} %shard_map.79.amps, bf16[4,8,64,256]{3,2,1,0:T(8,128)(2,1)S(1)} %collective-permute-done.20.amps_other, bf16[10,256,512]{2,1,0:T(8,128)(2,1)S(1)} %shard_map.76.one, bf16[16,256,512]{2,1,0:T(8,128)(2,1)S(1)} %shard_map.78.two), custom_call_target="tpu_custom_call" | custom-call | flops 1048576 | bytes 1024 | tf_op jit(solution)/shard_map/pallas_call | solution.py:240
  88.1 0.1 reshape.22
  88.2 19.9 %all_to_all.5 = bf16[128,2,512]{2,1,0:T(2,128)(2,1)S(1)} all-to-all(bf16[128,2,512]{2,1,0:T(2,128)(2,1)S(1)} %reshape.22), channel_id=1, replica_groups=mesh['zh'=2,'zl'=2,'y'=4,'x'=4,'core'=2] {'zh','zl','y','x','core'}, dimensions={0} | all-to-all | bytes 524288 | tf_op jit(solution)/shard_map/all_to_all | solution.py:308
  108.1 0.2 reduce
  108.4 0.6 copy.8
  (8 shorter events, 0.0 us)
Async XLA Ops:
  0.0 12.6 %collective-permute-start.4 = (bf16[4,128,3072]{2,1,0:T(8,128)(2,1)}, bf16[4,128,3072]{2,1,0:T(8,128)(2,1)S(1)}, u32[]{:S(2)}, u32[]{:S(2)}) collective-permute-start(bf16[4,128,3072]{2,1,0:T(8,128)(2,1)} %refs_5_.1), channel_id=1, source_target_pairs={{0,1},{1,0},{2,3},{3,2},{4,5},{5,4},{6,7},{7,6},{8,9},{9,8},{10,11... | collective-permute-start | bytes 9437192 | tf_op jit(solution)/shard_map/ppermute | solution.py:15
  3.1 8.9 %collective-permute-start.2 = (bf16[16,3072]{1,0:T(8,128)(2,1)}, bf16[16,3072]{1,0:T(8,128)(2,1)S(1)}, u32[]{:S(2)}, u32[]{:S(2)}) collective-permute-start(bf16[16,3072]{1,0:T(8,128)(2,1)} %get-tuple-element.73), channel_id=1, source_target_pairs={{0,65},{1,64},{64,1},{65,0},{2,67},{3,66},{66,3},{67,2},{4,69},{5,... | collective-permute-start | bytes 294920 | tf_op jit(solution)/shard_map/ppermute | solution.py:259
  6.6 5.4 %collective-permute-start = (bf16[16,3072]{1,0:T(8,128)(2,1)}, bf16[16,3072]{1,0:T(8,128)(2,1)S(1)}, u32[]{:S(2)}, u32[]{:S(2)}) collective-permute-start(bf16[16,3072]{1,0:T(8,128)(2,1)} %get-tuple-element.73), channel_id=1, source_target_pairs={{0,1},{1,0},{2,3},{3,2},{4,5},{5,4},{6,7},{7,6},{8,9},{9,8},{10,11... | collective-permute-start | bytes 294920 | tf_op jit(solution)/shard_map/ppermute | solution.py:15
  7.1 4.8 %collective-permute-start.3 = (s32[4]{0:T(128)}, s32[4]{0:T(128)S(1)}, u32[]{:S(2)}, u32[]{:S(2)}) collective-permute-start(s32[4]{0:T(128)} %param.13), channel_id=1, source_target_pairs={{0,32},{1,97},{32,64},{33,1},{64,96},{65,33},{96,0},{97,65},{2,34}... | collective-permute-start | bytes 56 | tf_op jit(solution)/shard_map/ppermute | solution.py:22
  7.6 5.0 %collective-permute-start.1 = (bf16[16,3072]{1,0:T(8,128)(2,1)S(1)}, bf16[16,3072]{1,0:T(8,128)(2,1)S(1)}, u32[]{:S(2)}, u32[]{:S(2)}) collective-permute-start(bf16[16,3072]{1,0:T(8,128)(2,1)S(1)} %get-tuple-element.38.mine), channel_id=1, source_target_pairs={{0,64},{64,0},{1,65},{65,1},{2,66},{66,2},{3,67},{67,3},{4,68},{68... | collective-permute-start | bytes 294920 | tf_op jit(solution)/shard_map/ppermute | solution.py:258
  9.8 2.2 %copy-start.5 = (s32[4]{0:T(128)S(1)}, s32[4]{0:T(128)}, u32[]{:S(2)}) copy-start(s32[4]{0:T(128)} %param.13) | copy-start | bytes 52
  13.2 17.3 %copy-start.1 = (bf16[64,16,512]{2,1,0:T(8,128)(2,1)S(1)}, bf16[64,16,512]{2,1,0:T(8,128)(2,1)}, u32[]{:S(2)}) copy-start(bf16[64,16,512]{2,1,0:T(8,128)(2,1)} %amps) | copy-start | bytes 3145732
  13.3 8.5 %collective-permute-start.7 = (bf16[64,3072]{1,0:T(8,128)(2,1)S(1)}, bf16[64,3072]{1,0:T(8,128)(2,1)S(1)}, u32[]{:S(2)}, u32[]{:S(2)}) collective-permute-start(bf16[64,3072]{1,0:T(8,128)(2,1)S(1)} %shard_map.73.refs_0_), channel_id=1, source_target_pairs={{0,4},{1,17},{2,6},{3,19},{4,0},{5,21},{6,2},{7,23},{8,12},{9,25},... | collective-permute-start | bytes 1179656 | tf_op jit(solution)/shard_map/ppermute | solution.py:33
  16.3 10.1 %collective-permute-start.6 = (bf16[64,3072]{1,0:T(8,128)(2,1)S(1)}, bf16[64,3072]{1,0:T(8,128)(2,1)S(1)}, u32[]{:S(2)}, u32[]{:S(2)}) collective-permute-start(bf16[64,3072]{1,0:T(8,128)(2,1)S(1)} %shard_map.73.refs_0_), channel_id=1, source_target_pairs={{0,6},{1,25},{2,0},{3,27},{4,2},{5,29},{6,4},{7,31},{8,14},{9,1},{... | collective-permute-start | bytes 1179656 | tf_op jit(solution)/shard_map/ppermute | solution.py:33
  17.0 9.3 %collective-permute-start.5 = (bf16[64,3072]{1,0:T(8,128)(2,1)S(1)}, bf16[64,3072]{1,0:T(8,128)(2,1)S(1)}, u32[]{:S(2)}, u32[]{:S(2)}) collective-permute-start(bf16[64,3072]{1,0:T(8,128)(2,1)S(1)} %shard_map.73.refs_0_), channel_id=1, source_target_pairs={{0,2},{1,9},{2,4},{3,11},{4,6},{5,13},{6,0},{7,15},{8,10},{9,17},{... | collective-permute-start | bytes 1179656 | tf_op jit(solution)/shard_map/ppermute | solution.py:33
  17.7 20.0 %collective-permute-start.10 = (bf16[2,128,3072]{2,1,0:T(8,128)(2,1)S(1)}, bf16[2,128,3072]{2,1,0:T(8,128)(2,1)S(1)}, u32[]{:S(2)}, u32[]{:S(2)}) collective-permute-start(bf16[2,128,3072]{2,1,0:T(8,128)(2,1)S(1)} %get-tuple-element.43), channel_id=1, source_target_pairs={{0,32},{1,97},{32,64},{33,1},{64,96},{65,33},{96,0},{97,65},{2,34}... | collective-permute-start | bytes 4718600 | tf_op jit(solution)/shard_map/ppermute | solution.py:22
  26.5 19.9 %collective-permute-start.9 = (bf16[256,3072]{1,0:T(8,128)(2,1)S(1)}, bf16[256,3072]{1,0:T(8,128)(2,1)S(1)}, u32[]{:S(2)}, u32[]{:S(2)}) collective-permute-start(bf16[256,3072]{1,0:T(8,128)(2,1)S(1)} %shard_map.74.refs_0_), channel_id=1, source_target_pairs={{0,24},{1,7},{2,26},{3,1},{4,28},{5,3},{6,30},{7,5},{8,0},{9,15},{... | collective-permute-start | bytes 4718600 | tf_op jit(solution)/shard_map/ppermute | solution.py:33
  29.0 20.8 %collective-permute-start.8 = (bf16[256,3072]{1,0:T(8,128)(2,1)S(1)}, bf16[256,3072]{1,0:T(8,128)(2,1)S(1)}, u32[]{:S(2)}, u32[]{:S(2)}) collective-permute-start(bf16[256,3072]{1,0:T(8,128)(2,1)S(1)} %shard_map.74.refs_0_), channel_id=1, source_target_pairs={{0,8},{1,3},{2,10},{3,5},{4,12},{5,7},{6,14},{7,1},{8,16},{9,11},{... | collective-permute-start | bytes 4718600 | tf_op jit(solution)/shard_map/ppermute | solution.py:33
  29.0 36.7 %collective-permute-start.11 = (bf16[2,128,3072]{2,1,0:T(8,128)(2,1)S(1)}, bf16[2,128,3072]{2,1,0:T(8,128)(2,1)S(1)}, u32[]{:S(2)}, u32[]{:S(2)}) collective-permute-start(bf16[2,128,3072]{2,1,0:T(8,128)(2,1)S(1)} %get-tuple-element.51), channel_id=1, source_target_pairs={{0,32},{1,97},{32,64},{33,1},{64,96},{65,33},{96,0},{97,65},{2,34}... | collective-permute-start | bytes 4718600 | tf_op jit(solution)/shard_map/ppermute | solution.py:22
  49.8 8.1 %copy-start = (bf16[4,128,3072]{2,1,0:T(8,128)(2,1)S(1)}, bf16[4,128,3072]{2,1,0:T(8,128)(2,1)}, u32[]{:S(2)}) copy-start(bf16[4,128,3072]{2,1,0:T(8,128)(2,1)} %refs_5_.1) | copy-start | bytes 9437188
  49.8 8.1 %copy-start.2 = (s32[512]{0:T(512)S(1)}, s32[512]{0:T(512)}, u32[]{:S(2)}) copy-start(s32[512]{0:T(512)} %param.12) | copy-start | bytes 6148
  49.8 8.1 %copy-start.3 = (s32[8]{0:T(128)S(1)}, s32[8]{0:T(128)}, u32[]{:S(2)}) copy-start(s32[8]{0:T(128)} %refs_14_.1) | copy-start | bytes 100
  49.8 8.1 %copy-start.4 = (s32[128]{0:T(128)S(1)}, s32[128]{0:T(128)}, u32[]{:S(2)}) copy-start(s32[128]{0:T(128)} %param.11) | copy-start | bytes 1540
  49.8 16.3 %collective-permute-start.15 = (bf16[2,128,3072]{2,1,0:T(8,128)(2,1)S(1)}, bf16[2,128,3072]{2,1,0:T(8,128)(2,1)S(1)}, u32[]{:S(2)}, u32[]{:S(2)}) collective-permute-start(bf16[2,128,3072]{2,1,0:T(8,128)(2,1)S(1)} %collective-permute-done.10.refs_5_.refs_7_), channel_id=1, source_target_pairs={{0,1},{1,0},{2,3},{3,2},{4,5},{5,4},{6,7},{7,6},{8,9},{9,8},{10,11... | collective-permute-start | bytes 4718600 | tf_op jit(solution)/shard_map/ppermute | solution.py:15
  53.7 12.4 %collective-permute-start.13 = (bf16[128,3072]{1,0:T(8,128)(2,1)S(1)}, bf16[128,3072]{1,0:T(8,128)(2,1)S(1)}, u32[]{:S(2)}, u32[]{:S(2)}) collective-permute-start(bf16[128,3072]{1,0:T(8,128)(2,1)S(1)} %get-tuple-element.55), channel_id=1, source_target_pairs={{0,8},{1,3},{2,10},{3,5},{4,12},{5,7},{6,14},{7,1},{8,16},{9,11},{... | collective-permute-start | bytes 2359304 | tf_op jit(solution)/shard_map/ppermute | solution.py:33
  54.9 11.2 %collective-permute-start.14 = (bf16[128,3072]{1,0:T(8,128)(2,1)S(1)}, bf16[128,3072]{1,0:T(8,128)(2,1)S(1)}, u32[]{:S(2)}, u32[]{:S(2)}) collective-permute-start(bf16[128,3072]{1,0:T(8,128)(2,1)S(1)} %get-tuple-element.56), channel_id=1, source_target_pairs={{0,24},{1,7},{2,26},{3,1},{4,28},{5,3},{6,30},{7,5},{8,0},{9,15},{... | collective-permute-start | bytes 2359304 | tf_op jit(solution)/shard_map/ppermute | solution.py:33
  56.5 1.4 %collective-permute-start.12 = (s32[8]{0:T(128)S(1)}, s32[8]{0:T(128)S(1)}, u32[]{:S(2)}, u32[]{:S(2)}) collective-permute-start(s32[8]{0:T(128)S(1)} %pad_add_fusion.refs_6_.refs_11_), channel_id=1, source_target_pairs={{0,1},{1,0},{2,3},{3,2},{4,5},{5,4},{6,7},{7,6},{8,9},{9,8},{10,11... | collective-permute-start | bytes 104 | tf_op jit(solution)/shard_map/ppermute | solution.py:15
  66.1 4.7 %collective-permute-start.16 = (bf16[2,128,3072]{2,1,0:T(8,128)(2,1)S(1)}, bf16[2,128,3072]{2,1,0:T(8,128)(2,1)S(1)}, u32[]{:S(2)}, u32[]{:S(2)}) collective-permute-start(bf16[2,128,3072]{2,1,0:T(8,128)(2,1)S(1)} %collective-permute-done.11.refs_9_), channel_id=1, source_target_pairs={{0,1},{1,0},{2,3},{3,2},{4,5},{5,4},{6,7},{7,6},{8,9},{9,8},{10,11... | collective-permute-start | bytes 4718600 | tf_op jit(solution)/shard_map/ppermute | solution.py:15
  67.0 12.6 %collective-permute-start.17 = (bf16[8,64,256]{2,1,0:T(8,128)(2,1)S(1)}, bf16[8,64,256]{2,1,0:T(8,128)(2,1)S(1)}, u32[]{:S(2)}, u32[]{:S(2)}) collective-permute-start(bf16[8,64,256]{2,1,0:T(8,128)(2,1)S(1)} %get-tuple-element.62), channel_id=1, source_target_pairs={{0,32},{32,64},{64,96},{96,0},{1,33},{33,65},{65,97},{97,1},{2,34}... | collective-permute-start | bytes 786440 | tf_op jit(solution)/shard_map/ppermute | solution.py:278
  67.5 14.6 %collective-permute-start.18 = (bf16[8,64,256]{2,1,0:T(8,128)(2,1)S(1)}, bf16[8,64,256]{2,1,0:T(8,128)(2,1)S(1)}, u32[]{:S(2)}, u32[]{:S(2)}) collective-permute-start(bf16[8,64,256]{2,1,0:T(8,128)(2,1)S(1)} %get-tuple-element.63), channel_id=1, source_target_pairs={{0,64},{32,96},{64,0},{96,32},{1,65},{33,97},{65,1},{97,33},{2,66}... | collective-permute-start | bytes 786440 | tf_op jit(solution)/shard_map/ppermute | solution.py:278
  70.1 12.0 %collective-permute-start.19 = (bf16[8,64,256]{2,1,0:T(8,128)(2,1)S(1)}, bf16[8,64,256]{2,1,0:T(8,128)(2,1)S(1)}, u32[]{:S(2)}, u32[]{:S(2)}) collective-permute-start(bf16[8,64,256]{2,1,0:T(8,128)(2,1)S(1)} %get-tuple-element.64), channel_id=1, source_target_pairs={{0,96},{32,0},{64,32},{96,64},{1,97},{33,1},{65,33},{97,65},{2,98}... | collective-permute-start | bytes 786440 | tf_op jit(solution)/shard_map/ppermute | solution.py:278
  82.8 3.4 %collective-permute-start.20 = (bf16[4,8,64,256]{3,2,1,0:T(8,128)(2,1)S(1)}, bf16[4,8,64,256]{3,2,1,0:T(8,128)(2,1)S(1)}, u32[]{:S(2)}, u32[]{:S(2)}) collective-permute-start(bf16[4,8,64,256]{3,2,1,0:T(8,128)(2,1)S(1)} %shard_map.79.amps), channel_id=1, source_target_pairs={{0,1},{1,0},{2,3},{3,2},{4,5},{5,4},{6,7},{7,6},{8,9},{9,8},{10,11... | collective-permute-start | bytes 3145736 | tf_op jit(solution)/shard_map/ppermute | solution.py:15

commit v4 on v3

--- a/solution.py
+++ b/solution.py
@@ -154,13 +154,16 @@
         groups.append(refs[:count])
         refs = refs[count:]
     blocks, bds, irreps = groups
-    where, irrep_a, irrep_b, irrep_c, held, labels, fourth = refs
+    where, irrep_a, irrep_b, irrep_c, *base, held, labels, fourth = refs
     if 3 in steps:
         fourth[:128], fourth[128:] = blocks[-2][...], blocks[-1][...]
         blocks = [*blocks[:-2], fourth]
 
-    if any(len(chunk[4]) < 4 for chunk in chunks):
-        held[...] = jnp.zeros_like(held)
+    done = base[0].shape[0] if base else 0
+    if base:
+        held[:done] = base[0][...]
+    if done < held.shape[0]:
+        held[done:] = jnp.zeros((held.shape[0] - done, 256, 512), jnp.bfloat16)
     row = lax.broadcasted_iota(jnp.int32, (256, 1), 0)
     shift, inner = row // 64, row % 16
     shift = jnp.where(shift == 1, 3, jnp.where(shift == 0, 0, shift - 1))
@@ -197,7 +200,7 @@
                         ]
 
 
-def integrals(blocks, pairs, where, irrep_a, irrep_b, irrep_c):
+def integrals(blocks, pairs, where, irrep_a, irrep_b, irrep_c, base=()):
     arrays = [[], []]
     chunks = []
     for *pair, used in pairs:
@@ -214,7 +217,7 @@
     return pl.pallas_call(
         functools.partial(integral_kernel, tuple(steps), tuple(chunks), counts),
         out_shape=jax.ShapeDtypeStruct((2 * len(pairs), 256, 512), jnp.bfloat16),
-        in_specs=[vmem] * sum(counts[:2]) + [smem] * (counts[2] + 2) + [vmem] * 2,
+        in_specs=[vmem] * sum(counts[:2]) + [smem] * (counts[2] + 2) + [vmem] * (2 + len(base)),
         out_specs=vmem,
         scratch_shapes=[
             pltpu.VMEM((256 * len(steps), 1), jnp.int32),
@@ -222,16 +225,14 @@
         ],
         compiler_params=pltpu.CompilerParams(vmem_limit_bytes=12 * 1024 * 1024),
         cost_estimate=pl.CostEstimate(flops=1 << 20, bytes_accessed=1 << 10, transcendentals=0),
-    )(*pieces, *arrays[0], *arrays[1], where, irrep_a, irrep_b, irrep_c)
-
-
-def ladder_kernel(amps, amps_other, one, two, out):
+    )(*pieces, *arrays[0], *arrays[1], where, irrep_a, irrep_b, irrep_c, *base)
+
+
+def ladder_kernel(amps, amps_other, held, out):
     order = [(amps, d) for d in range(4)] + [(amps_other, d) for d in range(4)]
     order += [(t, 4 + d) for d0 in (0, 2) for t in (amps, amps_other) for d in (d0, d0 + 1)]
     left = jnp.concatenate([t[:, d].reshape(256, 256) for t, d in order], axis=1)
-    n = one.shape[0] * 256
-    total = jnp.dot(left[:, :n], one[...].reshape(n, 512), preferred_element_type=jnp.float32)
-    total += jnp.dot(left, two[...].reshape(4096, 512), preferred_element_type=jnp.float32)
+    total = jnp.dot(left, held[...].reshape(4096, 512), preferred_element_type=jnp.float32)
     out[...] = total.astype(out.dtype)
 
 
@@ -240,7 +241,7 @@
     return pl.pallas_call(
         ladder_kernel,
         out_shape=jax.ShapeDtypeStruct((256, 512), jnp.bfloat16),
-        in_specs=[vmem] * 4,
+        in_specs=[vmem] * 3,
         out_specs=vmem,
         compiler_params=pltpu.CompilerParams(vmem_limit_bytes=12 * 1024 * 1024),
         cost_estimate=pl.CostEstimate(flops=1 << 20, bytes_accessed=1 << 10, transcendentals=0),
@@ -269,40 +270,41 @@
     near_first, near_last = around(bd_first), around(bd_last)
     other_far = swap(near_irreps)
     rows = join([rows] + lines)
-    rows, amplitudes = lax.optimization_barrier((rows, amplitudes))
+    rows, amplitudes, other_far = lax.optimization_barrier((rows, amplitudes, other_far))
     one, three = along(rows, "yx", (1, 3))
 
     parted = part_amplitudes(amplitudes, where)
-    one, three, near_first, *parted = lax.optimization_barrier((one, three, near_first, *parted))
+    rest = (where, irrep_a, irrep_b.reshape(1, 128), irrep_c.reshape(1, 512))
+    first = [((bd_factor, at), (near_irreps, at)) for at in (0, 2)]
+    first += [((bd_core, at), (other_far, at)) for at in (0, 2)]
+    held = integrals([[rows]], [(*pair, (0,)) for pair in first], *rest)
+    far_first = swap(near_first)
+    one, three, far_first, near_last, held, *parted = lax.optimization_barrier(
+        (one, three, far_first, near_last, held, *parted)
+    )
     parted = [
         lax.ppermute(part, Z, [(z, (z + step) % 4) for z in range(4)]) if step else part
         for step, part in enumerate(parted)
     ]
 
-    far_first = swap(near_first)
     one_half, three_half = halve(one, three)
     (two_first,) = along(one_half, "yx", (1,))
     (two_last,) = along(three_half, "yx", (3,))
 
-    rest = (where, irrep_a, irrep_b.reshape(1, 128), irrep_c.reshape(1, 512))
     blocks = [[rows], [one], [three], [two_first, two_last]]
-    first = [((bd_factor, at), (near_irreps, at)) for at in (0, 2)]
-    first += [((bd_core, at), (other_far, at)) for at in (0, 2)]
-    first += [((near_first, 0), (near_irreps, 4))]
-    held_first = integrals(blocks, [(*pair, (0, 1, 2)) for pair in first], *rest)
-    near_last, held_first, two_first, two_last, far_first = lax.optimization_barrier(
-        (near_last, held_first, two_first, two_last, far_first)
-    )
+    close = [((near_first, 0), (near_irreps, 4)), ((far_first, 0), (other_far, 4))]
+    far_last = swap(near_last)
+    close += [((near_last, 0), (near_irreps, 6)), ((far_last, 0), (other_far, 6))]
+    held = integrals(
+        blocks, [(*pair, (1, 2)) for pair in first] + [(*pair, (0, 1, 2)) for pair in close], *rest, (held,)
+    )
+    held, two_first, two_last, parted[2] = lax.optimization_barrier((held, two_first, two_last, parted[2]))
     blocks[3] = [two_first, two_last]
-    far_last = swap(near_last)
-    last = [((far_first, 0), (other_far, 4)), ((near_last, 0), (near_irreps, 6)), ((far_last, 0), (other_far, 6))]
-    held_last = integrals(
-        blocks, [(*pair, (3,)) for pair in first] + [(*pair, (0, 1, 2, 3)) for pair in last], *rest
-    )
-    held_last, *parted = lax.optimization_barrier((held_last, *parted))
+    held = integrals(blocks, [(*pair, (3,)) for pair in first + close], *rest, (held,))
+    held, *parted = lax.optimization_barrier((held, *parted))
     amps = order_pairs(*parted, where)
     amps_other = swap(amps)
-    total = ladder(amps, amps_other, held_first, held_last)
+    total = ladder(amps, amps_other, held)
 
     pieces = total.reshape(128, 2, 512)
     pieces = lax.all_to_all(pieces, ALL, split_axis=0, concat_axis=0, tiled=True)

time: 109 us -> 98.8 us (0.906)
  waiting for transfers between devices: 28.9 us -> 20.8 us
  blocking collectives: 19.9 us -> 16 us
  Pallas kernels: 24 us -> 25.5 us
    ppermute x7, waiting for transfers between devices: 19.7 us -> 8.77 us  [moved(): return lax.ppermute(block, ('y', 'x', 'core'), pairs)]
    ppermute x3, waiting for transfers between devices: 3.13 us -> 9.77 us  [around(): return lax.ppermute(block, Z + ('core',), pairs)]
    all_to_all x1, blocking collectives: 19.9 us -> 16 us  [body(): lax.all_to_all(pieces, ALL, split_axis=0, concat_axis=0, tiled=True)]
    ppermute x3, waiting for transfers between devices: 2.48 us -> 0.01 us  [body(): lax.ppermute(part, Z, [(z, (z + step) % 4) for z in range(4)])]
    pallas_call x2 -> x3, Pallas kernels: 16.6 us -> 18.8 us  [integrals(): pl.pallas_call(functools.partial(integral_kernel, tuple(steps), tuple(chu...]
    ppermute x1, starting transfers between devices: 2.09 us -> 0.01 us  [body(): from_z = lax.ppermute(mine, 'zh', [(0, 1), (1, 0)])]
    ppermute x6, starting transfers between devices: 8.33 us -> 6.73 us  [swap(): return lax.ppermute(block, 'core', [(0, 1), (1, 0)])]
    slice x1, local copies, waits for them, and re-layouts: 2.13 us -> 3.72 us  [body(): bd_factor[2:]]
  transfers between devices with their start and end apart: 21 -> 21, of which waited for: 10 -> 6; matrix products, arithmetic and copies ran while one was open for 4% -> 5% of each run, Pallas kernels for 19% -> 24%
where the time goes in v4:
time: 98.8 us; the launch traced here: 98.5 us
  starting transfers between devices  30.1 us (30%)
  Pallas kernels  25.5 us (26%)
  waiting for transfers between devices  20.8 us (21%)
  blocking collectives  16 us (16%)
  local copies, waits for them, and re-layouts  5.55 us (6%)
    pallas_call x3, Pallas kernels, integrals(): pl.pallas_call(functools.partial(integral_kernel, tuple(steps), tuple(chu...  18.8 us
    all_to_all x1, blocking collectives, body(): lax.all_to_all(pieces, ALL, split_axis=0, concat_axis=0, tiled=True)  16 us
    ppermute x7, starting transfers between devices, moved(): return lax.ppermute(block, ('y', 'x', 'core'), pairs)  9.94 us
    ppermute x3, waiting for transfers between devices, around(): return lax.ppermute(block, Z + ('core',), pairs)  9.77 us
    ppermute x7, waiting for transfers between devices, moved(): return lax.ppermute(block, ('y', 'x', 'core'), pairs)  8.77 us
    ppermute x6, starting transfers between devices, swap(): return lax.ppermute(block, 'core', [(0, 1), (1, 0)])  6.73 us
    ppermute x3, starting transfers between devices, body(): lax.ppermute(part, Z, [(z, (z + step) % 4) for z in range(4)])  4.87 us
    ppermute x3, starting transfers between devices, around(): return lax.ppermute(block, Z + ('core',), pairs)  4.51 us
  transfers between devices with their start and end apart: 21, of which 6 were waited for; matrix products, arithmetic and copies ran while one was open for 5% of the time, Pallas kernels for 24%

profile of v4, /device:TPU:1, one launch (start us, length us, event | category | flops | bytes accessed | tf_op | source)
XLA Modules:
  0.0 98.5 jit_solution(12308227331368621087)
XLA Ops:
  0.0 1.4 %collective-permute-start.4 = (bf16[4,128,3072]{2,1,0:T(8,128)(2,1)}, bf16[4,128,3072]{2,1,0:T(8,128)(2,1)S(1)}, u32[]{:S(2)}, u32[]{:S(2)}) collective-permute-start(bf16[4,128,3072]{2,1,0:T(8,128)(2,1)} %refs_2_.1), channel_id=1, source_target_pairs={{0,1},{1,0},{2,3},{3,2},{4,5},{5,4},{6,7},{7,6},{8,9},{9,8},{10,11... | collective-permute-start | bytes 9437192 | tf_op jit(solution)/shard_map/ppermute | solution.py:15
  1.4 1.0 reshape.19
  2.4 0.1 collective-permute-start
  2.5 4.1 %collective-permute-start.2 = (bf16[16,3072]{1,0:T(8,128)(2,1)S(1)}, bf16[16,3072]{1,0:T(8,128)(2,1)S(1)}, u32[]{:S(2)}, u32[]{:S(2)}) collective-permute-start(bf16[16,3072]{1,0:T(8,128)(2,1)S(1)} %get-tuple-element.77), channel_id=1, source_target_pairs={{0,65},{1,64},{64,1},{65,0},{2,67},{3,66},{66,3},{67,2},{4,69},{5,... | collective-permute-start | bytes 294920 | tf_op jit(solution)/shard_map/ppermute | solution.py:260
  6.6 0.0 collective-permute-start.1
  6.6 3.1 %collective-permute-start.3 = (s32[4]{0:T(128)}, s32[4]{0:T(128)S(1)}, u32[]{:S(2)}, u32[]{:S(2)}) collective-permute-start(s32[4]{0:T(128)} %param.13), channel_id=1, source_target_pairs={{0,32},{1,97},{32,64},{33,1},{64,96},{65,33},{96,0},{97,65},{2,34}... | collective-permute-start | bytes 56 | tf_op jit(solution)/shard_map/ppermute | solution.py:22
  9.7 3.7 %fusion = (bf16[2,128,3072]{2,1,0:T(8,128)(2,1)}, bf16[2,128,3072]{2,1,0:T(8,128)(2,1)}) fusion(bf16[4,128,3072]{2,1,0:T(8,128)(2,1)} %refs_2_.1), kind=kLoop, calls=%fused_computation.3 | loop fusion | bytes 6291456 | tf_op jit(solution)/shard_map/slice | solution.py:265
  13.5 0.0 collective-permute-done.3
  13.5 0.0 copy-done.5
  13.5 0.1 pad_add_fusion.refs_3_.refs_9_.refs_8_
  13.5 0.0 collective-permute-done.from_core
  13.5 0.0 collective-permute-done.1.from_z
  13.5 0.0 collective-permute-done.2.from_both
  13.6 0.0 collective-permute-done.4.refs_2_.refs_4_.refs_3_
  13.6 1.3 %collective-permute-start.11 = (bf16[2,128,3072]{2,1,0:T(8,128)(2,1)}, bf16[2,128,3072]{2,1,0:T(8,128)(2,1)}, u32[]{:S(2)}, u32[]{:S(2)}) collective-permute-start(bf16[2,128,3072]{2,1,0:T(8,128)(2,1)} %get-tuple-element.46), channel_id=1, source_target_pairs={{0,32},{1,97},{32,64},{33,1},{64,96},{65,33},{96,0},{97,65},{2,34}... | collective-permute-start | bytes 4718600 | tf_op jit(solution)/shard_map/ppermute | solution.py:22
  14.9 0.1 stack.23.where.refs_5_.refs_11_.refs_10_
  15.0 0.7 shard_map.73.refs_0_
  15.7 0.0 copy-start
  15.7 0.0 copy-start.2
  15.7 0.0 copy-start.3
  15.7 0.0 copy-start.4
  15.7 1.4 %collective-permute-start.5 = (bf16[64,3072]{1,0:T(8,128)(2,1)S(1)}, bf16[64,3072]{1,0:T(8,128)(2,1)S(1)}, u32[]{:S(2)}, u32[]{:S(2)}) collective-permute-start(bf16[64,3072]{1,0:T(8,128)(2,1)S(1)} %shard_map.73.refs_0_), channel_id=1, source_target_pairs={{0,2},{1,9},{2,4},{3,11},{4,6},{5,13},{6,0},{7,15},{8,10},{9,17},{... | collective-permute-start | bytes 1179656 | tf_op jit(solution)/shard_map/ppermute | solution.py:33
  17.1 1.5 %collective-permute-start.6 = (bf16[64,3072]{1,0:T(8,128)(2,1)S(1)}, bf16[64,3072]{1,0:T(8,128)(2,1)S(1)}, u32[]{:S(2)}, u32[]{:S(2)}) collective-permute-start(bf16[64,3072]{1,0:T(8,128)(2,1)S(1)} %shard_map.73.refs_0_), channel_id=1, source_target_pairs={{0,6},{1,25},{2,0},{3,27},{4,2},{5,29},{6,4},{7,31},{8,14},{9,1},{... | collective-permute-start | bytes 1179656 | tf_op jit(solution)/shard_map/ppermute | solution.py:33
  18.6 1.6 %collective-permute-start.7 = (bf16[64,3072]{1,0:T(8,128)(2,1)S(1)}, bf16[64,3072]{1,0:T(8,128)(2,1)S(1)}, u32[]{:S(2)}, u32[]{:S(2)}) collective-permute-start(bf16[64,3072]{1,0:T(8,128)(2,1)S(1)} %shard_map.73.refs_0_), channel_id=1, source_target_pairs={{0,4},{1,17},{2,6},{3,19},{4,0},{5,21},{6,2},{7,23},{8,12},{9,25},... | collective-permute-start | bytes 1179656 | tf_op jit(solution)/shard_map/ppermute | solution.py:33
  20.2 0.1 collective-permute-start.8
  20.3 3.8 %collective-permute-done.5.refs_1_ = bf16[64,3072]{1,0:T(8,128)(2,1)S(1)} collective-permute-done((bf16[64,3072]{1,0:T(8,128)(2,1)S(1)}, bf16[64,3072]{1,0:T(8,128)(2,1)S(1)}, u32[]{:S(2)}, u32[]{:S(2)}) %collective-permute-start.5) | collective-permute-done | bytes 393248 | tf_op jit(solution)/shard_map/ppermute | solution.py:33
  24.1 0.0 collective-permute-start.13
  24.1 3.4 %collective-permute-done.6.refs_2_ = bf16[64,3072]{1,0:T(8,128)(2,1)S(1)} collective-permute-done((bf16[64,3072]{1,0:T(8,128)(2,1)S(1)}, bf16[64,3072]{1,0:T(8,128)(2,1)S(1)}, u32[]{:S(2)}, u32[]{:S(2)}) %collective-permute-start.6) | collective-permute-done | bytes 393248 | tf_op jit(solution)/shard_map/ppermute | solution.py:33
  27.6 1.5 %collective-permute-done.7.refs_3_ = bf16[64,3072]{1,0:T(8,128)(2,1)S(1)} collective-permute-done((bf16[64,3072]{1,0:T(8,128)(2,1)S(1)}, bf16[64,3072]{1,0:T(8,128)(2,1)S(1)}, u32[]{:S(2)}, u32[]{:S(2)}) %collective-permute-start.7) | collective-permute-done | bytes 393248 | tf_op jit(solution)/shard_map/ppermute | solution.py:33
  29.1 0.1 shard_map.74.refs_0_
  29.2 0.0 collective-permute-done.8.refs_4_.refs_10_.refs_9_
  29.2 1.3 %collective-permute-start.9 = (bf16[256,3072]{1,0:T(8,128)(2,1)S(1)}, bf16[256,3072]{1,0:T(8,128)(2,1)S(1)}, u32[]{:S(2)}, u32[]{:S(2)}) collective-permute-start(bf16[256,3072]{1,0:T(8,128)(2,1)S(1)} %shard_map.74.refs_0_), channel_id=1, source_target_pairs={{0,8},{1,3},{2,10},{3,5},{4,12},{5,7},{6,14},{7,1},{8,16},{9,11},{... | collective-permute-start | bytes 4718600 | tf_op jit(solution)/shard_map/ppermute | solution.py:33
  30.5 1.5 %collective-permute-start.10 = (bf16[256,3072]{1,0:T(8,128)(2,1)S(1)}, bf16[256,3072]{1,0:T(8,128)(2,1)S(1)}, u32[]{:S(2)}, u32[]{:S(2)}) collective-permute-start(bf16[256,3072]{1,0:T(8,128)(2,1)S(1)} %shard_map.74.refs_0_), channel_id=1, source_target_pairs={{0,24},{1,7},{2,26},{3,1},{4,28},{5,3},{6,30},{7,5},{8,0},{9,15},{... | collective-permute-start | bytes 4718600 | tf_op jit(solution)/shard_map/ppermute | solution.py:33
  32.0 1.6 %collective-permute-done.11.refs_5_.refs_4_ = bf16[2,128,3072]{2,1,0:T(8,128)(2,1)} collective-permute-done((bf16[2,128,3072]{2,1,0:T(8,128)(2,1)}, bf16[2,128,3072]{2,1,0:T(8,128)(2,1)}, u32[]{:S(2)}, u32[]{:S(2)}) %collective-permute-start.11) | collective-permute-done | bytes 1572896 | tf_op jit(solution)/shard_map/ppermute | solution.py:22
  33.5 1.8 %collective-permute-start.12 = (bf16[2,128,3072]{2,1,0:T(8,128)(2,1)}, bf16[2,128,3072]{2,1,0:T(8,128)(2,1)S(1)}, u32[]{:S(2)}, u32[]{:S(2)}) collective-permute-start(bf16[2,128,3072]{2,1,0:T(8,128)(2,1)} %collective-permute-done.11.refs_5_.refs_4_), channel_id=1, source_target_pairs={{0,1},{1,0},{2,3},{3,2},{4,5},{5,4},{6,7},{7,6},{8,9},{9,8},{10,11... | collective-permute-start | bytes 4718600 | tf_op jit(solution)/shard_map/ppermute | solution.py:15
  35.3 4.0 %shard_map.76 = (bf16[8,64,256]{2,1,0:T(8,128)(2,1)S(1)}, bf16[8,64,256]{2,1,0:T(8,128)(2,1)S(1)}, bf16[8,64,256]{2,1,0:T(8,128)(2,1)S(1)}, bf16[8,64,256]{2,1,0:T(8,128)(2,1)S(1)}) custom-call(bf16[64,16,512]{2,1,0:T(8,128)(2,1)S(1)} %copy-done.1, s32[5]{0:T(128)S(1)} %stack.23.where.refs_5_.refs_11_.refs_10_), custom_call_target="tpu_custom_call" | custom-call | flops 1048576 | bytes 1024 | tf_op jit(solution)/shard_map/pallas_call | solution.py:59
  39.3 2.7 %shard_map.75.refs_15_ = bf16[8,256,512]{2,1,0:T(8,128)(2,1)S(1)} custom-call(bf16[256,3072]{1,0:T(8,128)(2,1)S(1)} %shard_map.74.refs_0_, bf16[4,128,3072]{2,1,0:T(8,128)(2,1)S(1)} %copy-done, bf16[4,128,3072]{2,1,0:T(8,128)(2,1)S(1)} %collective-permute-done.4.refs_2_.refs_4_.refs_3_, s32[8]{0:T(128)S(1)} %pad_add_fusion.refs_3_.refs_9_.refs_8_, ...), custom_call_target="tpu_custom_call" | custom-call | flops 1048576 | bytes 1024 | tf_op jit(solution)/shard_map/pallas_call | solution.py:217
  42.0 8.2 %collective-permute-done.13.refs_7_.refs_6_ = bf16[2,128,3072]{2,1,0:T(8,128)(2,1)S(1)} collective-permute-done((bf16[2,128,3072]{2,1,0:T(8,128)(2,1)}, bf16[2,128,3072]{2,1,0:T(8,128)(2,1)S(1)}, u32[]{:S(2)}, u32[]{:S(2)}) %collective-permute-start.13) | collective-permute-done | bytes 1572896 | tf_op jit(solution)/shard_map/ppermute | solution.py:22
  50.3 0.0 collective-permute-done.9.refs_1_.one
  50.3 0.0 collective-permute-done.10.refs_2_.three
  50.3 0.0 collective-permute-done.12.refs_6_.refs_5_
  50.3 1.8 %collective-permute-start.14 = (bf16[2,128,3072]{2,1,0:T(8,128)(2,1)S(1)}, bf16[2,128,3072]{2,1,0:T(8,128)(2,1)S(1)}, u32[]{:S(2)}, u32[]{:S(2)}) collective-permute-start(bf16[2,128,3072]{2,1,0:T(8,128)(2,1)S(1)} %collective-permute-done.13.refs_7_.refs_6_), channel_id=1, source_target_pairs={{0,1},{1,0},{2,3},{3,2},{4,5},{5,4},{6,7},{7,6},{8,9},{9,8},{10,11... | collective-permute-start | bytes 4718600 | tf_op jit(solution)/shard_map/ppermute | solution.py:15
  52.1 0.1 shard_map.78
  52.2 1.3 %collective-permute-start.15 = (bf16[128,3072]{1,0:T(8,128)(2,1)S(1)}, bf16[128,3072]{1,0:T(8,128)(2,1)S(1)}, u32[]{:S(2)}, u32[]{:S(2)}) collective-permute-start(bf16[128,3072]{1,0:T(8,128)(2,1)S(1)} %get-tuple-element.60), channel_id=1, source_target_pairs={{0,8},{1,3},{2,10},{3,5},{4,12},{5,7},{6,14},{7,1},{8,16},{9,11},{... | collective-permute-start | bytes 2359304 | tf_op jit(solution)/shard_map/ppermute | solution.py:33
  53.5 1.5 %collective-permute-start.16 = (bf16[128,3072]{1,0:T(8,128)(2,1)S(1)}, bf16[128,3072]{1,0:T(8,128)(2,1)S(1)}, u32[]{:S(2)}, u32[]{:S(2)}) collective-permute-start(bf16[128,3072]{1,0:T(8,128)(2,1)S(1)} %get-tuple-element.61), channel_id=1, source_target_pairs={{0,24},{1,7},{2,26},{3,1},{4,28},{5,3},{6,30},{7,5},{8,0},{9,15},{... | collective-permute-start | bytes 2359304 | tf_op jit(solution)/shard_map/ppermute | solution.py:33
  55.0 2.2 %collective-permute-start.17 = (bf16[8,64,256]{2,1,0:T(8,128)(2,1)S(1)}, bf16[8,64,256]{2,1,0:T(8,128)(2,1)S(1)}, u32[]{:S(2)}, u32[]{:S(2)}) collective-permute-start(bf16[8,64,256]{2,1,0:T(8,128)(2,1)S(1)} %get-tuple-element.62), channel_id=1, source_target_pairs={{0,64},{32,96},{64,0},{96,32},{1,65},{33,97},{65,1},{97,33},{2,66}... | collective-permute-start | bytes 786440 | tf_op jit(solution)/shard_map/ppermute | solution.py:286
  57.2 0.0 collective-permute-start.18
  57.2 0.0 collective-permute-done.14.refs_8_.refs_7_
  57.2 2.7 %collective-permute-start.19 = (bf16[8,64,256]{2,1,0:T(8,128)(2,1)S(1)}, bf16[8,64,256]{2,1,0:T(8,128)(2,1)S(1)}, u32[]{:S(2)}, u32[]{:S(2)}) collective-permute-start(bf16[8,64,256]{2,1,0:T(8,128)(2,1)S(1)} %get-tuple-element.69), channel_id=1, source_target_pairs={{0,96},{32,0},{64,32},{96,64},{1,97},{33,1},{65,33},{97,65},{2,98}... | collective-permute-start | bytes 786440 | tf_op jit(solution)/shard_map/ppermute | solution.py:286
  59.8 10.7 %shard_map.77.refs_14_ = bf16[16,256,512]{2,1,0:T(8,128)(2,1)S(1)} custom-call(bf16[256,3072]{1,0:T(8,128)(2,1)S(1)} %shard_map.74.refs_0_, bf16[256,3072]{1,0:T(8,128)(2,1)S(1)} %collective-permute-done.9.refs_1_.one, bf16[256,3072]{1,0:T(8,128)(2,1)S(1)} %collective-permute-done.10.refs_2_.three, bf16[4,128,3072]{2,1,0:T(8,128)(2,1)S(1)} %copy-done, ...), custom_call_target="tpu_custom_call" | custom-call | flops 1048576 | bytes 1024 | tf_op jit(solution)/shard_map/pallas_call | solution.py:217
  70.5 0.0 collective-permute-done.17.two
  70.6 0.0 collective-permute-done.15.refs_0_
  70.6 0.0 collective-permute-done.16.refs_1_
  70.6 5.3 %shard_map.79.held = bf16[16,256,512]{2,1,0:T(8,128)(2,1)S(1)} custom-call(bf16[128,3072]{1,0:T(8,128)(2,1)S(1)} %collective-permute-done.15.refs_0_, bf16[128,3072]{1,0:T(8,128)(2,1)S(1)} %collective-permute-done.16.refs_1_, bf16[4,128,3072]{2,1,0:T(8,128)(2,1)S(1)} %copy-done, bf16[4,128,3072]{2,1,0:T(8,128)(2,1)S(1)} %collective-permute-done.4.refs_2_.refs_4_.refs_3_, ...), custom_call_target="tpu_custom_call" | custom-call | flops 1048576 | bytes 1024 | tf_op jit(solution)/shard_map/pallas_call | solution.py:217
  75.9 0.0 collective-permute-done.18.one
  75.9 0.0 collective-permute-done.19.three
  75.9 0.6 shard_map.80.amps
  76.6 1.5 %collective-permute-start.20 = (bf16[4,8,64,256]{3,2,1,0:T(8,128)(2,1)S(1)}, bf16[4,8,64,256]{3,2,1,0:T(8,128)(2,1)S(1)}, u32[]{:S(2)}, u32[]{:S(2)}) collective-permute-start(bf16[4,8,64,256]{3,2,1,0:T(8,128)(2,1)S(1)} %shard_map.80.amps), channel_id=1, source_target_pairs={{0,1},{1,0},{2,3},{3,2},{4,5},{5,4},{6,7},{7,6},{8,9},{9,8},{10,11... | collective-permute-start | bytes 3145736 | tf_op jit(solution)/shard_map/ppermute | solution.py:15
  78.1 2.3 %collective-permute-done.20.amps_other = bf16[4,8,64,256]{3,2,1,0:T(8,128)(2,1)S(1)} collective-permute-done((bf16[4,8,64,256]{3,2,1,0:T(8,128)(2,1)S(1)}, bf16[4,8,64,256]{3,2,1,0:T(8,128)(2,1)S(1)}, u32[]{:S(2)}, u32[]{:S(2)}) %collective-permute-start.20) | collective-permute-done | bytes 1048608 | tf_op jit(solution)/shard_map/ppermute | solution.py:15
  80.3 1.2 %shard_map.81 = bf16[256,512]{1,0:T(8,128)(2,1)S(1)} custom-call(bf16[4,8,64,256]{3,2,1,0:T(8,128)(2,1)S(1)} %shard_map.80.amps, bf16[4,8,64,256]{3,2,1,0:T(8,128)(2,1)S(1)} %collective-permute-done.20.amps_other, bf16[16,256,512]{2,1,0:T(8,128)(2,1)S(1)} %shard_map.79.held), custom_call_target="tpu_custom_call" | custom-call | flops 1048576 | bytes 1024 | tf_op jit(solution)/shard_map/pallas_call | solution.py:241
  81.6 0.1 reshape.22
  81.7 16.0 %all_to_all.5 = bf16[128,2,512]{2,1,0:T(2,128)(2,1)S(1)} all-to-all(bf16[128,2,512]{2,1,0:T(2,128)(2,1)S(1)} %reshape.22), channel_id=1, replica_groups=mesh['zh'=2,'zl'=2,'y'=4,'x'=4,'core'=2] {'zh','zl','y','x','core'}, dimensions={0} | all-to-all | bytes 524288 | tf_op jit(solution)/shard_map/all_to_all | solution.py:310
  97.7 0.2 reduce
  97.9 0.6 copy.8
  (9 shorter events, 0.0 us)
Async XLA Ops:
  0.0 13.6 %collective-permute-start.4 = (bf16[4,128,3072]{2,1,0:T(8,128)(2,1)}, bf16[4,128,3072]{2,1,0:T(8,128)(2,1)S(1)}, u32[]{:S(2)}, u32[]{:S(2)}) collective-permute-start(bf16[4,128,3072]{2,1,0:T(8,128)(2,1)} %refs_2_.1), channel_id=1, source_target_pairs={{0,1},{1,0},{2,3},{3,2},{4,5},{5,4},{6,7},{7,6},{8,9},{9,8},{10,11... | collective-permute-start | bytes 9437192 | tf_op jit(solution)/shard_map/ppermute | solution.py:15
  2.4 11.1 %collective-permute-start = (bf16[16,3072]{1,0:T(8,128)(2,1)S(1)}, bf16[16,3072]{1,0:T(8,128)(2,1)S(1)}, u32[]{:S(2)}, u32[]{:S(2)}) collective-permute-start(bf16[16,3072]{1,0:T(8,128)(2,1)S(1)} %get-tuple-element.77), channel_id=1, source_target_pairs={{0,1},{1,0},{2,3},{3,2},{4,5},{5,4},{6,7},{7,6},{8,9},{9,8},{10,11... | collective-permute-start | bytes 294920 | tf_op jit(solution)/shard_map/ppermute | solution.py:15
  2.5 11.0 %collective-permute-start.2 = (bf16[16,3072]{1,0:T(8,128)(2,1)S(1)}, bf16[16,3072]{1,0:T(8,128)(2,1)S(1)}, u32[]{:S(2)}, u32[]{:S(2)}) collective-permute-start(bf16[16,3072]{1,0:T(8,128)(2,1)S(1)} %get-tuple-element.77), channel_id=1, source_target_pairs={{0,65},{1,64},{64,1},{65,0},{2,67},{3,66},{66,3},{67,2},{4,69},{5,... | collective-permute-start | bytes 294920 | tf_op jit(solution)/shard_map/ppermute | solution.py:260
  6.6 6.9 %copy-start.5 = (s32[4]{0:T(128)S(1)}, s32[4]{0:T(128)}, u32[]{:S(2)}) copy-start(s32[4]{0:T(128)} %param.13) | copy-start | bytes 52
  6.6 7.0 %collective-permute-start.1 = (bf16[16,3072]{1,0:T(8,128)(2,1)S(1)}, bf16[16,3072]{1,0:T(8,128)(2,1)S(1)}, u32[]{:S(2)}, u32[]{:S(2)}) collective-permute-start(bf16[16,3072]{1,0:T(8,128)(2,1)S(1)} %get-tuple-element.40.mine), channel_id=1, source_target_pairs={{0,64},{64,0},{1,65},{65,1},{2,66},{66,2},{3,67},{67,3},{4,68},{68... | collective-permute-start | bytes 294920 | tf_op jit(solution)/shard_map/ppermute | solution.py:259
  6.6 6.9 %collective-permute-start.3 = (s32[4]{0:T(128)}, s32[4]{0:T(128)S(1)}, u32[]{:S(2)}, u32[]{:S(2)}) collective-permute-start(s32[4]{0:T(128)} %param.13), channel_id=1, source_target_pairs={{0,32},{1,97},{32,64},{33,1},{64,96},{65,33},{96,0},{97,65},{2,34}... | collective-permute-start | bytes 56 | tf_op jit(solution)/shard_map/ppermute | solution.py:22
  13.6 19.9 %collective-permute-start.11 = (bf16[2,128,3072]{2,1,0:T(8,128)(2,1)}, bf16[2,128,3072]{2,1,0:T(8,128)(2,1)}, u32[]{:S(2)}, u32[]{:S(2)}) collective-permute-start(bf16[2,128,3072]{2,1,0:T(8,128)(2,1)} %get-tuple-element.46), channel_id=1, source_target_pairs={{0,32},{1,97},{32,64},{33,1},{64,96},{65,33},{96,0},{97,65},{2,34}... | collective-permute-start | bytes 4718600 | tf_op jit(solution)/shard_map/ppermute | solution.py:22
  15.0 20.3 %copy-start.1 = (bf16[64,16,512]{2,1,0:T(8,128)(2,1)S(1)}, bf16[64,16,512]{2,1,0:T(8,128)(2,1)}, u32[]{:S(2)}) copy-start(bf16[64,16,512]{2,1,0:T(8,128)(2,1)} %amps) | copy-start | bytes 3145732
  15.7 23.6 %copy-start = (bf16[4,128,3072]{2,1,0:T(8,128)(2,1)S(1)}, bf16[4,128,3072]{2,1,0:T(8,128)(2,1)}, u32[]{:S(2)}) copy-start(bf16[4,128,3072]{2,1,0:T(8,128)(2,1)} %refs_2_.1) | copy-start | bytes 9437188
  15.7 23.6 %copy-start.2 = (s32[512]{0:T(512)S(1)}, s32[512]{0:T(512)}, u32[]{:S(2)}) copy-start(s32[512]{0:T(512)} %param.12) | copy-start | bytes 6148
  15.7 23.6 %copy-start.3 = (s32[8]{0:T(128)S(1)}, s32[8]{0:T(128)}, u32[]{:S(2)}) copy-start(s32[8]{0:T(128)} %refs_11_.1) | copy-start | bytes 100
  15.7 23.6 %copy-start.4 = (s32[128]{0:T(128)S(1)}, s32[128]{0:T(128)}, u32[]{:S(2)}) copy-start(s32[128]{0:T(128)} %param.11) | copy-start | bytes 1540
  15.7 8.4 %collective-permute-start.5 = (bf16[64,3072]{1,0:T(8,128)(2,1)S(1)}, bf16[64,3072]{1,0:T(8,128)(2,1)S(1)}, u32[]{:S(2)}, u32[]{:S(2)}) collective-permute-start(bf16[64,3072]{1,0:T(8,128)(2,1)S(1)} %shard_map.73.refs_0_), channel_id=1, source_target_pairs={{0,2},{1,9},{2,4},{3,11},{4,6},{5,13},{6,0},{7,15},{8,10},{9,17},{... | collective-permute-start | bytes 1179656 | tf_op jit(solution)/shard_map/ppermute | solution.py:33
  17.1 10.5 %collective-permute-start.6 = (bf16[64,3072]{1,0:T(8,128)(2,1)S(1)}, bf16[64,3072]{1,0:T(8,128)(2,1)S(1)}, u32[]{:S(2)}, u32[]{:S(2)}) collective-permute-start(bf16[64,3072]{1,0:T(8,128)(2,1)S(1)} %shard_map.73.refs_0_), channel_id=1, source_target_pairs={{0,6},{1,25},{2,0},{3,27},{4,2},{5,29},{6,4},{7,31},{8,14},{9,1},{... | collective-permute-start | bytes 1179656 | tf_op jit(solution)/shard_map/ppermute | solution.py:33
  18.6 10.5 %collective-permute-start.7 = (bf16[64,3072]{1,0:T(8,128)(2,1)S(1)}, bf16[64,3072]{1,0:T(8,128)(2,1)S(1)}, u32[]{:S(2)}, u32[]{:S(2)}) collective-permute-start(bf16[64,3072]{1,0:T(8,128)(2,1)S(1)} %shard_map.73.refs_0_), channel_id=1, source_target_pairs={{0,4},{1,17},{2,6},{3,19},{4,0},{5,21},{6,2},{7,23},{8,12},{9,25},... | collective-permute-start | bytes 1179656 | tf_op jit(solution)/shard_map/ppermute | solution.py:33
  20.2 9.0 %collective-permute-start.8 = (s32[8]{0:T(128)S(1)}, s32[8]{0:T(128)S(1)}, u32[]{:S(2)}, u32[]{:S(2)}) collective-permute-start(s32[8]{0:T(128)S(1)} %pad_add_fusion.refs_3_.refs_9_.refs_8_), channel_id=1, source_target_pairs={{0,1},{1,0},{2,3},{3,2},{4,5},{5,4},{6,7},{7,6},{8,9},{9,8},{10,11... | collective-permute-start | bytes 104 | tf_op jit(solution)/shard_map/ppermute | solution.py:15
  24.1 26.2 %collective-permute-start.13 = (bf16[2,128,3072]{2,1,0:T(8,128)(2,1)}, bf16[2,128,3072]{2,1,0:T(8,128)(2,1)S(1)}, u32[]{:S(2)}, u32[]{:S(2)}) collective-permute-start(bf16[2,128,3072]{2,1,0:T(8,128)(2,1)} %get-tuple-element.47), channel_id=1, source_target_pairs={{0,32},{1,97},{32,64},{33,1},{64,96},{65,33},{96,0},{97,65},{2,34}... | collective-permute-start | bytes 4718600 | tf_op jit(solution)/shard_map/ppermute | solution.py:22
  29.2 21.0 %collective-permute-start.9 = (bf16[256,3072]{1,0:T(8,128)(2,1)S(1)}, bf16[256,3072]{1,0:T(8,128)(2,1)S(1)}, u32[]{:S(2)}, u32[]{:S(2)}) collective-permute-start(bf16[256,3072]{1,0:T(8,128)(2,1)S(1)} %shard_map.74.refs_0_), channel_id=1, source_target_pairs={{0,8},{1,3},{2,10},{3,5},{4,12},{5,7},{6,14},{7,1},{8,16},{9,11},{... | collective-permute-start | bytes 4718600 | tf_op jit(solution)/shard_map/ppermute | solution.py:33
  30.5 19.8 %collective-permute-start.10 = (bf16[256,3072]{1,0:T(8,128)(2,1)S(1)}, bf16[256,3072]{1,0:T(8,128)(2,1)S(1)}, u32[]{:S(2)}, u32[]{:S(2)}) collective-permute-start(bf16[256,3072]{1,0:T(8,128)(2,1)S(1)} %shard_map.74.refs_0_), channel_id=1, source_target_pairs={{0,24},{1,7},{2,26},{3,1},{4,28},{5,3},{6,30},{7,5},{8,0},{9,15},{... | collective-permute-start | bytes 4718600 | tf_op jit(solution)/shard_map/ppermute | solution.py:33
  33.5 16.8 %collective-permute-start.12 = (bf16[2,128,3072]{2,1,0:T(8,128)(2,1)}, bf16[2,128,3072]{2,1,0:T(8,128)(2,1)S(1)}, u32[]{:S(2)}, u32[]{:S(2)}) collective-permute-start(bf16[2,128,3072]{2,1,0:T(8,128)(2,1)} %collective-permute-done.11.refs_5_.refs_4_), channel_id=1, source_target_pairs={{0,1},{1,0},{2,3},{3,2},{4,5},{5,4},{6,7},{7,6},{8,9},{9,8},{10,11... | collective-permute-start | bytes 4718600 | tf_op jit(solution)/shard_map/ppermute | solution.py:15
  50.3 6.9 %collective-permute-start.14 = (bf16[2,128,3072]{2,1,0:T(8,128)(2,1)S(1)}, bf16[2,128,3072]{2,1,0:T(8,128)(2,1)S(1)}, u32[]{:S(2)}, u32[]{:S(2)}) collective-permute-start(bf16[2,128,3072]{2,1,0:T(8,128)(2,1)S(1)} %collective-permute-done.13.refs_7_.refs_6_), channel_id=1, source_target_pairs={{0,1},{1,0},{2,3},{3,2},{4,5},{5,4},{6,7},{7,6},{8,9},{9,8},{10,11... | collective-permute-start | bytes 4718600 | tf_op jit(solution)/shard_map/ppermute | solution.py:15
  52.2 18.3 %collective-permute-start.15 = (bf16[128,3072]{1,0:T(8,128)(2,1)S(1)}, bf16[128,3072]{1,0:T(8,128)(2,1)S(1)}, u32[]{:S(2)}, u32[]{:S(2)}) collective-permute-start(bf16[128,3072]{1,0:T(8,128)(2,1)S(1)} %get-tuple-element.60), channel_id=1, source_target_pairs={{0,8},{1,3},{2,10},{3,5},{4,12},{5,7},{6,14},{7,1},{8,16},{9,11},{... | collective-permute-start | bytes 2359304 | tf_op jit(solution)/shard_map/ppermute | solution.py:33
  53.5 17.1 %collective-permute-start.16 = (bf16[128,3072]{1,0:T(8,128)(2,1)S(1)}, bf16[128,3072]{1,0:T(8,128)(2,1)S(1)}, u32[]{:S(2)}, u32[]{:S(2)}) collective-permute-start(bf16[128,3072]{1,0:T(8,128)(2,1)S(1)} %get-tuple-element.61), channel_id=1, source_target_pairs={{0,24},{1,7},{2,26},{3,1},{4,28},{5,3},{6,30},{7,5},{8,0},{9,15},{... | collective-permute-start | bytes 2359304 | tf_op jit(solution)/shard_map/ppermute | solution.py:33
  55.0 15.6 %collective-permute-start.17 = (bf16[8,64,256]{2,1,0:T(8,128)(2,1)S(1)}, bf16[8,64,256]{2,1,0:T(8,128)(2,1)S(1)}, u32[]{:S(2)}, u32[]{:S(2)}) collective-permute-start(bf16[8,64,256]{2,1,0:T(8,128)(2,1)S(1)} %get-tuple-element.62), channel_id=1, source_target_pairs={{0,64},{32,96},{64,0},{96,32},{1,65},{33,97},{65,1},{97,33},{2,66}... | collective-permute-start | bytes 786440 | tf_op jit(solution)/shard_map/ppermute | solution.py:286
  57.2 18.8 %collective-permute-start.18 = (bf16[8,64,256]{2,1,0:T(8,128)(2,1)S(1)}, bf16[8,64,256]{2,1,0:T(8,128)(2,1)S(1)}, u32[]{:S(2)}, u32[]{:S(2)}) collective-permute-start(bf16[8,64,256]{2,1,0:T(8,128)(2,1)S(1)} %get-tuple-element.67), channel_id=1, source_target_pairs={{0,32},{32,64},{64,96},{96,0},{1,33},{33,65},{65,97},{97,1},{2,34}... | collective-permute-start | bytes 786440 | tf_op jit(solution)/shard_map/ppermute | solution.py:286
  57.2 18.8 %collective-permute-start.19 = (bf16[8,64,256]{2,1,0:T(8,128)(2,1)S(1)}, bf16[8,64,256]{2,1,0:T(8,128)(2,1)S(1)}, u32[]{:S(2)}, u32[]{:S(2)}) collective-permute-start(bf16[8,64,256]{2,1,0:T(8,128)(2,1)S(1)} %get-tuple-element.69), channel_id=1, source_target_pairs={{0,96},{32,0},{64,32},{96,64},{1,97},{33,1},{65,33},{97,65},{2,98}... | collective-permute-start | bytes 786440 | tf_op jit(solution)/shard_map/ppermute | solution.py:286
  76.6 3.8 %collective-permute-start.20 = (bf16[4,8,64,256]{3,2,1,0:T(8,128)(2,1)S(1)}, bf16[4,8,64,256]{3,2,1,0:T(8,128)(2,1)S(1)}, u32[]{:S(2)}, u32[]{:S(2)}) collective-permute-start(bf16[4,8,64,256]{3,2,1,0:T(8,128)(2,1)S(1)} %shard_map.80.amps), channel_id=1, source_target_pairs={{0,1},{1,0},{2,3},{3,2},{4,5},{5,4},{6,7},{7,6},{8,9},{9,8},{10,11... | collective-permute-start | bytes 3145736 | tf_op jit(solution)/shard_map/ppermute | solution.py:15

commit v5 on v4

--- a/solution.py
+++ b/solution.py
@@ -298,12 +298,12 @@
     held = integrals(
         blocks, [(*pair, (1, 2)) for pair in first] + [(*pair, (0, 1, 2)) for pair in close], *rest, (held,)
     )
-    held, two_first, two_last, parted[2] = lax.optimization_barrier((held, two_first, two_last, parted[2]))
+    held, two_first, two_last, *parted = lax.optimization_barrier((held, two_first, two_last, *parted))
     blocks[3] = [two_first, two_last]
+    amps = order_pairs(*parted, where)
+    held, amps = lax.optimization_barrier((held, amps))
+    amps_other = swap(amps)
     held = integrals(blocks, [(*pair, (3,)) for pair in first + close], *rest, (held,))
-    held, *parted = lax.optimization_barrier((held, *parted))
-    amps = order_pairs(*parted, where)
-    amps_other = swap(amps)
     total = ladder(amps, amps_other, held)
 
     pieces = total.reshape(128, 2, 512)

time: 98.8 us -> 98.4 us (level)
  blocking collectives: 16 us -> 18.2 us
  waiting for transfers between devices: 20.8 us -> 18.6 us
    ppermute x6, waiting for transfers between devices: 2.3 us -> 0.02 us  [swap(): return lax.ppermute(block, 'core', [(0, 1), (1, 0)])]
    all_to_all x1, blocking collectives: 16 us -> 18.2 us  [body(): lax.all_to_all(pieces, ALL, split_axis=0, concat_axis=0, tiled=True)]
  transfers between devices with their start and end apart: 21 -> 21, of which waited for: 6 -> 5; matrix products, arithmetic and copies ran while one was open for 5% -> 5% of each run, Pallas kernels for 24% -> 24%
where the time goes in v5:
time: 98.4 us; the launch traced here: 98.1 us
  starting transfers between devices  29.7 us (30%)
  Pallas kernels  25.5 us (26%)
  waiting for transfers between devices  18.6 us (19%)
  blocking collectives  18.2 us (18%)
  local copies, waits for them, and re-layouts  5.55 us (6%)
    pallas_call x3, Pallas kernels, integrals(): pl.pallas_call(functools.partial(integral_kernel, tuple(steps), tuple(chu...  18.8 us
    all_to_all x1, blocking collectives, body(): lax.all_to_all(pieces, ALL, split_axis=0, concat_axis=0, tiled=True)  18.2 us
    ppermute x7, starting transfers between devices, moved(): return lax.ppermute(block, ('y', 'x', 'core'), pairs)  9.94 us
    ppermute x3, waiting for transfers between devices, around(): return lax.ppermute(block, Z + ('core',), pairs)  9.77 us
    ppermute x7, waiting for transfers between devices, moved(): return lax.ppermute(block, ('y', 'x', 'core'), pairs)  8.77 us
    ppermute x6, starting transfers between devices, swap(): return lax.ppermute(block, 'core', [(0, 1), (1, 0)])  6.96 us
    ppermute x3, starting transfers between devices, around(): return lax.ppermute(block, Z + ('core',), pairs)  4.51 us
    ppermute x3, starting transfers between devices, body(): lax.ppermute(part, Z, [(z, (z + step) % 4) for z in range(4)])  4.26 us
  transfers between devices with their start and end apart: 21, of which 5 were waited for; matrix products, arithmetic and copies ran while one was open for 5% of the time, Pallas kernels for 24%

profile of v5, /device:TPU:1, one launch (start us, length us, event | category | flops | bytes accessed | tf_op | source)
XLA Modules:
  0.0 98.1 jit_solution(676876057580078915)
XLA Ops:
  0.0 1.4 %collective-permute-start.4 = (bf16[4,128,3072]{2,1,0:T(8,128)(2,1)}, bf16[4,128,3072]{2,1,0:T(8,128)(2,1)S(1)}, u32[]{:S(2)}, u32[]{:S(2)}) collective-permute-start(bf16[4,128,3072]{2,1,0:T(8,128)(2,1)} %refs_2_.1), channel_id=1, source_target_pairs={{0,1},{1,0},{2,3},{3,2},{4,5},{5,4},{6,7},{7,6},{8,9},{9,8},{10,11... | collective-permute-start | bytes 9437192 | tf_op jit(solution)/shard_map/ppermute | solution.py:15
  1.4 1.0 reshape.19
  2.4 0.1 collective-permute-start
  2.5 4.1 %collective-permute-start.2 = (bf16[16,3072]{1,0:T(8,128)(2,1)S(1)}, bf16[16,3072]{1,0:T(8,128)(2,1)S(1)}, u32[]{:S(2)}, u32[]{:S(2)}) collective-permute-start(bf16[16,3072]{1,0:T(8,128)(2,1)S(1)} %get-tuple-element.77), channel_id=1, source_target_pairs={{0,65},{1,64},{64,1},{65,0},{2,67},{3,66},{66,3},{67,2},{4,69},{5,... | collective-permute-start | bytes 294920 | tf_op jit(solution)/shard_map/ppermute | solution.py:260
  6.6 0.0 collective-permute-start.1
  6.6 3.1 %collective-permute-start.3 = (s32[4]{0:T(128)}, s32[4]{0:T(128)S(1)}, u32[]{:S(2)}, u32[]{:S(2)}) collective-permute-start(s32[4]{0:T(128)} %param.13), channel_id=1, source_target_pairs={{0,32},{1,97},{32,64},{33,1},{64,96},{65,33},{96,0},{97,65},{2,34}... | collective-permute-start | bytes 56 | tf_op jit(solution)/shard_map/ppermute | solution.py:22
  9.7 3.7 %fusion = (bf16[2,128,3072]{2,1,0:T(8,128)(2,1)}, bf16[2,128,3072]{2,1,0:T(8,128)(2,1)}) fusion(bf16[4,128,3072]{2,1,0:T(8,128)(2,1)} %refs_2_.1), kind=kLoop, calls=%fused_computation.3 | loop fusion | bytes 6291456 | tf_op jit(solution)/shard_map/slice | solution.py:265
  13.5 0.0 collective-permute-done.3
  13.5 0.0 copy-done.5
  13.5 0.1 pad_add_fusion.refs_3_.refs_9_.refs_8_
  13.5 0.0 collective-permute-done.from_core
  13.5 0.0 collective-permute-done.1.from_z
  13.5 0.0 collective-permute-done.2.from_both
  13.6 0.0 collective-permute-done.4.refs_2_.refs_4_.refs_3_
  13.6 1.3 %collective-permute-start.11 = (bf16[2,128,3072]{2,1,0:T(8,128)(2,1)}, bf16[2,128,3072]{2,1,0:T(8,128)(2,1)}, u32[]{:S(2)}, u32[]{:S(2)}) collective-permute-start(bf16[2,128,3072]{2,1,0:T(8,128)(2,1)} %get-tuple-element.46), channel_id=1, source_target_pairs={{0,32},{1,97},{32,64},{33,1},{64,96},{65,33},{96,0},{97,65},{2,34}... | collective-permute-start | bytes 4718600 | tf_op jit(solution)/shard_map/ppermute | solution.py:22
  14.9 0.1 stack.23.where.refs_5_.refs_11_.refs_10_
  15.0 0.7 shard_map.73.refs_0_
  15.7 0.0 copy-start
  15.7 0.0 copy-start.2
  15.7 0.0 copy-start.3
  15.7 0.0 copy-start.4
  15.7 1.4 %collective-permute-start.5 = (bf16[64,3072]{1,0:T(8,128)(2,1)S(1)}, bf16[64,3072]{1,0:T(8,128)(2,1)S(1)}, u32[]{:S(2)}, u32[]{:S(2)}) collective-permute-start(bf16[64,3072]{1,0:T(8,128)(2,1)S(1)} %shard_map.73.refs_0_), channel_id=1, source_target_pairs={{0,2},{1,9},{2,4},{3,11},{4,6},{5,13},{6,0},{7,15},{8,10},{9,17},{... | collective-permute-start | bytes 1179656 | tf_op jit(solution)/shard_map/ppermute | solution.py:33
  17.1 1.5 %collective-permute-start.6 = (bf16[64,3072]{1,0:T(8,128)(2,1)S(1)}, bf16[64,3072]{1,0:T(8,128)(2,1)S(1)}, u32[]{:S(2)}, u32[]{:S(2)}) collective-permute-start(bf16[64,3072]{1,0:T(8,128)(2,1)S(1)} %shard_map.73.refs_0_), channel_id=1, source_target_pairs={{0,6},{1,25},{2,0},{3,27},{4,2},{5,29},{6,4},{7,31},{8,14},{9,1},{... | collective-permute-start | bytes 1179656 | tf_op jit(solution)/shard_map/ppermute | solution.py:33
  18.6 1.6 %collective-permute-start.7 = (bf16[64,3072]{1,0:T(8,128)(2,1)S(1)}, bf16[64,3072]{1,0:T(8,128)(2,1)S(1)}, u32[]{:S(2)}, u32[]{:S(2)}) collective-permute-start(bf16[64,3072]{1,0:T(8,128)(2,1)S(1)} %shard_map.73.refs_0_), channel_id=1, source_target_pairs={{0,4},{1,17},{2,6},{3,19},{4,0},{5,21},{6,2},{7,23},{8,12},{9,25},... | collective-permute-start | bytes 1179656 | tf_op jit(solution)/shard_map/ppermute | solution.py:33
  20.2 0.1 collective-permute-start.8
  20.3 3.8 %collective-permute-done.5.refs_1_ = bf16[64,3072]{1,0:T(8,128)(2,1)S(1)} collective-permute-done((bf16[64,3072]{1,0:T(8,128)(2,1)S(1)}, bf16[64,3072]{1,0:T(8,128)(2,1)S(1)}, u32[]{:S(2)}, u32[]{:S(2)}) %collective-permute-start.5) | collective-permute-done | bytes 393248 | tf_op jit(solution)/shard_map/ppermute | solution.py:33
  24.1 0.0 collective-permute-start.13
  24.1 3.4 %collective-permute-done.6.refs_2_ = bf16[64,3072]{1,0:T(8,128)(2,1)S(1)} collective-permute-done((bf16[64,3072]{1,0:T(8,128)(2,1)S(1)}, bf16[64,3072]{1,0:T(8,128)(2,1)S(1)}, u32[]{:S(2)}, u32[]{:S(2)}) %collective-permute-start.6) | collective-permute-done | bytes 393248 | tf_op jit(solution)/shard_map/ppermute | solution.py:33
  27.6 1.5 %collective-permute-done.7.refs_3_ = bf16[64,3072]{1,0:T(8,128)(2,1)S(1)} collective-permute-done((bf16[64,3072]{1,0:T(8,128)(2,1)S(1)}, bf16[64,3072]{1,0:T(8,128)(2,1)S(1)}, u32[]{:S(2)}, u32[]{:S(2)}) %collective-permute-start.7) | collective-permute-done | bytes 393248 | tf_op jit(solution)/shard_map/ppermute | solution.py:33
  29.1 0.1 shard_map.74.refs_0_
  29.2 0.0 collective-permute-done.8.refs_4_.refs_10_.refs_9_
  29.2 1.3 %collective-permute-start.9 = (bf16[256,3072]{1,0:T(8,128)(2,1)S(1)}, bf16[256,3072]{1,0:T(8,128)(2,1)S(1)}, u32[]{:S(2)}, u32[]{:S(2)}) collective-permute-start(bf16[256,3072]{1,0:T(8,128)(2,1)S(1)} %shard_map.74.refs_0_), channel_id=1, source_target_pairs={{0,8},{1,3},{2,10},{3,5},{4,12},{5,7},{6,14},{7,1},{8,16},{9,11},{... | collective-permute-start | bytes 4718600 | tf_op jit(solution)/shard_map/ppermute | solution.py:33
  30.5 1.5 %collective-permute-start.10 = (bf16[256,3072]{1,0:T(8,128)(2,1)S(1)}, bf16[256,3072]{1,0:T(8,128)(2,1)S(1)}, u32[]{:S(2)}, u32[]{:S(2)}) collective-permute-start(bf16[256,3072]{1,0:T(8,128)(2,1)S(1)} %shard_map.74.refs_0_), channel_id=1, source_target_pairs={{0,24},{1,7},{2,26},{3,1},{4,28},{5,3},{6,30},{7,5},{8,0},{9,15},{... | collective-permute-start | bytes 4718600 | tf_op jit(solution)/shard_map/ppermute | solution.py:33
  32.0 1.6 %collective-permute-done.11.refs_5_.refs_4_ = bf16[2,128,3072]{2,1,0:T(8,128)(2,1)} collective-permute-done((bf16[2,128,3072]{2,1,0:T(8,128)(2,1)}, bf16[2,128,3072]{2,1,0:T(8,128)(2,1)}, u32[]{:S(2)}, u32[]{:S(2)}) %collective-permute-start.11) | collective-permute-done | bytes 1572896 | tf_op jit(solution)/shard_map/ppermute | solution.py:22
  33.5 1.8 %collective-permute-start.12 = (bf16[2,128,3072]{2,1,0:T(8,128)(2,1)}, bf16[2,128,3072]{2,1,0:T(8,128)(2,1)S(1)}, u32[]{:S(2)}, u32[]{:S(2)}) collective-permute-start(bf16[2,128,3072]{2,1,0:T(8,128)(2,1)} %collective-permute-done.11.refs_5_.refs_4_), channel_id=1, source_target_pairs={{0,1},{1,0},{2,3},{3,2},{4,5},{5,4},{6,7},{7,6},{8,9},{9,8},{10,11... | collective-permute-start | bytes 4718600 | tf_op jit(solution)/shard_map/ppermute | solution.py:15
  35.3 4.0 %shard_map.76 = (bf16[8,64,256]{2,1,0:T(8,128)(2,1)S(1)}, bf16[8,64,256]{2,1,0:T(8,128)(2,1)S(1)}, bf16[8,64,256]{2,1,0:T(8,128)(2,1)S(1)}, bf16[8,64,256]{2,1,0:T(8,128)(2,1)S(1)}) custom-call(bf16[64,16,512]{2,1,0:T(8,128)(2,1)S(1)} %copy-done.1, s32[5]{0:T(128)S(1)} %stack.23.where.refs_5_.refs_11_.refs_10_), custom_call_target="tpu_custom_call" | custom-call | flops 1048576 | bytes 1024 | tf_op jit(solution)/shard_map/pallas_call | solution.py:59
  39.3 2.7 %shard_map.75.refs_15_ = bf16[8,256,512]{2,1,0:T(8,128)(2,1)S(1)} custom-call(bf16[256,3072]{1,0:T(8,128)(2,1)S(1)} %shard_map.74.refs_0_, bf16[4,128,3072]{2,1,0:T(8,128)(2,1)S(1)} %copy-done, bf16[4,128,3072]{2,1,0:T(8,128)(2,1)S(1)} %collective-permute-done.4.refs_2_.refs_4_.refs_3_, s32[8]{0:T(128)S(1)} %pad_add_fusion.refs_3_.refs_9_.refs_8_, ...), custom_call_target="tpu_custom_call" | custom-call | flops 1048576 | bytes 1024 | tf_op jit(solution)/shard_map/pallas_call | solution.py:217
  42.0 8.2 %collective-permute-done.13.refs_7_.refs_6_ = bf16[2,128,3072]{2,1,0:T(8,128)(2,1)S(1)} collective-permute-done((bf16[2,128,3072]{2,1,0:T(8,128)(2,1)}, bf16[2,128,3072]{2,1,0:T(8,128)(2,1)S(1)}, u32[]{:S(2)}, u32[]{:S(2)}) %collective-permute-start.13) | collective-permute-done | bytes 1572896 | tf_op jit(solution)/shard_map/ppermute | solution.py:22
  50.3 0.0 collective-permute-done.9.refs_1_.one
  50.3 0.0 collective-permute-done.10.refs_2_.three
  50.3 0.0 collective-permute-done.12.refs_6_.refs_5_
  50.3 1.8 %collective-permute-start.14 = (bf16[2,128,3072]{2,1,0:T(8,128)(2,1)S(1)}, bf16[2,128,3072]{2,1,0:T(8,128)(2,1)S(1)}, u32[]{:S(2)}, u32[]{:S(2)}) collective-permute-start(bf16[2,128,3072]{2,1,0:T(8,128)(2,1)S(1)} %collective-permute-done.13.refs_7_.refs_6_), channel_id=1, source_target_pairs={{0,1},{1,0},{2,3},{3,2},{4,5},{5,4},{6,7},{7,6},{8,9},{9,8},{10,11... | collective-permute-start | bytes 4718600 | tf_op jit(solution)/shard_map/ppermute | solution.py:15
  52.1 0.1 shard_map.78
  52.2 1.3 %collective-permute-start.15 = (bf16[128,3072]{1,0:T(8,128)(2,1)S(1)}, bf16[128,3072]{1,0:T(8,128)(2,1)S(1)}, u32[]{:S(2)}, u32[]{:S(2)}) collective-permute-start(bf16[128,3072]{1,0:T(8,128)(2,1)S(1)} %get-tuple-element.60), channel_id=1, source_target_pairs={{0,8},{1,3},{2,10},{3,5},{4,12},{5,7},{6,14},{7,1},{8,16},{9,11},{... | collective-permute-start | bytes 2359304 | tf_op jit(solution)/shard_map/ppermute | solution.py:33
  53.5 1.5 %collective-permute-start.16 = (bf16[128,3072]{1,0:T(8,128)(2,1)S(1)}, bf16[128,3072]{1,0:T(8,128)(2,1)S(1)}, u32[]{:S(2)}, u32[]{:S(2)}) collective-permute-start(bf16[128,3072]{1,0:T(8,128)(2,1)S(1)} %get-tuple-element.61), channel_id=1, source_target_pairs={{0,24},{1,7},{2,26},{3,1},{4,28},{5,3},{6,30},{7,5},{8,0},{9,15},{... | collective-permute-start | bytes 2359304 | tf_op jit(solution)/shard_map/ppermute | solution.py:33
  55.0 0.6 collective-permute-start.17
  55.5 2.0 %collective-permute-start.18 = (bf16[8,64,256]{2,1,0:T(8,128)(2,1)S(1)}, bf16[8,64,256]{2,1,0:T(8,128)(2,1)S(1)}, u32[]{:S(2)}, u32[]{:S(2)}) collective-permute-start(bf16[8,64,256]{2,1,0:T(8,128)(2,1)S(1)} %get-tuple-element.64), channel_id=1, source_target_pairs={{0,64},{32,96},{64,0},{96,32},{1,65},{33,97},{65,1},{97,33},{2,66}... | collective-permute-start | bytes 786440 | tf_op jit(solution)/shard_map/ppermute | solution.py:286
  57.6 0.0 collective-permute-done.14.refs_8_.refs_7_
  57.6 1.6 %collective-permute-start.19 = (bf16[8,64,256]{2,1,0:T(8,128)(2,1)S(1)}, bf16[8,64,256]{2,1,0:T(8,128)(2,1)S(1)}, u32[]{:S(2)}, u32[]{:S(2)}) collective-permute-start(bf16[8,64,256]{2,1,0:T(8,128)(2,1)S(1)} %get-tuple-element.65), channel_id=1, source_target_pairs={{0,96},{32,0},{64,32},{96,64},{1,97},{33,1},{65,33},{97,65},{2,98}... | collective-permute-start | bytes 786440 | tf_op jit(solution)/shard_map/ppermute | solution.py:286
  59.2 10.7 %shard_map.77.refs_14_ = bf16[16,256,512]{2,1,0:T(8,128)(2,1)S(1)} custom-call(bf16[256,3072]{1,0:T(8,128)(2,1)S(1)} %shard_map.74.refs_0_, bf16[256,3072]{1,0:T(8,128)(2,1)S(1)} %collective-permute-done.9.refs_1_.one, bf16[256,3072]{1,0:T(8,128)(2,1)S(1)} %collective-permute-done.10.refs_2_.three, bf16[4,128,3072]{2,1,0:T(8,128)(2,1)S(1)} %copy-done, ...), custom_call_target="tpu_custom_call" | custom-call | flops 1048576 | bytes 1024 | tf_op jit(solution)/shard_map/pallas_call | solution.py:217
  69.9 0.0 collective-permute-done.17.one
  69.9 0.0 collective-permute-done.18.two
  70.0 0.0 collective-permute-done.19.three
  70.0 0.0 collective-permute-done.15.refs_0_
  70.0 0.0 collective-permute-done.16.refs_1_
  70.0 0.6 shard_map.79.amps
  70.6 1.7 %collective-permute-start.20 = (bf16[4,8,64,256]{3,2,1,0:T(8,128)(2,1)S(1)}, bf16[4,8,64,256]{3,2,1,0:T(8,128)(2,1)S(1)}, u32[]{:S(2)}, u32[]{:S(2)}) collective-permute-start(bf16[4,8,64,256]{3,2,1,0:T(8,128)(2,1)S(1)} %shard_map.79.amps), channel_id=1, source_target_pairs={{0,1},{1,0},{2,3},{3,2},{4,5},{5,4},{6,7},{7,6},{8,9},{9,8},{10,11... | collective-permute-start | bytes 3145736 | tf_op jit(solution)/shard_map/ppermute | solution.py:15
  72.3 5.3 %shard_map.80.held = bf16[16,256,512]{2,1,0:T(8,128)(2,1)S(1)} custom-call(bf16[128,3072]{1,0:T(8,128)(2,1)S(1)} %collective-permute-done.15.refs_0_, bf16[128,3072]{1,0:T(8,128)(2,1)S(1)} %collective-permute-done.16.refs_1_, bf16[4,128,3072]{2,1,0:T(8,128)(2,1)S(1)} %copy-done, bf16[4,128,3072]{2,1,0:T(8,128)(2,1)S(1)} %collective-permute-done.4.refs_2_.refs_4_.refs_3_, ...), custom_call_target="tpu_custom_call" | custom-call | flops 1048576 | bytes 1024 | tf_op jit(solution)/shard_map/pallas_call | solution.py:217
  77.7 0.0 collective-permute-done.20.amps_other
  77.7 1.2 %shard_map.81 = bf16[256,512]{1,0:T(8,128)(2,1)S(1)} custom-call(bf16[4,8,64,256]{3,2,1,0:T(8,128)(2,1)S(1)} %shard_map.79.amps, bf16[4,8,64,256]{3,2,1,0:T(8,128)(2,1)S(1)} %collective-permute-done.20.amps_other, bf16[16,256,512]{2,1,0:T(8,128)(2,1)S(1)} %shard_map.80.held), custom_call_target="tpu_custom_call" | custom-call | flops 1048576 | bytes 1024 | tf_op jit(solution)/shard_map/pallas_call | solution.py:241
  78.9 0.1 reshape.22
  79.0 18.2 %all_to_all.5 = bf16[128,2,512]{2,1,0:T(2,128)(2,1)S(1)} all-to-all(bf16[128,2,512]{2,1,0:T(2,128)(2,1)S(1)} %reshape.22), channel_id=1, replica_groups=mesh['zh'=2,'zl'=2,'y'=4,'x'=4,'core'=2] {'zh','zl','y','x','core'}, dimensions={0} | all-to-all | bytes 524288 | tf_op jit(solution)/shard_map/all_to_all | solution.py:310
  97.3 0.2 reduce
  97.5 0.6 copy.8
  (9 shorter events, 0.0 us)
Async XLA Ops:
  0.0 13.6 %collective-permute-start.4 = (bf16[4,128,3072]{2,1,0:T(8,128)(2,1)}, bf16[4,128,3072]{2,1,0:T(8,128)(2,1)S(1)}, u32[]{:S(2)}, u32[]{:S(2)}) collective-permute-start(bf16[4,128,3072]{2,1,0:T(8,128)(2,1)} %refs_2_.1), channel_id=1, source_target_pairs={{0,1},{1,0},{2,3},{3,2},{4,5},{5,4},{6,7},{7,6},{8,9},{9,8},{10,11... | collective-permute-start | bytes 9437192 | tf_op jit(solution)/shard_map/ppermute | solution.py:15
  2.4 11.1 %collective-permute-start = (bf16[16,3072]{1,0:T(8,128)(2,1)S(1)}, bf16[16,3072]{1,0:T(8,128)(2,1)S(1)}, u32[]{:S(2)}, u32[]{:S(2)}) collective-permute-start(bf16[16,3072]{1,0:T(8,128)(2,1)S(1)} %get-tuple-element.77), channel_id=1, source_target_pairs={{0,1},{1,0},{2,3},{3,2},{4,5},{5,4},{6,7},{7,6},{8,9},{9,8},{10,11... | collective-permute-start | bytes 294920 | tf_op jit(solution)/shard_map/ppermute | solution.py:15
  2.5 11.0 %collective-permute-start.2 = (bf16[16,3072]{1,0:T(8,128)(2,1)S(1)}, bf16[16,3072]{1,0:T(8,128)(2,1)S(1)}, u32[]{:S(2)}, u32[]{:S(2)}) collective-permute-start(bf16[16,3072]{1,0:T(8,128)(2,1)S(1)} %get-tuple-element.77), channel_id=1, source_target_pairs={{0,65},{1,64},{64,1},{65,0},{2,67},{3,66},{66,3},{67,2},{4,69},{5,... | collective-permute-start | bytes 294920 | tf_op jit(solution)/shard_map/ppermute | solution.py:260
  6.6 6.9 %copy-start.5 = (s32[4]{0:T(128)S(1)}, s32[4]{0:T(128)}, u32[]{:S(2)}) copy-start(s32[4]{0:T(128)} %param.13) | copy-start | bytes 52
  6.6 7.0 %collective-permute-start.1 = (bf16[16,3072]{1,0:T(8,128)(2,1)S(1)}, bf16[16,3072]{1,0:T(8,128)(2,1)S(1)}, u32[]{:S(2)}, u32[]{:S(2)}) collective-permute-start(bf16[16,3072]{1,0:T(8,128)(2,1)S(1)} %get-tuple-element.40.mine), channel_id=1, source_target_pairs={{0,64},{64,0},{1,65},{65,1},{2,66},{66,2},{3,67},{67,3},{4,68},{68... | collective-permute-start | bytes 294920 | tf_op jit(solution)/shard_map/ppermute | solution.py:259
  6.6 6.9 %collective-permute-start.3 = (s32[4]{0:T(128)}, s32[4]{0:T(128)S(1)}, u32[]{:S(2)}, u32[]{:S(2)}) collective-permute-start(s32[4]{0:T(128)} %param.13), channel_id=1, source_target_pairs={{0,32},{1,97},{32,64},{33,1},{64,96},{65,33},{96,0},{97,65},{2,34}... | collective-permute-start | bytes 56 | tf_op jit(solution)/shard_map/ppermute | solution.py:22
  13.6 19.9 %collective-permute-start.11 = (bf16[2,128,3072]{2,1,0:T(8,128)(2,1)}, bf16[2,128,3072]{2,1,0:T(8,128)(2,1)}, u32[]{:S(2)}, u32[]{:S(2)}) collective-permute-start(bf16[2,128,3072]{2,1,0:T(8,128)(2,1)} %get-tuple-element.46), channel_id=1, source_target_pairs={{0,32},{1,97},{32,64},{33,1},{64,96},{65,33},{96,0},{97,65},{2,34}... | collective-permute-start | bytes 4718600 | tf_op jit(solution)/shard_map/ppermute | solution.py:22
  15.0 20.3 %copy-start.1 = (bf16[64,16,512]{2,1,0:T(8,128)(2,1)S(1)}, bf16[64,16,512]{2,1,0:T(8,128)(2,1)}, u32[]{:S(2)}) copy-start(bf16[64,16,512]{2,1,0:T(8,128)(2,1)} %amps) | copy-start | bytes 3145732
  15.7 23.6 %copy-start = (bf16[4,128,3072]{2,1,0:T(8,128)(2,1)S(1)}, bf16[4,128,3072]{2,1,0:T(8,128)(2,1)}, u32[]{:S(2)}) copy-start(bf16[4,128,3072]{2,1,0:T(8,128)(2,1)} %refs_2_.1) | copy-start | bytes 9437188
  15.7 23.6 %copy-start.2 = (s32[512]{0:T(512)S(1)}, s32[512]{0:T(512)}, u32[]{:S(2)}) copy-start(s32[512]{0:T(512)} %param.12) | copy-start | bytes 6148
  15.7 23.6 %copy-start.3 = (s32[8]{0:T(128)S(1)}, s32[8]{0:T(128)}, u32[]{:S(2)}) copy-start(s32[8]{0:T(128)} %refs_11_.1) | copy-start | bytes 100
  15.7 23.6 %copy-start.4 = (s32[128]{0:T(128)S(1)}, s32[128]{0:T(128)}, u32[]{:S(2)}) copy-start(s32[128]{0:T(128)} %param.11) | copy-start | bytes 1540
  15.7 8.4 %collective-permute-start.5 = (bf16[64,3072]{1,0:T(8,128)(2,1)S(1)}, bf16[64,3072]{1,0:T(8,128)(2,1)S(1)}, u32[]{:S(2)}, u32[]{:S(2)}) collective-permute-start(bf16[64,3072]{1,0:T(8,128)(2,1)S(1)} %shard_map.73.refs_0_), channel_id=1, source_target_pairs={{0,2},{1,9},{2,4},{3,11},{4,6},{5,13},{6,0},{7,15},{8,10},{9,17},{... | collective-permute-start | bytes 1179656 | tf_op jit(solution)/shard_map/ppermute | solution.py:33
  17.1 10.5 %collective-permute-start.6 = (bf16[64,3072]{1,0:T(8,128)(2,1)S(1)}, bf16[64,3072]{1,0:T(8,128)(2,1)S(1)}, u32[]{:S(2)}, u32[]{:S(2)}) collective-permute-start(bf16[64,3072]{1,0:T(8,128)(2,1)S(1)} %shard_map.73.refs_0_), channel_id=1, source_target_pairs={{0,6},{1,25},{2,0},{3,27},{4,2},{5,29},{6,4},{7,31},{8,14},{9,1},{... | collective-permute-start | bytes 1179656 | tf_op jit(solution)/shard_map/ppermute | solution.py:33
  18.6 10.5 %collective-permute-start.7 = (bf16[64,3072]{1,0:T(8,128)(2,1)S(1)}, bf16[64,3072]{1,0:T(8,128)(2,1)S(1)}, u32[]{:S(2)}, u32[]{:S(2)}) collective-permute-start(bf16[64,3072]{1,0:T(8,128)(2,1)S(1)} %shard_map.73.refs_0_), channel_id=1, source_target_pairs={{0,4},{1,17},{2,6},{3,19},{4,0},{5,21},{6,2},{7,23},{8,12},{9,25},... | collective-permute-start | bytes 1179656 | tf_op jit(solution)/shard_map/ppermute | solution.py:33
  20.2 9.0 %collective-permute-start.8 = (s32[8]{0:T(128)S(1)}, s32[8]{0:T(128)S(1)}, u32[]{:S(2)}, u32[]{:S(2)}) collective-permute-start(s32[8]{0:T(128)S(1)} %pad_add_fusion.refs_3_.refs_9_.refs_8_), channel_id=1, source_target_pairs={{0,1},{1,0},{2,3},{3,2},{4,5},{5,4},{6,7},{7,6},{8,9},{9,8},{10,11... | collective-permute-start | bytes 104 | tf_op jit(solution)/shard_map/ppermute | solution.py:15
  24.1 26.2 %collective-permute-start.13 = (bf16[2,128,3072]{2,1,0:T(8,128)(2,1)}, bf16[2,128,3072]{2,1,0:T(8,128)(2,1)S(1)}, u32[]{:S(2)}, u32[]{:S(2)}) collective-permute-start(bf16[2,128,3072]{2,1,0:T(8,128)(2,1)} %get-tuple-element.47), channel_id=1, source_target_pairs={{0,32},{1,97},{32,64},{33,1},{64,96},{65,33},{96,0},{97,65},{2,34}... | collective-permute-start | bytes 4718600 | tf_op jit(solution)/shard_map/ppermute | solution.py:22
  29.2 21.0 %collective-permute-start.9 = (bf16[256,3072]{1,0:T(8,128)(2,1)S(1)}, bf16[256,3072]{1,0:T(8,128)(2,1)S(1)}, u32[]{:S(2)}, u32[]{:S(2)}) collective-permute-start(bf16[256,3072]{1,0:T(8,128)(2,1)S(1)} %shard_map.74.refs_0_), channel_id=1, source_target_pairs={{0,8},{1,3},{2,10},{3,5},{4,12},{5,7},{6,14},{7,1},{8,16},{9,11},{... | collective-permute-start | bytes 4718600 | tf_op jit(solution)/shard_map/ppermute | solution.py:33
  30.5 19.8 %collective-permute-start.10 = (bf16[256,3072]{1,0:T(8,128)(2,1)S(1)}, bf16[256,3072]{1,0:T(8,128)(2,1)S(1)}, u32[]{:S(2)}, u32[]{:S(2)}) collective-permute-start(bf16[256,3072]{1,0:T(8,128)(2,1)S(1)} %shard_map.74.refs_0_), channel_id=1, source_target_pairs={{0,24},{1,7},{2,26},{3,1},{4,28},{5,3},{6,30},{7,5},{8,0},{9,15},{... | collective-permute-start | bytes 4718600 | tf_op jit(solution)/shard_map/ppermute | solution.py:33
  33.5 16.8 %collective-permute-start.12 = (bf16[2,128,3072]{2,1,0:T(8,128)(2,1)}, bf16[2,128,3072]{2,1,0:T(8,128)(2,1)S(1)}, u32[]{:S(2)}, u32[]{:S(2)}) collective-permute-start(bf16[2,128,3072]{2,1,0:T(8,128)(2,1)} %collective-permute-done.11.refs_5_.refs_4_), channel_id=1, source_target_pairs={{0,1},{1,0},{2,3},{3,2},{4,5},{5,4},{6,7},{7,6},{8,9},{9,8},{10,11... | collective-permute-start | bytes 4718600 | tf_op jit(solution)/shard_map/ppermute | solution.py:15
  50.3 7.3 %collective-permute-start.14 = (bf16[2,128,3072]{2,1,0:T(8,128)(2,1)S(1)}, bf16[2,128,3072]{2,1,0:T(8,128)(2,1)S(1)}, u32[]{:S(2)}, u32[]{:S(2)}) collective-permute-start(bf16[2,128,3072]{2,1,0:T(8,128)(2,1)S(1)} %collective-permute-done.13.refs_7_.refs_6_), channel_id=1, source_target_pairs={{0,1},{1,0},{2,3},{3,2},{4,5},{5,4},{6,7},{7,6},{8,9},{9,8},{10,11... | collective-permute-start | bytes 4718600 | tf_op jit(solution)/shard_map/ppermute | solution.py:15
  52.2 17.7 %collective-permute-start.15 = (bf16[128,3072]{1,0:T(8,128)(2,1)S(1)}, bf16[128,3072]{1,0:T(8,128)(2,1)S(1)}, u32[]{:S(2)}, u32[]{:S(2)}) collective-permute-start(bf16[128,3072]{1,0:T(8,128)(2,1)S(1)} %get-tuple-element.60), channel_id=1, source_target_pairs={{0,8},{1,3},{2,10},{3,5},{4,12},{5,7},{6,14},{7,1},{8,16},{9,11},{... | collective-permute-start | bytes 2359304 | tf_op jit(solution)/shard_map/ppermute | solution.py:33
  53.5 16.5 %collective-permute-start.16 = (bf16[128,3072]{1,0:T(8,128)(2,1)S(1)}, bf16[128,3072]{1,0:T(8,128)(2,1)S(1)}, u32[]{:S(2)}, u32[]{:S(2)}) collective-permute-start(bf16[128,3072]{1,0:T(8,128)(2,1)S(1)} %get-tuple-element.61), channel_id=1, source_target_pairs={{0,24},{1,7},{2,26},{3,1},{4,28},{5,3},{6,30},{7,5},{8,0},{9,15},{... | collective-permute-start | bytes 2359304 | tf_op jit(solution)/shard_map/ppermute | solution.py:33
  55.0 15.0 %collective-permute-start.17 = (bf16[8,64,256]{2,1,0:T(8,128)(2,1)S(1)}, bf16[8,64,256]{2,1,0:T(8,128)(2,1)S(1)}, u32[]{:S(2)}, u32[]{:S(2)}) collective-permute-start(bf16[8,64,256]{2,1,0:T(8,128)(2,1)S(1)} %get-tuple-element.63), channel_id=1, source_target_pairs={{0,32},{32,64},{64,96},{96,0},{1,33},{33,65},{65,97},{97,1},{2,34}... | collective-permute-start | bytes 786440 | tf_op jit(solution)/shard_map/ppermute | solution.py:286
  55.5 14.4 %collective-permute-start.18 = (bf16[8,64,256]{2,1,0:T(8,128)(2,1)S(1)}, bf16[8,64,256]{2,1,0:T(8,128)(2,1)S(1)}, u32[]{:S(2)}, u32[]{:S(2)}) collective-permute-start(bf16[8,64,256]{2,1,0:T(8,128)(2,1)S(1)} %get-tuple-element.64), channel_id=1, source_target_pairs={{0,64},{32,96},{64,0},{96,32},{1,65},{33,97},{65,1},{97,33},{2,66}... | collective-permute-start | bytes 786440 | tf_op jit(solution)/shard_map/ppermute | solution.py:286
  57.6 12.4 %collective-permute-start.19 = (bf16[8,64,256]{2,1,0:T(8,128)(2,1)S(1)}, bf16[8,64,256]{2,1,0:T(8,128)(2,1)S(1)}, u32[]{:S(2)}, u32[]{:S(2)}) collective-permute-start(bf16[8,64,256]{2,1,0:T(8,128)(2,1)S(1)} %get-tuple-element.65), channel_id=1, source_target_pairs={{0,96},{32,0},{64,32},{96,64},{1,97},{33,1},{65,33},{97,65},{2,98}... | collective-permute-start | bytes 786440 | tf_op jit(solution)/shard_map/ppermute | solution.py:286
  70.6 7.1 %collective-permute-start.20 = (bf16[4,8,64,256]{3,2,1,0:T(8,128)(2,1)S(1)}, bf16[4,8,64,256]{3,2,1,0:T(8,128)(2,1)S(1)}, u32[]{:S(2)}, u32[]{:S(2)}) collective-permute-start(bf16[4,8,64,256]{3,2,1,0:T(8,128)(2,1)S(1)} %shard_map.79.amps), channel_id=1, source_target_pairs={{0,1},{1,0},{2,3},{3,2},{4,5},{5,4},{6,7},{7,6},{8,9},{9,8},{10,11... | collective-permute-start | bytes 3145736 | tf_op jit(solution)/shard_map/ppermute | solution.py:15

commit v6 on v5

--- a/solution.py
+++ b/solution.py
@@ -277,8 +277,9 @@
     rest = (where, irrep_a, irrep_b.reshape(1, 128), irrep_c.reshape(1, 512))
     first = [((bd_factor, at), (near_irreps, at)) for at in (0, 2)]
     first += [((bd_core, at), (other_far, at)) for at in (0, 2)]
+    far_first = swap(near_first)
+    first += [((near_first, 0), (near_irreps, 4))]
     held = integrals([[rows]], [(*pair, (0,)) for pair in first], *rest)
-    far_first = swap(near_first)
     one, three, far_first, near_last, held, *parted = lax.optimization_barrier(
         (one, three, far_first, near_last, held, *parted)
     )
@@ -292,7 +293,7 @@
     (two_last,) = along(three_half, "yx", (3,))
 
     blocks = [[rows], [one], [three], [two_first, two_last]]
-    close = [((near_first, 0), (near_irreps, 4)), ((far_first, 0), (other_far, 4))]
+    close = [((far_first, 0), (other_far, 4))]
     far_last = swap(near_last)
     close += [((near_last, 0), (near_irreps, 6)), ((far_last, 0), (other_far, 6))]
     held = integrals(

time: 98.4 us -> 98.4 us (level)
  waiting for transfers between devices: 18.6 us -> 17.4 us
    ppermute x3, waiting for transfers between devices: 9.77 us -> 8.49 us  [around(): return lax.ppermute(block, Z + ('core',), pairs)]
  transfers between devices with their start and end apart: 21 -> 21, of which waited for: 5 -> 6; matrix products, arithmetic and copies ran while one was open for 5% -> 5% of each run, Pallas kernels for 24% -> 25%
where the time goes in v6:
time: 98.4 us; the launch traced here: 98.1 us
  starting transfers between devices  29.9 us (30%)
  Pallas kernels  26.4 us (27%)
  blocking collectives  18.4 us (19%)
  waiting for transfers between devices  17.4 us (18%)
  local copies, waits for them, and re-layouts  5.55 us (6%)
    pallas_call x3, Pallas kernels, integrals(): pl.pallas_call(functools.partial(integral_kernel, tuple(steps), tuple(chu...  19.7 us
    all_to_all x1, blocking collectives, body(): lax.all_to_all(pieces, ALL, split_axis=0, concat_axis=0, tiled=True)  18.4 us
    ppermute x7, starting transfers between devices, moved(): return lax.ppermute(block, ('y', 'x', 'core'), pairs)  10 us
    ppermute x7, waiting for transfers between devices, moved(): return lax.ppermute(block, ('y', 'x', 'core'), pairs)  8.77 us
    ppermute x3, waiting for transfers between devices, around(): return lax.ppermute(block, Z + ('core',), pairs)  8.49 us
    ppermute x6, starting transfers between devices, swap(): return lax.ppermute(block, 'core', [(0, 1), (1, 0)])  7.11 us
    ppermute x3, starting transfers between devices, around(): return lax.ppermute(block, Z + ('core',), pairs)  4.51 us
    ppermute x3, starting transfers between devices, body(): lax.ppermute(part, Z, [(z, (z + step) % 4) for z in range(4)])  4.2 us
  transfers between devices with their start and end apart: 21, of which 6 were waited for; matrix products, arithmetic and copies ran while one was open for 5% of the time, Pallas kernels for 25%

profile of v6, /device:TPU:1, one launch (start us, length us, event | category | flops | bytes accessed | tf_op | source)
XLA Modules:
  0.0 98.1 jit_solution(11511974202869375730)
XLA Ops:
  0.0 1.4 %collective-permute-start.4 = (bf16[4,128,3072]{2,1,0:T(8,128)(2,1)}, bf16[4,128,3072]{2,1,0:T(8,128)(2,1)S(1)}, u32[]{:S(2)}, u32[]{:S(2)}) collective-permute-start(bf16[4,128,3072]{2,1,0:T(8,128)(2,1)} %refs_2_.1), channel_id=1, source_target_pairs={{0,1},{1,0},{2,3},{3,2},{4,5},{5,4},{6,7},{7,6},{8,9},{9,8},{10,11... | collective-permute-start | bytes 9437192 | tf_op jit(solution)/shard_map/ppermute | solution.py:15
  1.4 1.0 reshape.19
  2.4 0.1 collective-permute-start
  2.5 4.1 %collective-permute-start.2 = (bf16[16,3072]{1,0:T(8,128)(2,1)S(1)}, bf16[16,3072]{1,0:T(8,128)(2,1)S(1)}, u32[]{:S(2)}, u32[]{:S(2)}) collective-permute-start(bf16[16,3072]{1,0:T(8,128)(2,1)S(1)} %get-tuple-element.77), channel_id=1, source_target_pairs={{0,65},{1,64},{64,1},{65,0},{2,67},{3,66},{66,3},{67,2},{4,69},{5,... | collective-permute-start | bytes 294920 | tf_op jit(solution)/shard_map/ppermute | solution.py:260
  6.6 0.0 collective-permute-start.1
  6.6 3.1 %collective-permute-start.3 = (s32[4]{0:T(128)}, s32[4]{0:T(128)S(1)}, u32[]{:S(2)}, u32[]{:S(2)}) collective-permute-start(s32[4]{0:T(128)} %param.13), channel_id=1, source_target_pairs={{0,32},{1,97},{32,64},{33,1},{64,96},{65,33},{96,0},{97,65},{2,34}... | collective-permute-start | bytes 56 | tf_op jit(solution)/shard_map/ppermute | solution.py:22
  9.7 3.7 %fusion = (bf16[2,128,3072]{2,1,0:T(8,128)(2,1)}, bf16[2,128,3072]{2,1,0:T(8,128)(2,1)}) fusion(bf16[4,128,3072]{2,1,0:T(8,128)(2,1)} %refs_2_.1), kind=kLoop, calls=%fused_computation.3 | loop fusion | bytes 6291456 | tf_op jit(solution)/shard_map/slice | solution.py:265
  13.5 0.0 collective-permute-done.3
  13.5 0.0 copy-done.5
  13.5 0.1 pad_add_fusion.refs_4_.refs_9_.refs_8_
  13.5 0.0 collective-permute-done.from_core
  13.5 0.0 collective-permute-done.1.from_z
  13.5 0.0 collective-permute-done.2.from_both
  13.6 0.0 collective-permute-done.4.refs_2_.refs_4_.refs_3_
  13.6 1.3 %collective-permute-start.11 = (bf16[2,128,3072]{2,1,0:T(8,128)(2,1)}, bf16[2,128,3072]{2,1,0:T(8,128)(2,1)}, u32[]{:S(2)}, u32[]{:S(2)}) collective-permute-start(bf16[2,128,3072]{2,1,0:T(8,128)(2,1)} %get-tuple-element.46), channel_id=1, source_target_pairs={{0,32},{1,97},{32,64},{33,1},{64,96},{65,33},{96,0},{97,65},{2,34}... | collective-permute-start | bytes 4718600 | tf_op jit(solution)/shard_map/ppermute | solution.py:22
  14.9 0.1 stack.23.where.refs_6_.refs_11_.refs_10_
  15.0 0.7 shard_map.73.refs_0_
  15.7 0.0 copy-start
  15.7 0.0 copy-start.2
  15.7 0.0 copy-start.3
  15.7 0.0 copy-start.4
  15.7 1.4 %collective-permute-start.5 = (bf16[64,3072]{1,0:T(8,128)(2,1)S(1)}, bf16[64,3072]{1,0:T(8,128)(2,1)S(1)}, u32[]{:S(2)}, u32[]{:S(2)}) collective-permute-start(bf16[64,3072]{1,0:T(8,128)(2,1)S(1)} %shard_map.73.refs_0_), channel_id=1, source_target_pairs={{0,2},{1,9},{2,4},{3,11},{4,6},{5,13},{6,0},{7,15},{8,10},{9,17},{... | collective-permute-start | bytes 1179656 | tf_op jit(solution)/shard_map/ppermute | solution.py:33
  17.1 1.5 %collective-permute-start.6 = (bf16[64,3072]{1,0:T(8,128)(2,1)S(1)}, bf16[64,3072]{1,0:T(8,128)(2,1)S(1)}, u32[]{:S(2)}, u32[]{:S(2)}) collective-permute-start(bf16[64,3072]{1,0:T(8,128)(2,1)S(1)} %shard_map.73.refs_0_), channel_id=1, source_target_pairs={{0,6},{1,25},{2,0},{3,27},{4,2},{5,29},{6,4},{7,31},{8,14},{9,1},{... | collective-permute-start | bytes 1179656 | tf_op jit(solution)/shard_map/ppermute | solution.py:33
  18.6 1.6 %collective-permute-start.7 = (bf16[64,3072]{1,0:T(8,128)(2,1)S(1)}, bf16[64,3072]{1,0:T(8,128)(2,1)S(1)}, u32[]{:S(2)}, u32[]{:S(2)}) collective-permute-start(bf16[64,3072]{1,0:T(8,128)(2,1)S(1)} %shard_map.73.refs_0_), channel_id=1, source_target_pairs={{0,4},{1,17},{2,6},{3,19},{4,0},{5,21},{6,2},{7,23},{8,12},{9,25},... | collective-permute-start | bytes 1179656 | tf_op jit(solution)/shard_map/ppermute | solution.py:33
  20.2 0.1 collective-permute-start.8
  20.3 3.8 %collective-permute-done.5.refs_1_ = bf16[64,3072]{1,0:T(8,128)(2,1)S(1)} collective-permute-done((bf16[64,3072]{1,0:T(8,128)(2,1)S(1)}, bf16[64,3072]{1,0:T(8,128)(2,1)S(1)}, u32[]{:S(2)}, u32[]{:S(2)}) %collective-permute-start.5) | collective-permute-done | bytes 393248 | tf_op jit(solution)/shard_map/ppermute | solution.py:33
  24.1 0.0 collective-permute-start.13
  24.1 3.4 %collective-permute-done.6.refs_2_ = bf16[64,3072]{1,0:T(8,128)(2,1)S(1)} collective-permute-done((bf16[64,3072]{1,0:T(8,128)(2,1)S(1)}, bf16[64,3072]{1,0:T(8,128)(2,1)S(1)}, u32[]{:S(2)}, u32[]{:S(2)}) %collective-permute-start.6) | collective-permute-done | bytes 393248 | tf_op jit(solution)/shard_map/ppermute | solution.py:33
  27.6 1.5 %collective-permute-done.7.refs_3_ = bf16[64,3072]{1,0:T(8,128)(2,1)S(1)} collective-permute-done((bf16[64,3072]{1,0:T(8,128)(2,1)S(1)}, bf16[64,3072]{1,0:T(8,128)(2,1)S(1)}, u32[]{:S(2)}, u32[]{:S(2)}) %collective-permute-start.7) | collective-permute-done | bytes 393248 | tf_op jit(solution)/shard_map/ppermute | solution.py:33
  29.1 0.1 shard_map.74.refs_0_
  29.2 0.0 collective-permute-done.8.refs_5_.refs_10_.refs_9_
  29.2 1.3 %collective-permute-start.9 = (bf16[256,3072]{1,0:T(8,128)(2,1)S(1)}, bf16[256,3072]{1,0:T(8,128)(2,1)S(1)}, u32[]{:S(2)}, u32[]{:S(2)}) collective-permute-start(bf16[256,3072]{1,0:T(8,128)(2,1)S(1)} %shard_map.74.refs_0_), channel_id=1, source_target_pairs={{0,8},{1,3},{2,10},{3,5},{4,12},{5,7},{6,14},{7,1},{8,16},{9,11},{... | collective-permute-start | bytes 4718600 | tf_op jit(solution)/shard_map/ppermute | solution.py:33
  30.5 1.5 %collective-permute-start.10 = (bf16[256,3072]{1,0:T(8,128)(2,1)S(1)}, bf16[256,3072]{1,0:T(8,128)(2,1)S(1)}, u32[]{:S(2)}, u32[]{:S(2)}) collective-permute-start(bf16[256,3072]{1,0:T(8,128)(2,1)S(1)} %shard_map.74.refs_0_), channel_id=1, source_target_pairs={{0,24},{1,7},{2,26},{3,1},{4,28},{5,3},{6,30},{7,5},{8,0},{9,15},{... | collective-permute-start | bytes 4718600 | tf_op jit(solution)/shard_map/ppermute | solution.py:33
  32.0 1.6 %collective-permute-done.11.refs_3_.refs_5_.refs_4_ = bf16[2,128,3072]{2,1,0:T(8,128)(2,1)} collective-permute-done((bf16[2,128,3072]{2,1,0:T(8,128)(2,1)}, bf16[2,128,3072]{2,1,0:T(8,128)(2,1)}, u32[]{:S(2)}, u32[]{:S(2)}) %collective-permute-start.11) | collective-permute-done | bytes 1572896 | tf_op jit(solution)/shard_map/ppermute | solution.py:22
  33.5 1.8 %collective-permute-start.12 = (bf16[2,128,3072]{2,1,0:T(8,128)(2,1)}, bf16[2,128,3072]{2,1,0:T(8,128)(2,1)S(1)}, u32[]{:S(2)}, u32[]{:S(2)}) collective-permute-start(bf16[2,128,3072]{2,1,0:T(8,128)(2,1)} %collective-permute-done.11.refs_3_.refs_5_.refs_4_), channel_id=1, source_target_pairs={{0,1},{1,0},{2,3},{3,2},{4,5},{5,4},{6,7},{7,6},{8,9},{9,8},{10,11... | collective-permute-start | bytes 4718600 | tf_op jit(solution)/shard_map/ppermute | solution.py:15
  35.3 4.0 %shard_map.76 = (bf16[8,64,256]{2,1,0:T(8,128)(2,1)S(1)}, bf16[8,64,256]{2,1,0:T(8,128)(2,1)S(1)}, bf16[8,64,256]{2,1,0:T(8,128)(2,1)S(1)}, bf16[8,64,256]{2,1,0:T(8,128)(2,1)S(1)}) custom-call(bf16[64,16,512]{2,1,0:T(8,128)(2,1)S(1)} %copy-done.1, s32[5]{0:T(128)S(1)} %stack.23.where.refs_6_.refs_11_.refs_10_), custom_call_target="tpu_custom_call" | custom-call | flops 1048576 | bytes 1024 | tf_op jit(solution)/shard_map/pallas_call | solution.py:59
  39.3 4.0 %shard_map.75.refs_15_ = bf16[10,256,512]{2,1,0:T(8,128)(2,1)S(1)} custom-call(bf16[256,3072]{1,0:T(8,128)(2,1)S(1)} %shard_map.74.refs_0_, bf16[4,128,3072]{2,1,0:T(8,128)(2,1)S(1)} %copy-done, bf16[4,128,3072]{2,1,0:T(8,128)(2,1)S(1)} %collective-permute-done.4.refs_2_.refs_4_.refs_3_, ...), custom_call_target="tpu_custom_call" | custom-call | flops 1048576 | bytes 1024 | tf_op jit(solution)/shard_map/pallas_call | solution.py:217
  43.3 6.9 %collective-permute-done.13.refs_7_.refs_6_ = bf16[2,128,3072]{2,1,0:T(8,128)(2,1)S(1)} collective-permute-done((bf16[2,128,3072]{2,1,0:T(8,128)(2,1)}, bf16[2,128,3072]{2,1,0:T(8,128)(2,1)S(1)}, u32[]{:S(2)}, u32[]{:S(2)}) %collective-permute-start.13) | collective-permute-done | bytes 1572896 | tf_op jit(solution)/shard_map/ppermute | solution.py:22
  50.3 0.0 collective-permute-done.9.refs_1_.one
  50.3 0.0 collective-permute-done.10.refs_2_.three
  50.3 0.0 collective-permute-done.12.refs_6_.refs_5_
  50.3 1.8 %collective-permute-start.14 = (bf16[2,128,3072]{2,1,0:T(8,128)(2,1)S(1)}, bf16[2,128,3072]{2,1,0:T(8,128)(2,1)S(1)}, u32[]{:S(2)}, u32[]{:S(2)}) collective-permute-start(bf16[2,128,3072]{2,1,0:T(8,128)(2,1)S(1)} %collective-permute-done.13.refs_7_.refs_6_), channel_id=1, source_target_pairs={{0,1},{1,0},{2,3},{3,2},{4,5},{5,4},{6,7},{7,6},{8,9},{9,8},{10,11... | collective-permute-start | bytes 4718600 | tf_op jit(solution)/shard_map/ppermute | solution.py:15
  52.1 0.1 shard_map.78
  52.2 1.3 %collective-permute-start.15 = (bf16[128,3072]{1,0:T(8,128)(2,1)S(1)}, bf16[128,3072]{1,0:T(8,128)(2,1)S(1)}, u32[]{:S(2)}, u32[]{:S(2)}) collective-permute-start(bf16[128,3072]{1,0:T(8,128)(2,1)S(1)} %get-tuple-element.60), channel_id=1, source_target_pairs={{0,8},{1,3},{2,10},{3,5},{4,12},{5,7},{6,14},{7,1},{8,16},{9,11},{... | collective-permute-start | bytes 2359304 | tf_op jit(solution)/shard_map/ppermute | solution.py:33
  53.5 1.5 %collective-permute-start.16 = (bf16[128,3072]{1,0:T(8,128)(2,1)S(1)}, bf16[128,3072]{1,0:T(8,128)(2,1)S(1)}, u32[]{:S(2)}, u32[]{:S(2)}) collective-permute-start(bf16[128,3072]{1,0:T(8,128)(2,1)S(1)} %get-tuple-element.61), channel_id=1, source_target_pairs={{0,24},{1,7},{2,26},{3,1},{4,28},{5,3},{6,30},{7,5},{8,0},{9,15},{... | collective-permute-start | bytes 2359304 | tf_op jit(solution)/shard_map/ppermute | solution.py:33
  55.0 0.5 collective-permute-start.17
  55.5 2.0 %collective-permute-start.18 = (bf16[8,64,256]{2,1,0:T(8,128)(2,1)S(1)}, bf16[8,64,256]{2,1,0:T(8,128)(2,1)S(1)}, u32[]{:S(2)}, u32[]{:S(2)}) collective-permute-start(bf16[8,64,256]{2,1,0:T(8,128)(2,1)S(1)} %get-tuple-element.64), channel_id=1, source_target_pairs={{0,64},{32,96},{64,0},{96,32},{1,65},{33,97},{65,1},{97,33},{2,66}... | collective-permute-start | bytes 786440 | tf_op jit(solution)/shard_map/ppermute | solution.py:287
  57.6 0.0 collective-permute-done.14.refs_8_.refs_7_
  57.6 1.6 %collective-permute-start.19 = (bf16[8,64,256]{2,1,0:T(8,128)(2,1)S(1)}, bf16[8,64,256]{2,1,0:T(8,128)(2,1)S(1)}, u32[]{:S(2)}, u32[]{:S(2)}) collective-permute-start(bf16[8,64,256]{2,1,0:T(8,128)(2,1)S(1)} %get-tuple-element.65), channel_id=1, source_target_pairs={{0,96},{32,0},{64,32},{96,64},{1,97},{33,1},{65,33},{97,65},{2,98}... | collective-permute-start | bytes 786440 | tf_op jit(solution)/shard_map/ppermute | solution.py:287
  59.2 10.3 %shard_map.77.refs_14_ = bf16[16,256,512]{2,1,0:T(8,128)(2,1)S(1)} custom-call(bf16[256,3072]{1,0:T(8,128)(2,1)S(1)} %shard_map.74.refs_0_, bf16[256,3072]{1,0:T(8,128)(2,1)S(1)} %collective-permute-done.9.refs_1_.one, bf16[256,3072]{1,0:T(8,128)(2,1)S(1)} %collective-permute-done.10.refs_2_.three, bf16[4,128,3072]{2,1,0:T(8,128)(2,1)S(1)} %copy-done, ...), custom_call_target="tpu_custom_call" | custom-call | flops 1048576 | bytes 1024 | tf_op jit(solution)/shard_map/pallas_call | solution.py:217
  69.6 0.0 collective-permute-done.17.one
  69.6 0.0 collective-permute-done.18.two
  69.6 0.1 collective-permute-done.19.three
  69.7 0.0 collective-permute-done.15.refs_0_
  69.7 0.0 collective-permute-done.16.refs_1_
  69.7 0.6 shard_map.79.amps
  70.3 1.9 %collective-permute-start.20 = (bf16[4,8,64,256]{3,2,1,0:T(8,128)(2,1)S(1)}, bf16[4,8,64,256]{3,2,1,0:T(8,128)(2,1)S(1)}, u32[]{:S(2)}, u32[]{:S(2)}) collective-permute-start(bf16[4,8,64,256]{3,2,1,0:T(8,128)(2,1)S(1)} %shard_map.79.amps), channel_id=1, source_target_pairs={{0,1},{1,0},{2,3},{3,2},{4,5},{5,4},{6,7},{7,6},{8,9},{9,8},{10,11... | collective-permute-start | bytes 3145736 | tf_op jit(solution)/shard_map/ppermute | solution.py:15
  72.1 5.3 %shard_map.80.held = bf16[16,256,512]{2,1,0:T(8,128)(2,1)S(1)} custom-call(bf16[128,3072]{1,0:T(8,128)(2,1)S(1)} %collective-permute-done.15.refs_0_, bf16[128,3072]{1,0:T(8,128)(2,1)S(1)} %collective-permute-done.16.refs_1_, bf16[4,128,3072]{2,1,0:T(8,128)(2,1)S(1)} %copy-done, bf16[4,128,3072]{2,1,0:T(8,128)(2,1)S(1)} %collective-permute-done.4.refs_2_.refs_4_.refs_3_, ...), custom_call_target="tpu_custom_call" | custom-call | flops 1048576 | bytes 1024 | tf_op jit(solution)/shard_map/pallas_call | solution.py:217
  77.5 0.0 collective-permute-done.20.amps_other
  77.5 1.2 %shard_map.81 = bf16[256,512]{1,0:T(8,128)(2,1)S(1)} custom-call(bf16[4,8,64,256]{3,2,1,0:T(8,128)(2,1)S(1)} %shard_map.79.amps, bf16[4,8,64,256]{3,2,1,0:T(8,128)(2,1)S(1)} %collective-permute-done.20.amps_other, bf16[16,256,512]{2,1,0:T(8,128)(2,1)S(1)} %shard_map.80.held), custom_call_target="tpu_custom_call" | custom-call | flops 1048576 | bytes 1024 | tf_op jit(solution)/shard_map/pallas_call | solution.py:241
  78.7 0.1 reshape.22
  78.8 18.4 %all_to_all.5 = bf16[128,2,512]{2,1,0:T(2,128)(2,1)S(1)} all-to-all(bf16[128,2,512]{2,1,0:T(2,128)(2,1)S(1)} %reshape.22), channel_id=1, replica_groups=mesh['zh'=2,'zl'=2,'y'=4,'x'=4,'core'=2] {'zh','zl','y','x','core'}, dimensions={0} | all-to-all | bytes 524288 | tf_op jit(solution)/shard_map/all_to_all | solution.py:311
  97.3 0.2 reduce
  97.5 0.6 copy.8
  (9 shorter events, 0.0 us)
Async XLA Ops:
  0.0 13.6 %collective-permute-start.4 = (bf16[4,128,3072]{2,1,0:T(8,128)(2,1)}, bf16[4,128,3072]{2,1,0:T(8,128)(2,1)S(1)}, u32[]{:S(2)}, u32[]{:S(2)}) collective-permute-start(bf16[4,128,3072]{2,1,0:T(8,128)(2,1)} %refs_2_.1), channel_id=1, source_target_pairs={{0,1},{1,0},{2,3},{3,2},{4,5},{5,4},{6,7},{7,6},{8,9},{9,8},{10,11... | collective-permute-start | bytes 9437192 | tf_op jit(solution)/shard_map/ppermute | solution.py:15
  2.4 11.1 %collective-permute-start = (bf16[16,3072]{1,0:T(8,128)(2,1)S(1)}, bf16[16,3072]{1,0:T(8,128)(2,1)S(1)}, u32[]{:S(2)}, u32[]{:S(2)}) collective-permute-start(bf16[16,3072]{1,0:T(8,128)(2,1)S(1)} %get-tuple-element.77), channel_id=1, source_target_pairs={{0,1},{1,0},{2,3},{3,2},{4,5},{5,4},{6,7},{7,6},{8,9},{9,8},{10,11... | collective-permute-start | bytes 294920 | tf_op jit(solution)/shard_map/ppermute | solution.py:15
  2.5 11.0 %collective-permute-start.2 = (bf16[16,3072]{1,0:T(8,128)(2,1)S(1)}, bf16[16,3072]{1,0:T(8,128)(2,1)S(1)}, u32[]{:S(2)}, u32[]{:S(2)}) collective-permute-start(bf16[16,3072]{1,0:T(8,128)(2,1)S(1)} %get-tuple-element.77), channel_id=1, source_target_pairs={{0,65},{1,64},{64,1},{65,0},{2,67},{3,66},{66,3},{67,2},{4,69},{5,... | collective-permute-start | bytes 294920 | tf_op jit(solution)/shard_map/ppermute | solution.py:260
  6.6 6.9 %copy-start.5 = (s32[4]{0:T(128)S(1)}, s32[4]{0:T(128)}, u32[]{:S(2)}) copy-start(s32[4]{0:T(128)} %param.13) | copy-start | bytes 52
  6.6 7.0 %collective-permute-start.1 = (bf16[16,3072]{1,0:T(8,128)(2,1)S(1)}, bf16[16,3072]{1,0:T(8,128)(2,1)S(1)}, u32[]{:S(2)}, u32[]{:S(2)}) collective-permute-start(bf16[16,3072]{1,0:T(8,128)(2,1)S(1)} %get-tuple-element.40.mine), channel_id=1, source_target_pairs={{0,64},{64,0},{1,65},{65,1},{2,66},{66,2},{3,67},{67,3},{4,68},{68... | collective-permute-start | bytes 294920 | tf_op jit(solution)/shard_map/ppermute | solution.py:259
  6.6 6.9 %collective-permute-start.3 = (s32[4]{0:T(128)}, s32[4]{0:T(128)S(1)}, u32[]{:S(2)}, u32[]{:S(2)}) collective-permute-start(s32[4]{0:T(128)} %param.13), channel_id=1, source_target_pairs={{0,32},{1,97},{32,64},{33,1},{64,96},{65,33},{96,0},{97,65},{2,34}... | collective-permute-start | bytes 56 | tf_op jit(solution)/shard_map/ppermute | solution.py:22
  13.6 19.9 %collective-permute-start.11 = (bf16[2,128,3072]{2,1,0:T(8,128)(2,1)}, bf16[2,128,3072]{2,1,0:T(8,128)(2,1)}, u32[]{:S(2)}, u32[]{:S(2)}) collective-permute-start(bf16[2,128,3072]{2,1,0:T(8,128)(2,1)} %get-tuple-element.46), channel_id=1, source_target_pairs={{0,32},{1,97},{32,64},{33,1},{64,96},{65,33},{96,0},{97,65},{2,34}... | collective-permute-start | bytes 4718600 | tf_op jit(solution)/shard_map/ppermute | solution.py:22
  15.0 20.3 %copy-start.1 = (bf16[64,16,512]{2,1,0:T(8,128)(2,1)S(1)}, bf16[64,16,512]{2,1,0:T(8,128)(2,1)}, u32[]{:S(2)}) copy-start(bf16[64,16,512]{2,1,0:T(8,128)(2,1)} %amps) | copy-start | bytes 3145732
  15.7 23.6 %copy-start = (bf16[4,128,3072]{2,1,0:T(8,128)(2,1)S(1)}, bf16[4,128,3072]{2,1,0:T(8,128)(2,1)}, u32[]{:S(2)}) copy-start(bf16[4,128,3072]{2,1,0:T(8,128)(2,1)} %refs_2_.1) | copy-start | bytes 9437188
  15.7 23.6 %copy-start.2 = (s32[512]{0:T(512)S(1)}, s32[512]{0:T(512)}, u32[]{:S(2)}) copy-start(s32[512]{0:T(512)} %param.12) | copy-start | bytes 6148
  15.7 23.6 %copy-start.3 = (s32[8]{0:T(128)S(1)}, s32[8]{0:T(128)}, u32[]{:S(2)}) copy-start(s32[8]{0:T(128)} %refs_11_.1) | copy-start | bytes 100
  15.7 23.6 %copy-start.4 = (s32[128]{0:T(128)S(1)}, s32[128]{0:T(128)}, u32[]{:S(2)}) copy-start(s32[128]{0:T(128)} %param.11) | copy-start | bytes 1540
  15.7 8.4 %collective-permute-start.5 = (bf16[64,3072]{1,0:T(8,128)(2,1)S(1)}, bf16[64,3072]{1,0:T(8,128)(2,1)S(1)}, u32[]{:S(2)}, u32[]{:S(2)}) collective-permute-start(bf16[64,3072]{1,0:T(8,128)(2,1)S(1)} %shard_map.73.refs_0_), channel_id=1, source_target_pairs={{0,2},{1,9},{2,4},{3,11},{4,6},{5,13},{6,0},{7,15},{8,10},{9,17},{... | collective-permute-start | bytes 1179656 | tf_op jit(solution)/shard_map/ppermute | solution.py:33
  17.1 10.5 %collective-permute-start.6 = (bf16[64,3072]{1,0:T(8,128)(2,1)S(1)}, bf16[64,3072]{1,0:T(8,128)(2,1)S(1)}, u32[]{:S(2)}, u32[]{:S(2)}) collective-permute-start(bf16[64,3072]{1,0:T(8,128)(2,1)S(1)} %shard_map.73.refs_0_), channel_id=1, source_target_pairs={{0,6},{1,25},{2,0},{3,27},{4,2},{5,29},{6,4},{7,31},{8,14},{9,1},{... | collective-permute-start | bytes 1179656 | tf_op jit(solution)/shard_map/ppermute | solution.py:33
  18.6 10.5 %collective-permute-start.7 = (bf16[64,3072]{1,0:T(8,128)(2,1)S(1)}, bf16[64,3072]{1,0:T(8,128)(2,1)S(1)}, u32[]{:S(2)}, u32[]{:S(2)}) collective-permute-start(bf16[64,3072]{1,0:T(8,128)(2,1)S(1)} %shard_map.73.refs_0_), channel_id=1, source_target_pairs={{0,4},{1,17},{2,6},{3,19},{4,0},{5,21},{6,2},{7,23},{8,12},{9,25},... | collective-permute-start | bytes 1179656 | tf_op jit(solution)/shard_map/ppermute | solution.py:33
  20.2 9.0 %collective-permute-start.8 = (s32[8]{0:T(128)S(1)}, s32[8]{0:T(128)S(1)}, u32[]{:S(2)}, u32[]{:S(2)}) collective-permute-start(s32[8]{0:T(128)S(1)} %pad_add_fusion.refs_4_.refs_9_.refs_8_), channel_id=1, source_target_pairs={{0,1},{1,0},{2,3},{3,2},{4,5},{5,4},{6,7},{7,6},{8,9},{9,8},{10,11... | collective-permute-start | bytes 104 | tf_op jit(solution)/shard_map/ppermute | solution.py:15
  24.1 26.2 %collective-permute-start.13 = (bf16[2,128,3072]{2,1,0:T(8,128)(2,1)}, bf16[2,128,3072]{2,1,0:T(8,128)(2,1)S(1)}, u32[]{:S(2)}, u32[]{:S(2)}) collective-permute-start(bf16[2,128,3072]{2,1,0:T(8,128)(2,1)} %get-tuple-element.47), channel_id=1, source_target_pairs={{0,32},{1,97},{32,64},{33,1},{64,96},{65,33},{96,0},{97,65},{2,34}... | collective-permute-start | bytes 4718600 | tf_op jit(solution)/shard_map/ppermute | solution.py:22
  29.2 21.0 %collective-permute-start.9 = (bf16[256,3072]{1,0:T(8,128)(2,1)S(1)}, bf16[256,3072]{1,0:T(8,128)(2,1)S(1)}, u32[]{:S(2)}, u32[]{:S(2)}) collective-permute-start(bf16[256,3072]{1,0:T(8,128)(2,1)S(1)} %shard_map.74.refs_0_), channel_id=1, source_target_pairs={{0,8},{1,3},{2,10},{3,5},{4,12},{5,7},{6,14},{7,1},{8,16},{9,11},{... | collective-permute-start | bytes 4718600 | tf_op jit(solution)/shard_map/ppermute | solution.py:33
  30.5 19.8 %collective-permute-start.10 = (bf16[256,3072]{1,0:T(8,128)(2,1)S(1)}, bf16[256,3072]{1,0:T(8,128)(2,1)S(1)}, u32[]{:S(2)}, u32[]{:S(2)}) collective-permute-start(bf16[256,3072]{1,0:T(8,128)(2,1)S(1)} %shard_map.74.refs_0_), channel_id=1, source_target_pairs={{0,24},{1,7},{2,26},{3,1},{4,28},{5,3},{6,30},{7,5},{8,0},{9,15},{... | collective-permute-start | bytes 4718600 | tf_op jit(solution)/shard_map/ppermute | solution.py:33
  33.5 16.8 %collective-permute-start.12 = (bf16[2,128,3072]{2,1,0:T(8,128)(2,1)}, bf16[2,128,3072]{2,1,0:T(8,128)(2,1)S(1)}, u32[]{:S(2)}, u32[]{:S(2)}) collective-permute-start(bf16[2,128,3072]{2,1,0:T(8,128)(2,1)} %collective-permute-done.11.refs_3_.refs_5_.refs_4_), channel_id=1, source_target_pairs={{0,1},{1,0},{2,3},{3,2},{4,5},{5,4},{6,7},{7,6},{8,9},{9,8},{10,11... | collective-permute-start | bytes 4718600 | tf_op jit(solution)/shard_map/ppermute | solution.py:15
  50.3 7.3 %collective-permute-start.14 = (bf16[2,128,3072]{2,1,0:T(8,128)(2,1)S(1)}, bf16[2,128,3072]{2,1,0:T(8,128)(2,1)S(1)}, u32[]{:S(2)}, u32[]{:S(2)}) collective-permute-start(bf16[2,128,3072]{2,1,0:T(8,128)(2,1)S(1)} %collective-permute-done.13.refs_7_.refs_6_), channel_id=1, source_target_pairs={{0,1},{1,0},{2,3},{3,2},{4,5},{5,4},{6,7},{7,6},{8,9},{9,8},{10,11... | collective-permute-start | bytes 4718600 | tf_op jit(solution)/shard_map/ppermute | solution.py:15
  52.2 17.4 %collective-permute-start.15 = (bf16[128,3072]{1,0:T(8,128)(2,1)S(1)}, bf16[128,3072]{1,0:T(8,128)(2,1)S(1)}, u32[]{:S(2)}, u32[]{:S(2)}) collective-permute-start(bf16[128,3072]{1,0:T(8,128)(2,1)S(1)} %get-tuple-element.60), channel_id=1, source_target_pairs={{0,8},{1,3},{2,10},{3,5},{4,12},{5,7},{6,14},{7,1},{8,16},{9,11},{... | collective-permute-start | bytes 2359304 | tf_op jit(solution)/shard_map/ppermute | solution.py:33
  53.5 16.2 %collective-permute-start.16 = (bf16[128,3072]{1,0:T(8,128)(2,1)S(1)}, bf16[128,3072]{1,0:T(8,128)(2,1)S(1)}, u32[]{:S(2)}, u32[]{:S(2)}) collective-permute-start(bf16[128,3072]{1,0:T(8,128)(2,1)S(1)} %get-tuple-element.61), channel_id=1, source_target_pairs={{0,24},{1,7},{2,26},{3,1},{4,28},{5,3},{6,30},{7,5},{8,0},{9,15},{... | collective-permute-start | bytes 2359304 | tf_op jit(solution)/shard_map/ppermute | solution.py:33
  55.0 14.5 %collective-permute-start.17 = (bf16[8,64,256]{2,1,0:T(8,128)(2,1)S(1)}, bf16[8,64,256]{2,1,0:T(8,128)(2,1)S(1)}, u32[]{:S(2)}, u32[]{:S(2)}) collective-permute-start(bf16[8,64,256]{2,1,0:T(8,128)(2,1)S(1)} %get-tuple-element.63), channel_id=1, source_target_pairs={{0,32},{32,64},{64,96},{96,0},{1,33},{33,65},{65,97},{97,1},{2,34}... | collective-permute-start | bytes 786440 | tf_op jit(solution)/shard_map/ppermute | solution.py:287
  55.5 14.0 %collective-permute-start.18 = (bf16[8,64,256]{2,1,0:T(8,128)(2,1)S(1)}, bf16[8,64,256]{2,1,0:T(8,128)(2,1)S(1)}, u32[]{:S(2)}, u32[]{:S(2)}) collective-permute-start(bf16[8,64,256]{2,1,0:T(8,128)(2,1)S(1)} %get-tuple-element.64), channel_id=1, source_target_pairs={{0,64},{32,96},{64,0},{96,32},{1,65},{33,97},{65,1},{97,33},{2,66}... | collective-permute-start | bytes 786440 | tf_op jit(solution)/shard_map/ppermute | solution.py:287
  57.6 12.1 %collective-permute-start.19 = (bf16[8,64,256]{2,1,0:T(8,128)(2,1)S(1)}, bf16[8,64,256]{2,1,0:T(8,128)(2,1)S(1)}, u32[]{:S(2)}, u32[]{:S(2)}) collective-permute-start(bf16[8,64,256]{2,1,0:T(8,128)(2,1)S(1)} %get-tuple-element.65), channel_id=1, source_target_pairs={{0,96},{32,0},{64,32},{96,64},{1,97},{33,1},{65,33},{97,65},{2,98}... | collective-permute-start | bytes 786440 | tf_op jit(solution)/shard_map/ppermute | solution.py:287
  70.3 7.2 %collective-permute-start.20 = (bf16[4,8,64,256]{3,2,1,0:T(8,128)(2,1)S(1)}, bf16[4,8,64,256]{3,2,1,0:T(8,128)(2,1)S(1)}, u32[]{:S(2)}, u32[]{:S(2)}) collective-permute-start(bf16[4,8,64,256]{3,2,1,0:T(8,128)(2,1)S(1)} %shard_map.79.amps), channel_id=1, source_target_pairs={{0,1},{1,0},{2,3},{3,2},{4,5},{5,4},{6,7},{7,6},{8,9},{9,8},{10,11... | collective-permute-start | bytes 3145736 | tf_op jit(solution)/shard_map/ppermute | solution.py:15
